TPU v7x, 32 devices: a whole 2x2x4 slice. The times are simulated.
32 devices in a mesh: seq: 4 (over z), mp: 2 (over core), dp: 4 (over y, x).
Axes of the slice: x: 2, y: 2, z: 4, core: 2. Of those that a mesh axis runs over, the one named last changes fastest.
Arguments:
- tokens: bfloat16 [8, 1024, 2048], P('dp', 'seq'), may hold values from -6 to 6
- cotangent: bfloat16 [8, 1024, 2048], P('dp', 'seq'), may hold values from -6 to 6
- attention_norm_gain: bfloat16 [2048], replicated, may hold values from 0.5 to 1.5
- feedforward_norm_gain: bfloat16 [2048], replicated, may hold values from 0.5 to 1.5
- query_weight: bfloat16 [2048, 2048], P('seq', 'mp'), may hold values from -0.125 to 0.125
- key_weight: bfloat16 [2048, 512], P('seq', 'mp'), may hold values from -0.125 to 0.125
- value_weight: bfloat16 [2048, 512], P('seq', 'mp'), may hold values from -0.125 to 0.125
- output_weight: bfloat16 [2048, 2048], P('mp', 'seq'), may hold values from -0.5 to 0.5
- gate_weight: bfloat16 [2048, 8192], P('seq', 'mp'), may hold values from -0.125 to 0.125
- up_weight: bfloat16 [2048, 8192], P('seq', 'mp'), may hold values from -0.125 to 0.125
- down_weight: bfloat16 [8192, 2048], P('mp', 'seq'), may hold values from -0.0625 to 0.0625
- query_adapter_down: bfloat16 [2048, 8], replicated, may hold values from -0.125 to 0.125
- query_adapter_up: bfloat16 [8, 2048], P(None, 'mp'), may hold values from -2 to 2
- key_adapter_down: bfloat16 [2048, 8], replicated, may hold values from -0.125 to 0.125
- key_adapter_up: bfloat16 [8, 512], P(None, 'mp'), may hold values from -2 to 2
- value_adapter_down: bfloat16 [2048, 8], replicated, may hold values from -0.125 to 0.125
- value_adapter_up: bfloat16 [8, 512], P(None, 'mp'), may hold values from -2 to 2
- output_adapter_down: bfloat16 [2048, 8], P('mp'), may hold values from -0.5 to 0.5
- output_adapter_up: bfloat16 [8, 2048], replicated, may hold values from -2 to 2
- query_feature_matrix: bfloat16 [32, 64, 64], P('mp'), may hold values from -0.75 to 0.75
- key_feature_matrix: bfloat16 [8, 64, 64], P('mp'), may hold values from -0.75 to 0.75
Outputs:
- output: bfloat16 [8, 1024, 2048], P('dp', 'seq')
- tokens_grad: float32 [8, 1024, 2048], P('dp', 'seq')
- attn_gain_grad: float32 [2048], replicated
- mlp_gain_grad: float32 [2048], replicated
- qdown_grad: float32 [2048, 8], replicated
- qup_grad: float32 [8, 2048], P(None, 'mp')
- kdown_grad: float32 [2048, 8], replicated
- kup_grad: float32 [8, 512], P(None, 'mp')
- vdown_grad: float32 [2048, 8], replicated
- vup_grad: float32 [8, 512], P(None, 'mp')
- odown_grad: float32 [2048, 8], P('mp')
- oup_grad: float32 [8, 2048], replicated
- query_maps_grad: float32 [32, 64, 64], P('mp')
- key_maps_grad: float32 [8, 64, 64], P('mp')
All inputs are finite; a program needn't handle non-finite values.
Results may differ from a plain program's by a relative error of at most 0.018.
Values may be sent and summed in bfloat16 or wider, within the bound.
A program may use at most 320 MiB of HBM per device.

v0:
```python
import math

import jax
import jax.numpy as jnp
from jax import lax
from jax.sharding import PartitionSpec as P

SOFTMAX_SPAN = 64


highest = lax.Precision.HIGHEST
epsilon = 1e-05


def from_behind(value, axis, steps):
    count = lax.axis_size(axis)
    first, last = (max(0, -steps), min(count, count - steps))
    return lax.ppermute(value, axis, [(source, source + steps) for source in range(first, last)])


def entering(value, axis, join, neutral):
    place = lax.axis_index(axis)
    gathered = jax.tree.map(
        lambda a, kind: lax.all_gather(a.astype(kind), axis), value, (jnp.bfloat16, jnp.bfloat16)
    )
    state = jax.tree.map(lambda a, e: jnp.zeros_like(a) + jnp.asarray(e, a.dtype), value, neutral)

    def one(turn, state):
        return join(
            state,
            jax.tree.map(
                lambda a, own: lax.dynamic_index_in_dim(a, turn, 0, False).astype(own.dtype),
                gathered,
                value,
            ),
        )

    return lax.fori_loop(0, place, one, state)


def entering_2(value, axis, join, neutral):
    count = lax.axis_size(axis)
    place = lax.axis_index(axis)
    ahead = count - 1 - place
    gathered = jax.tree.map(
        lambda a, kind: lax.all_gather(a.astype(kind), axis),
        value,
        jax.tree.map(lambda a: jnp.bfloat16 if a.dtype == jnp.float32 else a.dtype, value),
    )
    state = jax.tree.map(lambda a, e: jnp.zeros_like(a) + jnp.asarray(e, a.dtype), value, neutral)

    def one(turn, state):
        source = count - 1 - turn
        return join(
            state,
            jax.tree.map(
                lambda a, own: lax.dynamic_index_in_dim(a, source, 0, False).astype(own.dtype),
                gathered,
                value,
            ),
        )

    return lax.fori_loop(0, ahead, one, state)


def key_features(key_block, feature_maps):
    logits = jnp.einsum("ekd,kdf->ekf", key_block, feature_maps, preferred_element_type=jnp.float32)
    return jnp.concatenate([jax.nn.softmax(logits, -1), jax.nn.softmax(-logits, -1)], -1)


def query_features(query_rows, feature_maps):
    logits = jnp.einsum(
        "tkgd,kgdf->tkgf", query_rows, feature_maps, preferred_element_type=jnp.float32
    )
    return jnp.concatenate([jax.nn.softmax(logits, -1), jax.nn.softmax(-logits, -1)], -1)


def state_piece(features, values, valid_mask, rows_here):
    kept_feats = jnp.where(valid_mask[:rows_here, None, None], features[:rows_here], 0.0)
    state_sum = jnp.einsum(
        "ekf,ekd->kfd", kept_feats, values[:rows_here], preferred_element_type=jnp.float32
    )
    return (state_sum, jnp.sum(kept_feats, 0))


def attend(query_rows, key_block, values, features, state_sum, totals, feature_maps, valid_mask):
    rows_here = query_rows.shape[0]
    extent = key_block.shape[0]
    reach_back = extent - rows_here
    query_feats = query_features(query_rows, feature_maps)
    scores = jnp.einsum(
        "tkgd,ekd->kgte", query_rows, key_block, preferred_element_type=jnp.float32
    ) / math.sqrt(query_rows.shape[-1])
    rowpos = jnp.arange(rows_here, dtype=jnp.int32)[:, None]
    colpos = jnp.arange(extent, dtype=jnp.int32)[None, :]
    inside = (colpos > rowpos) & (colpos <= rowpos + reach_back) & valid_mask[None, :]
    older_mask = (colpos <= rowpos) & valid_mask[None, :]
    window_part = jnp.where(inside, jnp.exp(jnp.where(inside, scores, 0.0)), 0.0)
    linear_part = jnp.where(
        older_mask,
        jnp.einsum("tkgf,ekf->kgte", query_feats, features, preferred_element_type=jnp.float32),
        0.0,
    )
    weights = window_part + linear_part
    numerator = jnp.einsum("kgte,ekd->tkgd", weights, values, preferred_element_type=jnp.float32)
    numerator = numerator + jnp.einsum(
        "tkgf,kfd->tkgd", query_feats, state_sum, preferred_element_type=jnp.float32
    )
    denominator = jnp.transpose(jnp.sum(weights, -1), (2, 0, 1))
    denominator = denominator + jnp.einsum(
        "tkgf,kf->tkg", query_feats, totals, preferred_element_type=jnp.float32
    )
    return numerator / denominator[..., None]


def simple_product(left, right):
    return jnp.dot(left, right, preferred_element_type=jnp.float32)


def dot_transposed(left, right):
    return lax.dot_general(
        left, right, (((1,), (1,)), ((), ())), preferred_element_type=jnp.float32
    )


def exact_dot(left, right):
    return jnp.dot(left, right, precision=highest)


def norm_back(inputs, inv_rms, gain, dnormed):
    return inv_rms * gain * dnormed - inputs * inv_rms**3 * jnp.mean(
        gain * dnormed * inputs, -1, keepdims=True
    )


def add_pair(earlier, later):
    return (earlier[0] + later[0], earlier[1] + later[1])


def per_device(
    tokens,
    cotangent,
    attention_norm_gain,
    feedforward_norm_gain,
    query_weight,
    key_weight,
    value_weight,
    output_weight,
    gate_weight,
    up_weight,
    down_weight,
    query_adapter_down,
    query_adapter_up,
    key_adapter_down,
    key_adapter_up,
    value_adapter_down,
    value_adapter_up,
    output_adapter_down,
    output_adapter_up,
    query_feature_matrix,
    key_feature_matrix,
):
    shards = (
        query_weight,
        key_weight,
        value_weight,
        output_weight,
        gate_weight,
        up_weight,
        down_weight,
    )
    gathered = (
        lax.all_gather(shards[0], "seq", axis=0, tiled=True),
        lax.all_gather(shards[1], "seq", axis=0, tiled=True),
        lax.all_gather(shards[2], "seq", axis=0, tiled=True),
        lax.all_gather(shards[3], "seq", axis=1, tiled=True),
        lax.all_gather(shards[4], "seq", axis=0, tiled=True),
        lax.all_gather(shards[5], "seq", axis=0, tiled=True),
        lax.all_gather(shards[6], "seq", axis=1, tiled=True),
    )
    complete_query, complete_key, complete_value, full_out, full_gate, full_up, full_down = gathered
    seq_count, rows_here, width = tokens.shape
    total_rows = seq_count * rows_here
    heads_kv = key_feature_matrix.shape[0]
    head_size = key_feature_matrix.shape[1]
    query_group_count = query_feature_matrix.shape[0] // heads_kv
    extent = rows_here + SOFTMAX_SPAN
    position = lax.axis_index("seq")
    inputs = tokens.reshape(total_rows, width).astype(jnp.float32)
    gain_attn = attention_norm_gain.astype(jnp.float32)
    rms_attn = lax.rsqrt(jnp.mean(inputs * inputs, -1, keepdims=True) + epsilon)
    normed = (inputs * rms_attn * gain_attn).astype(jnp.bfloat16)
    normed_wide = normed.astype(jnp.float32)

    def apply_projection(weight_matrix, first, second):
        inner = simple_product(normed, first)
        full = simple_product(normed, weight_matrix) + exact_dot(inner, second.astype(jnp.float32))
        return (inner, full.astype(jnp.bfloat16))

    inner_query, query_half = apply_projection(complete_query, query_adapter_down, query_adapter_up)
    inner_key, key_half = apply_projection(complete_key, key_adapter_down, key_adapter_up)
    inner_value, value_half = apply_projection(complete_value, value_adapter_down, value_adapter_up)
    key3 = key_half.reshape(seq_count, rows_here, heads_kv * head_size)
    value3 = value_half.reshape(seq_count, rows_here, heads_kv * head_size)
    key_prev, value_prev = from_behind(
        (key3[:, rows_here - SOFTMAX_SPAN :], value3[:, rows_here - SOFTMAX_SPAN :]), "seq", 1
    )
    key_ext = (
        jnp.concatenate([key_prev, key3], 1)
        .astype(jnp.float32)
        .reshape(seq_count, extent, heads_kv, head_size)
    )
    value_ext = (
        jnp.concatenate([value_prev, value3], 1)
        .astype(jnp.float32)
        .reshape(seq_count, extent, heads_kv, head_size)
    )
    valid_mask = position * rows_here - SOFTMAX_SPAN + jnp.arange(extent, dtype=jnp.int32) >= 0
    kmaps = key_feature_matrix.astype(jnp.float32)
    query_feature_set = query_feature_matrix.astype(jnp.float32).reshape(
        heads_kv, query_group_count, head_size, head_size
    )

    def features_all(key_in, maps_in):
        return jax.vmap(key_features, (0, None))(key_in, maps_in)

    features, features_back = jax.vjp(features_all, key_ext, kmaps)

    def pieces_all(feats_in, values_in):
        return jax.vmap(state_piece, (0, 0, None, None))(feats_in, values_in, valid_mask, rows_here)

    (piece_state, piece_totals), pieces_back = jax.vjp(pieces_all, features, value_ext)
    zero_pair = (jnp.zeros_like(piece_state), jnp.zeros_like(piece_totals))
    state_sum, totals = entering((piece_state, piece_totals), "seq", add_pair, zero_pair)
    queries5 = query_half.reshape(
        seq_count, rows_here, heads_kv, query_group_count, head_size
    ).astype(jnp.float32)

    def attend_all(query_in, key_in, value_in, feats_in, state_in, totals_in, maps_in):
        return jax.vmap(attend, (0, 0, 0, 0, 0, 0, None, None))(
            query_in, key_in, value_in, feats_in, state_in, totals_in, maps_in, valid_mask
        )

    attn5, attend_back = jax.vjp(
        attend_all, queries5, key_ext, value_ext, features, state_sum, totals, query_feature_set
    )
    attention_half = attn5.reshape(total_rows, -1).astype(jnp.bfloat16)
    inner_output = simple_product(attention_half, output_adapter_down)
    output_up_broad = output_adapter_up.astype(jnp.float32)
    branch = lax.psum(
        simple_product(attention_half, full_out) + exact_dot(inner_output, output_up_broad), "mp"
    )
    resid = inputs + branch
    gain_mlp = feedforward_norm_gain.astype(jnp.float32)
    rms_mlp = lax.rsqrt(jnp.mean(resid * resid, -1, keepdims=True) + epsilon)
    normed_mlp = (resid * rms_mlp * gain_mlp).astype(jnp.bfloat16)
    gate = simple_product(normed_mlp, full_gate)
    up_vals = simple_product(normed_mlp, full_up)
    sigmoid_gate = jax.nn.sigmoid(gate)
    activated = gate * sigmoid_gate
    hidden = (activated * up_vals).astype(jnp.bfloat16)
    mlp_out = lax.psum(simple_product(hidden, full_down).astype(jnp.bfloat16), "mp").astype(
        jnp.float32
    )
    output = (resid + mlp_out).astype(jnp.bfloat16).reshape(seq_count, rows_here, width)
    regathered = (
        lax.all_gather(shards[0], "seq", axis=0, tiled=True),
        lax.all_gather(shards[1], "seq", axis=0, tiled=True),
        lax.all_gather(shards[2], "seq", axis=0, tiled=True),
        lax.all_gather(shards[3], "seq", axis=1, tiled=True),
        lax.all_gather(shards[4], "seq", axis=0, tiled=True),
        lax.all_gather(shards[5], "seq", axis=0, tiled=True),
        lax.all_gather(shards[6], "seq", axis=1, tiled=True),
    )
    complete_query, complete_key, complete_value, full_out, full_gate, full_up, full_down = (
        regathered
    )
    grad_rows16 = cotangent.reshape(total_rows, width)
    grad_out = grad_rows16.astype(jnp.float32)
    dhidden = dot_transposed(grad_rows16, full_down)
    dgate = (dhidden * up_vals * sigmoid_gate * (1.0 + gate * (1.0 - sigmoid_gate))).astype(
        jnp.bfloat16
    )
    dup_vals = (dhidden * activated).astype(jnp.bfloat16)
    dnormed_mlp = lax.psum(
        (dot_transposed(dgate, full_gate) + dot_transposed(dup_vals, full_up)).astype(jnp.bfloat16),
        "mp",
    ).astype(jnp.float32)
    mlp_gain_term = jnp.sum(dnormed_mlp * resid * rms_mlp, 0)
    dresid = grad_out + norm_back(resid, rms_mlp, gain_mlp, dnormed_mlp)
    dresid16 = dresid.astype(jnp.bfloat16)
    dresid_wide = dresid16.astype(jnp.float32)
    inner_output_gradient = exact_dot(dresid_wide, output_up_broad.T)
    oup_term = exact_dot(inner_output.T, dresid_wide)
    odown_term = exact_dot(attention_half.astype(jnp.float32).T, inner_output_gradient)
    dattn = dot_transposed(dresid16, full_out) + exact_dot(
        inner_output_gradient, output_adapter_down.astype(jnp.float32).T
    )
    dattn16 = dattn.astype(jnp.bfloat16).astype(jnp.float32).reshape(attn5.shape)
    dqueries, dkey_ext, dvalue_ext, dfeatures, dstate, dtotals, dqmaps = attend_back(dattn16)
    later_state, later_totals = entering_2((dstate, dtotals), "seq", add_pair, zero_pair)
    dfeatures_more, dvalue_more = pieces_back((later_state, later_totals))
    dkey_more, dkmaps = features_back(dfeatures + dfeatures_more)
    dkey_ext = (dkey_ext + dkey_more).reshape(seq_count, extent, heads_kv * head_size)
    dvalue_ext = (dvalue_ext + dvalue_more).reshape(seq_count, extent, heads_kv * head_size)
    back_key, back_value = (
        from_behind(dkey_ext[:, :SOFTMAX_SPAN].astype(jnp.bfloat16), "seq", -1).astype(jnp.float32),
        from_behind(dvalue_ext[:, :SOFTMAX_SPAN].astype(jnp.bfloat16), "seq", -1).astype(
            jnp.float32
        ),
    )
    dkey_own = dkey_ext[:, SOFTMAX_SPAN:]
    dvalue_own = dvalue_ext[:, SOFTMAX_SPAN:]
    dkey_own = jnp.concatenate(
        [
            dkey_own[:, : rows_here - SOFTMAX_SPAN],
            dkey_own[:, rows_here - SOFTMAX_SPAN :] + back_key,
        ],
        1,
    )
    dvalue_own = jnp.concatenate(
        [
            dvalue_own[:, : rows_here - SOFTMAX_SPAN],
            dvalue_own[:, rows_here - SOFTMAX_SPAN :] + back_value,
        ],
        1,
    )
    query_gradient_half = dqueries.reshape(total_rows, -1).astype(jnp.bfloat16)
    key_gradient_half = dkey_own.reshape(total_rows, -1).astype(jnp.bfloat16)
    value_gradient_half = dvalue_own.reshape(total_rows, -1).astype(jnp.bfloat16)

    def projection_pullback_rule(dproj16, weight_matrix, first, second, inner):
        dproj_wide = dproj16.astype(jnp.float32)
        dinner = exact_dot(dproj_wide, second.astype(jnp.float32).T)
        dnormed_part = dot_transposed(dproj16, weight_matrix) + exact_dot(
            dinner, first.astype(jnp.float32).T
        )
        return (dnormed_part, exact_dot(normed_wide.T, dinner), exact_dot(inner.T, dproj_wide))

    dnormed_q, qdown_term, qup_term = projection_pullback_rule(
        query_gradient_half, complete_query, query_adapter_down, query_adapter_up, inner_query
    )
    normed_key_gradient, key_down_product, key_up_product = projection_pullback_rule(
        key_gradient_half, complete_key, key_adapter_down, key_adapter_up, inner_key
    )
    dnormed_v, vdown_term, vup_term = projection_pullback_rule(
        value_gradient_half, complete_value, value_adapter_down, value_adapter_up, inner_value
    )
    dnormed = lax.psum(
        (dnormed_q + normed_key_gradient + dnormed_v).astype(jnp.bfloat16), "mp"
    ).astype(jnp.float32)
    attn_gain_term = jnp.sum(dnormed * inputs * rms_attn, 0)
    tokens_grad = (dresid + norm_back(inputs, rms_attn, gain_attn, dnormed)).reshape(
        seq_count, rows_here, width
    )
    split_sums = lax.psum(
        (
            qup_term,
            key_up_product,
            vup_term,
            odown_term,
            dqmaps.reshape(query_feature_matrix.shape),
            dkmaps,
            attn_gain_term,
            mlp_gain_term,
        ),
        ("seq", "dp"),
    )
    whole_sums = lax.psum((qdown_term, key_down_product, vdown_term, oup_term), ("seq", "mp", "dp"))
    return (
        output,
        tokens_grad,
        split_sums[6],
        split_sums[7],
        whole_sums[0],
        split_sums[0],
        whole_sums[1],
        split_sums[1],
        whole_sums[2],
        split_sums[2],
        split_sums[3],
        whole_sums[3],
        split_sums[4],
        split_sums[5],
    )


def solution(mesh):
    placed = (
        P("dp", "seq", None),
        P("dp", "seq", None),
        P(),
        P(),
        P("seq", "mp"),
        P("seq", "mp"),
        P("seq", "mp"),
        P("mp", "seq"),
        P("seq", "mp"),
        P("seq", "mp"),
        P("mp", "seq"),
        P(),
        P(None, "mp"),
        P(),
        P(None, "mp"),
        P(),
        P(None, "mp"),
        P("mp", None),
        P(),
        P("mp", None, None),
        P("mp", None, None),
    )
    return jax.shard_map(
        per_device,
        mesh=mesh,
        in_specs=placed,
        out_specs=(
            P("dp", "seq", None),
            P("dp", "seq", None),
            P(),
            P(),
            P(),
            P(None, "mp"),
            P(),
            P(None, "mp"),
            P(),
            P(None, "mp"),
            P("mp", None),
            P(),
            P("mp", None, None),
            P("mp", None, None),
        ),
        check_vma=False,
    )
```

profile of v0, /device:TPU:0, one launch (start us, length us, event | category | flops | bytes accessed | tf_op | source)
XLA Modules:
  0.0 1769.6 jit_solution(4046753118571501815)
XLA Ops:
  19.4 20.9 %all-gather.14.cloned.1.call-done = bf16[2048,256]{1,0:T(8,128)(2,1)} async-done(((bf16[512,256]{1,0:T(8,128)(2,1)}), bf16[2048,256]{1,0:T(8,128)(2,1)}) %all-gather.14.cloned.1.call-update) | async-done | bytes 1048592 | tf_op jit(solution)/shard_map/all_gather | solution.py:174
  47.7 21.6 %all-gather.12.cloned.1.call-done = bf16[2048,256]{1,0:T(8,128)(2,1)} async-done(((bf16[512,256]{1,0:T(8,128)(2,1)}), bf16[2048,256]{1,0:T(8,128)(2,1)}) %all-gather.12.cloned.1.call-update) | async-done | bytes 1048592 | tf_op jit(solution)/shard_map/all_gather | solution.py:175
  89.4 21.9 %all-gather = bf16[8,4,128,64]{2,3,1,0:T(8,128)(2,1)} all-gather(bf16[2,4,128,64]{2,3,1,0:T(8,128)(2,1)S(1)} %convolution_convert_fusion), channel_id=2, replica_groups=mesh['seq'=4,'mp'=2,'dp'=4] {'seq'}, dimensions={0}, use_global_device_ids=true | all-gather | bytes 655360 | tf_op jit(solution)/shard_map/all_gather | solution.py:24
  111.3 12.1 all-gather.1
  123.9 35.7 %all-gather.16.cloned.1.call-done = bf16[2048,1024]{1,0:T(8,128)(2,1)} async-done(((bf16[512,1024]{1,0:T(8,128)(2,1)}), bf16[2048,1024]{1,0:T(8,128)(2,1)}) %all-gather.16.cloned.1.call-update) | async-done | bytes 4194320 | tf_op jit(solution)/shard_map/all_gather | solution.py:173
  186.4 4.6 fusion.182
  196.4 44.7 %all-gather.18.cloned.1.call-done = bf16[1024,2048]{1,0:T(8,128)(2,1)} async-done(((bf16[1024,512]{1,0:T(8,128)(2,1)}), bf16[1024,2048]{1,0:T(8,128)(2,1)}) %all-gather.18.cloned.1.call-update) | async-done | bytes 4194320 | tf_op jit(solution)/shard_map/all_gather | solution.py:176
  255.4 21.5 %all-reduce.13.cloned.1.call-done = f32[512,2048]{1,0:T(8,128)} async-done(((f32[512,2048]{1,0:T(8,128)}), f32[512,2048]{1,0:T(8,128)}) %all-reduce.13.cloned.1.call-update) | async-done | bytes 4194320 | tf_op jit(solution)/shard_map/psum | solution.py:250
  276.9 4.7 multiply_reduce_fusion
  282.2 284.2 %all-gather.22.cloned.1.call-done = bf16[2048,4096]{1,0:T(8,128)(2,1)} async-done(((bf16[512,4096]{1,0:T(8,128)(2,1)}), bf16[2048,4096]{1,0:T(8,128)(2,1)}) %all-gather.22.cloned.1.call-update) | async-done | bytes 16777232 | tf_op jit(solution)/shard_map/all_gather | solution.py:178
  566.4 15.9 fusion.162
  582.3 270.8 %all-gather.20.cloned.1.call-done = bf16[2048,4096]{1,0:T(8,128)(2,1)} async-done(((bf16[512,4096]{1,0:T(8,128)(2,1)}), bf16[2048,4096]{1,0:T(8,128)(2,1)}) %all-gather.20.cloned.1.call-update) | async-done | bytes 16777232 | tf_op jit(solution)/shard_map/all_gather | solution.py:177
  853.0 15.7 fusion.163
  868.7 271.0 %all-gather.24.cloned.1.call-done = bf16[4096,2048]{1,0:T(8,128)(2,1)} async-done(((bf16[4096,512]{1,0:T(8,128)(2,1)}), bf16[4096,2048]{1,0:T(8,128)(2,1)}) %all-gather.24.cloned.1.call-update) | async-done | bytes 16777232 | tf_op jit(solution)/shard_map/all_gather | solution.py:179
  1139.7 14.4 fusion.193
  1154.1 20.4 %fusion.32 = f32[512,2048]{1,0:T(8,128)} fusion(bf16[2048,4096]{1,0:T(8,128)(2,1)} %all-gather.20.cloned.1.call-done, f32[512,4096]{1,0:T(8,128)} %fusion.163, f32[512,4096]{1,0:T(8,128)} %fusion.193, f32[512,4096]{1,0:T(8,128)} %fusion.162), kind=kOutput, calls=%fused_computation.63 | convolution fusion | flops 8610906112 | bytes 46137344 | tf_op jit(solution)/shard_map/dot_general | solution.py:121
  1174.5 19.3 %add_convert_fusion.1 = bf16[512,2048]{1,0:T(8,128)(2,1)} fusion(f32[512,2048]{1,0:T(8,128)} %fusion.32, bf16[2048,4096]{1,0:T(8,128)(2,1)} %all-gather.22.cloned.1.call-done, f32[512,4096]{1,0:T(8,128)} %fusion.193, f32[512,4096]{1,0:T(8,128)} %fusion.163), kind=kOutput, calls=%fused_computation.59 | convolution fusion | flops 8604614656 | bytes 39845888 | tf_op jit(solution)/shard_map/dot_general | solution.py:121
  1193.9 19.4 %fusion.42 = bf16[512,2048]{1,0:T(8,128)(2,1)} fusion(bf16[4096,2048]{1,0:T(8,128)(2,1)} %all-gather.24.cloned.1.call-done, f32[512,4096]{1,0:T(8,128)} %fusion.162, f32[512,4096]{1,0:T(8,128)} %fusion.163), kind=kOutput, calls=%fused_computation.74 | convolution fusion | flops 8603566080 | bytes 35651584 | tf_op jit(solution)/shard_map/dot_general | solution.py:117
  1213.4 4.9 fusion.18
  1240.9 16.7 all-gather.2
  1258.2 12.0 all-gather.3
  1275.5 5.0 fusion.81
  1285.9 5.2 fusion.11
  1295.2 9.9 convolution_bitcast_fusion.1
  1310.7 5.0 add_bitcast_fusion
  1321.5 11.7 fusion.45
  1370.7 10.8 all-reduce.23.cloned.1.call-done
  1386.0 4.9 fusion.20
  1390.9 4.9 add_convert_fusion.2
  1395.8 120.6 %all-reduce.17.cloned.1.call-done = (f32[2048,8]{0,1:T(8,128)}, f32[2048,8]{0,1:T(8,128)}, f32[2048,8]{0,1:T(8,128)}, f32[8,2048]{1,0:T(8,128)}) async-done(((f32[2048,8]{0,1:T(8,128)}, f32[2048,8]{0,1:T(8,128)}, f32[2048,8]{0,1:T(8,128)}, f32[8,2048]{1,0:T(8,128)}), (f32[2048,8]{0,1:T(8,128)}, f32[2048,8]{0,1:T(8,128)}, f32[2048,8]{0,1:T(8,128)}, f32[8,2048]{1,0:T(8,128)})) %all-reduce.17.cloned.1.call-update) | async-done | bytes 262160 | tf_op jit(solution)/shard_map/psum | solution.py:369
  1516.4 115.4 %all-reduce.21.cloned.1.call-done = (f32[16,64,64]{2,1,0:T(8,128)}, f32[4,64,64]{2,1,0:T(8,128)}) async-done(((f32[16,64,64]{2,1,0:T(8,128)}, f32[4,64,64]{2,1,0:T(8,128)}), (f32[16,64,64]{2,1,0:T(8,128)}, f32[4,64,64]{2,1,0:T(8,128)})) %all-reduce.21.cloned.1.call-update) | async-done | bytes 327696 | tf_op jit(solution)/shard_map/psum | solution.py:356
  1631.9 113.7 %all-reduce.19.cloned.1.call-done = (f32[2048]{0:T(1024)}, f32[2048]{0:T(1024)}, f32[8,1024]{1,0:T(8,128)}, f32[8,256]{1,0:T(8,128)}, f32[8,256]{1,0:T(8,128)}, /*index=5*/f32[1024,8]{0,1:T(8,128)}) async-done(((f32[2048]{0:T(1024)}, f32[2048]{0:T(1024)}, f32[8,1024]{1,0:T(8,128)}, f32[8,256]{1,0:T(8,128)}, f32[8,256]{1,0:T(8,128)}, /*index=5*/f32[1024,8]{0,1:T(8,128)}), (f32[2048]{0:T(1024)}, ...) | async-done | bytes 98320 | tf_op jit(solution)/shard_map/psum | solution.py:356
  (457 shorter events, 197.7 us)
Async XLA Ops:
  7.2 159.8 %copy-start = (bf16[16,64,64]{2,1,0:T(8,128)(2,1)S(1)}, bf16[16,64,64]{2,1,0:T(8,128)(2,1)}, u32[]{:S(2)}) copy-start(bf16[16,64,64]{2,1,0:T(8,128)(2,1)} %param.44) | copy-start | bytes 393220
  7.2 33.1 %all-gather.14.cloned.1.call-start = ((), (), s32[]{:S(2)}) async-start(), calls=%async_computation.1 | async-start | bytes 1310720 | tf_op jit(solution)/shard_map/all_gather | solution.py:174
  7.9 61.4 %all-gather.12.cloned.1.call-start = ((), (), s32[]{:S(2)}) async-start(), calls=%async_computation | async-start | bytes 1310720 | tf_op jit(solution)/shard_map/all_gather | solution.py:175
  8.7 150.9 %all-gather.16.cloned.1.call-start = ((), (), s32[]{:S(2)}) async-start(), calls=%async_computation.2 | async-start | bytes 5242880 | tf_op jit(solution)/shard_map/all_gather | solution.py:173
  9.4 231.7 %all-gather.18.cloned.1.call-start = ((), (), s32[]{:S(2)}) async-start(), calls=%async_computation.3 | async-start | bytes 5242880 | tf_op jit(solution)/shard_map/all_gather | solution.py:176
  10.0 266.9 %all-reduce.13.cloned.1.call-start = ((), (), s32[]{:S(2)}) async-start(), calls=%async_computation.4 | async-start | bytes 8388608 | tf_op jit(solution)/shard_map/psum | solution.py:250
  15.1 144.6 %copy-start.1 = (bf16[512,2048]{1,0:T(8,128)(2,1)}, bf16[512,2048]{1,0:T(8,128)(2,1)S(1)}, u32[]{:S(2)}) copy-start(bf16[512,2048]{1,0:T(8,128)(2,1)S(1)} %fusion.30) | copy-start | bytes 6291460
  16.4 72.5 %copy-start.125 = (pred[320]{0:T(512)(128)(4,1)}, pred[320]{0:T(512)(128)(4,1)S(1)}, u32[]{:S(2)}) copy-start(pred[320]{0:T(512)(128)(4,1)S(1)} %add_compare_fusion) | copy-start | bytes 964
  43.6 37.1 %collective-permute-start.1 = (bf16[2,64,256]{2,1,0:T(8,128)(2,1)}, bf16[2,64,256]{2,1,0:T(8,128)(2,1)}, u32[]{:S(2)}, u32[]{:S(2)}) collective-permute-start(bf16[2,64,256]{2,1,0:T(8,128)(2,1)} %slice.55), channel_id=1, source_target_pairs={{0,8},{8,16},{16,24},{1,9},{9,17},{17,25},{2,10},{10,18},{18,26},{... | collective-permute-start | bytes 196616 | tf_op jit(solution)/shard_map/ppermute | solution.py:18
  74.2 117.5 %copy-start.36 = (bf16[2,256,4,64]{1,3,2,0:T(8,128)(2,1)}, bf16[2,256,4,64]{1,3,2,0:T(8,128)(2,1)S(1)}, u32[]{:S(2)}) copy-start(bf16[2,256,4,64]{1,3,2,0:T(8,128)(2,1)S(1)} %copy.228) | copy-start | bytes 786436
  75.8 10.6 collective-permute-start
  83.2 170.2 %copy-start.103 = (f32[2,320,4]{1,0,2:T(2,128)}, f32[2,320,4]{1,0,2:T(2,128)S(1)}, u32[]{:S(2)}) copy-start(f32[2,320,4]{1,0,2:T(2,128)S(1)} %get-tuple-element.255) | copy-start | bytes 30724
  87.3 36.2 %copy-start.50 = (bf16[2,64,256]{1,2,0:T(8,128)(2,1)}, bf16[2,64,256]{1,2,0:T(8,128)(2,1)S(1)}, u32[]{:S(2)}) copy-start(bf16[2,64,256]{1,2,0:T(8,128)(2,1)S(1)} %copy.226) | copy-start | bytes 196612
  123.9 69.1 %copy-start.14 = (f32[2,4,128,64]{3,2,1,0:T(8,128)}, f32[2,4,128,64]{3,2,1,0:T(8,128)S(1)}, u32[]{:S(2)}) copy-start(f32[2,4,128,64]{3,2,1,0:T(8,128)S(1)} %get-tuple-element.129) | copy-start | bytes 786436
  123.9 40.2 %copy-start.77 = (f32[512,8]{0,1:T(8,128)S(1)}, f32[512,8]{0,1:T(8,128)}, u32[]{:S(2)}) copy-start(f32[512,8]{0,1:T(8,128)} %fusion.190) | copy-start | bytes 49156
  123.9 40.2 %copy-start.113 = (bf16[8,1024]{1,0:T(8,128)(2,1)S(1)}, bf16[8,1024]{1,0:T(8,128)(2,1)}, u32[]{:S(2)}) copy-start(bf16[8,1024]{1,0:T(8,128)(2,1)} %param.37) | copy-start | bytes 49156
  169.3 84.8 %copy-start.75 = (f32[2,256,4,4]{1,0,3,2:T(2,128)}, f32[2,256,4,4]{1,0,3,2:T(2,128)S(1)}, u32[]{:S(2)}) copy-start(f32[2,256,4,4]{1,0,3,2:T(2,128)S(1)} %get-tuple-element.251) | copy-start | bytes 98308
  175.4 79.3 %copy-start.67 = (f32[2,256,4,4]{1,0,3,2:T(2,128)}, f32[2,256,4,4]{1,0,3,2:T(2,128)S(1)}, u32[]{:S(2)}) copy-start(f32[2,256,4,4]{1,0,3,2:T(2,128)S(1)} %get-tuple-element.253) | copy-start | bytes 98308
  196.2 49.6 %copy-start.11 = (bf16[128,8,2,256]{3,1,2,0:T(8,128)(2,1)}, bf16[128,8,2,256]{3,1,2,0:T(8,128)(2,1)S(1)}, u32[]{:S(2)}) copy-start(bf16[128,8,2,256]{3,1,2,0:T(8,128)(2,1)S(1)} %copy.342) | copy-start | bytes 3145732
  196.4 49.3 %copy-start.79 = (f32[512,8]{0,1:T(8,128)}, f32[512,8]{0,1:T(8,128)S(1)}, u32[]{:S(2)}) copy-start(f32[512,8]{0,1:T(8,128)S(1)} %fusion.192) | copy-start | bytes 49156
  196.4 49.3 %copy-start.88 = (bf16[8,2048]{1,0:T(8,128)(2,1)S(1)}, bf16[8,2048]{1,0:T(8,128)(2,1)}, u32[]{:S(2)}) copy-start(bf16[8,2048]{1,0:T(8,128)(2,1)} %param.43) | copy-start | bytes 98308
  249.8 316.6 %all-gather.22.cloned.1.call-start = ((), (), s32[]{:S(2)}) async-start(), calls=%async_computation.6 | async-start | bytes 20971520 | tf_op jit(solution)/shard_map/all_gather | solution.py:178
  250.4 602.6 %all-gather.20.cloned.1.call-start = ((), (), s32[]{:S(2)}) async-start(), calls=%async_computation.5 | async-start | bytes 20971520 | tf_op jit(solution)/shard_map/all_gather | solution.py:177
  251.2 888.5 %all-gather.24.cloned.1.call-start = ((), (), s32[]{:S(2)}) async-start(), calls=%async_computation.7 | async-start | bytes 20971520 | tf_op jit(solution)/shard_map/all_gather | solution.py:179
  251.9 961.4 %all-reduce.15.cloned.1.call-start = ((), (), s32[]{:S(2)}) async-start(), calls=%async_computation.8 | async-start | bytes 4194304 | tf_op jit(solution)/shard_map/psum | solution.py:285
  582.3 557.4 %copy-start.55 = (bf16[2,256,2048]{2,1,0:T(8,128)(2,1)S(1)}, bf16[2,256,2048]{2,1,0:T(8,128)(2,1)}, u32[]{:S(2)}) copy-start(bf16[2,256,2048]{2,1,0:T(8,128)(2,1)} %param.26) | copy-start | bytes 6291460
  1193.8 187.6 %all-reduce.23.cloned.1.call-start = ((), (), s32[]{:S(2)}) async-start(), calls=%async_computation.12 | async-start | bytes 8388608 | tf_op jit(solution)/shard_map/psum | solution.py:262
  1284.5 57.9 %collective-permute-start.3 = (bf16[2,64,256]{2,1,0:T(8,128)(2,1)}, bf16[2,64,256]{2,1,0:T(8,128)(2,1)}, u32[]{:S(2)}, u32[]{:S(2)}) collective-permute-start(bf16[2,64,256]{2,1,0:T(8,128)(2,1)} %slice.65), channel_id=1, source_target_pairs={{8,0},{16,8},{24,16},{9,1},{17,9},{25,17},{10,2},{18,10},{26,18},{... | collective-permute-start | bytes 196616 | tf_op jit(solution)/shard_map/ppermute | solution.py:18
  1308.9 31.3 %collective-permute-start.2 = (bf16[2,64,256]{2,1,0:T(8,128)(2,1)S(1)}, bf16[2,64,256]{2,1,0:T(8,128)(2,1)S(1)}, u32[]{:S(2)}, u32[]{:S(2)}) collective-permute-start(bf16[2,64,256]{2,1,0:T(8,128)(2,1)S(1)} %slice.62), channel_id=1, source_target_pairs={{8,0},{16,8},{24,16},{9,1},{17,9},{25,17},{10,2},{18,10},{26,18},{... | collective-permute-start | bytes 196616 | tf_op jit(solution)/shard_map/ppermute | solution.py:18
  1350.3 166.1 %all-reduce.17.cloned.1.call-start = ((), (), s32[]{:S(2)}) async-start(), calls=%async_computation.9 | async-start | bytes 524288 | tf_op jit(solution)/shard_map/psum | solution.py:369
  1366.0 265.9 %all-reduce.21.cloned.1.call-start = ((), (), s32[]{:S(2)}) async-start(), calls=%async_computation.11 | async-start | bytes 1310720 | tf_op jit(solution)/shard_map/psum | solution.py:356
  1368.1 377.5 %all-reduce.19.cloned.1.call-start = ((), (), s32[]{:S(2)}) async-start(), calls=%async_computation.10 | async-start | bytes 196608 | tf_op jit(solution)/shard_map/psum | solution.py:356
  (120 other events, 753.2 us)
Sparse Core Ops, SparseCore 0:
  9.6 30.6 all-gather.13
  41.9 27.3 all-gather.11
  70.9 88.7 all-gather.15
  161.0 80.0 all-gather.17
  249.9 26.9 all-reduce.12
  278.4 287.9 all-gather.21
  568.0 284.9 all-gather.19
  854.7 284.9 all-gather.23
  1193.9 19.4 all-reduce.14
  1350.4 30.9 all-reduce.22
  1389.4 126.9 all-reduce.16
  1523.0 108.8 all-reduce.20
  1640.5 105.0 all-reduce.18
where the time goes:
time: 1780 us; the launch traced here: 1770 us
  waiting for transfers between devices  1340 us (75%)
  matrix products  234 us (13%)
  blocking collectives  62.7 us (4%)
  local copies, waits for them, and re-layouts  60.5 us (3%)
  other arithmetic  48.5 us (3%)
    all_gather x1, waiting for transfers between devices, per_device(): lax.all_gather(shards[5], 'seq', axis=0, tiled=True)  284 us
    all_gather x1, waiting for transfers between devices, per_device(): lax.all_gather(shards[6], 'seq', axis=1, tiled=True)  271 us
    all_gather x1, waiting for transfers between devices, per_device(): lax.all_gather(shards[4], 'seq', axis=0, tiled=True)  271 us
    psum x2, waiting for transfers between devices, per_device(): lax.psum((qup_term, key_up_product, vup_term, odown_term, dqmaps.reshape(...  229 us
    psum x1, waiting for transfers between devices, per_device(): lax.psum((qdown_term, key_down_product, vdown_term, oup_term), ('seq', 'm...  121 us
    dot_general x11, matrix products, simple_product(): return jnp.dot(left, right, preferred_element_type=jnp.float32)  66.8 us
    dot_general x7, matrix products, dot_transposed(): lax.dot_general(left, right, (((1,), (1,)), ((), ())), preferred_element_...  60.8 us
    all_gather x1, waiting for transfers between devices, per_device(): lax.all_gather(shards[3], 'seq', axis=1, tiled=True)  44.7 us
  transfers between devices with their start and end apart: 17, of which 13 were waited for; matrix products, arithmetic and copies ran while one was open for 12% of the time, Pallas kernels for 0%

commit v1 on v0

v1 whole, which is shorter than its diff:
```python
import math
import functools
import jax
import jax.numpy as jnp
from jax import lax
from jax.experimental import pallas as pl
from jax.experimental.pallas import tpu as pltpu
from jax.sharding import PartitionSpec as P

SOFTMAX_SPAN = 64
epsilon = 1e-05

MESH = pl.DeviceIdType.MESH
ANY = pl.ANY


class Spot:
    def __init__(self):
        self.s, self.m, self.d = (lax.axis_index(a) for a in ("seq", "mp", "dp"))
        self.x = self.d + 1 - 2 * (self.d % 2)
        self.y = (self.d + 2) % 4
        self.diag = (self.x + 2) % 4

    def to(self, kind):
        s, m, d = self.s, self.m, self.d
        if kind == "x":
            d = self.x
        elif kind == "y":
            d = self.y
        elif kind == "c":
            m = 1 - m
        elif kind == "up":
            s = s + 1
        elif kind == "dn":
            s = s - 1
        return {"seq": s, "mp": m, "dp": d}


def remote(src, dst, send, recv, where):
    return pltpu.make_async_remote_copy(
        src_ref=src, dst_ref=dst, send_sem=send, recv_sem=recv, device_id=where, device_id_type=MESH
    )


def greet(spot, n, kinds):
    bar = pltpu.get_barrier_semaphore()
    count = 0
    for kind in kinds:
        if kind in ("up", "dn"):
            there = spot.s + 1 < n if kind == "up" else spot.s > 0

            @pl.when(there)
            def _(kind=kind):
                pl.semaphore_signal(bar, inc=1, device_id=spot.to(kind), device_id_type=MESH)

            count = count + there.astype(jnp.int32)
        else:
            pl.semaphore_signal(bar, inc=1, device_id=spot.to(kind), device_id_type=MESH)
            count = count + 1
    pl.semaphore_wait(bar, count)


def gather_weights_kernel(n, k, *refs):
    ins, outs = refs[:k], refs[k : 2 * k]
    own_sem, z_send, z_recv, p_send, p_recv = refs[2 * k :]
    spot = Spot()
    s, d = spot.s, spot.d
    own = [pltpu.make_async_copy(ins[a], outs[a].at[s], own_sem.at[a]) for a in range(k)]
    for c in own:
        c.start()
    greet(spot, n, ("x", "y", "up", "dn"))

    def rows(a, who, part=None):
        size = ins[a].shape[0] // 4
        if part is None:
            return pl.ds(who * size, size)
        return pl.ds(who * size + part * (size // 2), size // 2)

    def sends(up, t):
        return ((s - t >= 0) & (s + 1 < n)) if up else ((s + t < n) & (s > 0))

    def receives(up, t):
        return s - 1 - t >= 0 if up else s + 1 + t < n

    def z_copy(a, up, t, sending):
        way = 0 if up else 1
        piece = (s - t if up else s + t) if sending else (s - 1 - t if up else s + 1 + t)
        dst = outs[a].at[piece, rows(a, d)]
        src = ins[a].at[rows(a, d)] if (t == 0 and sending) else dst
        return remote(src, dst, z_send.at[a, way, t], z_recv.at[a, way, t], spot.to("up" if up else "dn"))

    def piece_of(up, t):
        return s - 1 - t if up else s + 1 + t

    def plane_copy(a, up, t, kind):
        way = 0 if up else 1
        who = (d, d, spot.y, spot.x)[kind]
        part = (None, None, 0, 1)[kind]
        ref = outs[a].at[piece_of(up, t), rows(a, who, part)]
        return remote(ref, ref, p_send.at[a, way, t, kind], p_recv.at[a, way, t, kind], spot.to("xyxy"[kind]))

    def landed(a, up, t, kind):
        way = 0 if up else 1
        who = (spot.x, spot.y, spot.diag, spot.diag)[kind]
        part = (None, None, 0, 1)[kind]
        ref = outs[a].at[piece_of(up, t), rows(a, who, part)]
        return remote(ref, ref, p_send.at[a, way, t, kind], p_recv.at[a, way, t, kind], spot.to("xyxy"[kind]))

    for a in range(k):
        for up in (True, False):

            @pl.when(sends(up, 0))
            def _():
                z_copy(a, up, 0, True).start()

    for t in range(n):
        if t < n - 1:
            for a in range(k):
                for up in (True, False):

                    @pl.when(receives(up, t))
                    def _():
                        z_copy(a, up, t, False).wait_recv()
                        if t + 1 < n - 1:

                            @pl.when(sends(up, t + 1))
                            def _():
                                z_copy(a, up, t + 1, True).start()

                        plane_copy(a, up, t, 0).start()
                        plane_copy(a, up, t, 1).start()

        if t > 0:
            for a in range(k):
                for up in (True, False):

                    @pl.when(receives(up, t - 1))
                    def _():
                        landed(a, up, t - 1, 0).wait_recv()
                        plane_copy(a, up, t - 1, 3).start()
                        landed(a, up, t - 1, 1).wait_recv()
                        plane_copy(a, up, t - 1, 2).start()

    for t in range(n - 1):
        for a in range(k):
            for up in (True, False):

                @pl.when(sends(up, t))
                def _():
                    z_copy(a, up, t, True).wait_send()

                @pl.when(receives(up, t))
                def _():
                    landed(a, up, t, 2).wait_recv()
                    landed(a, up, t, 3).wait_recv()
                    for kind in range(4):
                        plane_copy(a, up, t, kind).wait_send()

    for c in own:
        c.wait()


def gather_weights(n, arrays, cid):
    k = len(arrays)
    DMA = pltpu.SemaphoreType.DMA
    return pl.pallas_call(
        functools.partial(gather_weights_kernel, n, k),
        out_shape=[jax.ShapeDtypeStruct((n,) + a.shape, a.dtype) for a in arrays],
        in_specs=[pl.BlockSpec(memory_space=ANY)] * k,
        out_specs=[pl.BlockSpec(memory_space=ANY)] * k,
        scratch_shapes=[DMA((k,)), DMA((k, 2, n - 1)), DMA((k, 2, n - 1)), DMA((k, 2, n - 1, 4)), DMA((k, 2, n - 1, 4))],
        compiler_params=pltpu.CompilerParams(collective_id=cid, has_side_effects=True),
        name="gather_weights",
    )(*arrays)


def plane_gather_kernel(own, out, own_sem, c_send, c_recv, p_send, p_recv):
    spot = Spot()
    m, d = spot.m, spot.d
    half = own.shape[0] // 2
    mine = pltpu.make_async_copy(own, out.at[d, m], own_sem)
    mine.start()
    greet(spot, 0, ("x", "y", "c"))
    parts = (pl.ds(0, half), pl.ds(half, half))

    def copy(kind, sending):
        who = (d, d, spot.y, spot.x)[kind] if sending else (spot.x, spot.y, spot.diag, spot.diag)[kind]
        if kind < 2:
            dst = out.at[who, m]
            src = own if sending else dst
        else:
            dst = out.at[who, m, parts[kind - 2]]
            src = dst
        return remote(src, dst, p_send.at[kind], p_recv.at[kind], spot.to("xyxy"[kind]))

    def core(index, sending):
        who = (d, spot.x, spot.y, spot.diag, spot.diag)[index]
        col = m if sending else 1 - m
        if index < 3:
            dst = out.at[who, col]
            src = own if (sending and index == 0) else dst
        else:
            dst = out.at[who, col, parts[index - 3]]
            src = dst
        return remote(src, dst, c_send.at[index], c_recv.at[index], spot.to("c"))

    copy(0, True).start()
    copy(1, True).start()
    core(0, True).start()
    copy(0, False).wait_recv()
    copy(3, True).start()
    core(1, True).start()
    copy(1, False).wait_recv()
    copy(2, True).start()
    core(2, True).start()
    copy(2, False).wait_recv()
    core(3, True).start()
    copy(3, False).wait_recv()
    core(4, True).start()
    for index in range(5):
        core(index, False).wait_recv()
        core(index, True).wait_send()
    for kind in range(4):
        copy(kind, True).wait_send()
    mine.wait()


def plane_gather(own, cid):
    DMA = pltpu.SemaphoreType.DMA
    return pl.pallas_call(
        plane_gather_kernel,
        out_shape=jax.ShapeDtypeStruct((4, 2) + own.shape, own.dtype),
        in_specs=[pl.BlockSpec(memory_space=ANY)],
        out_specs=pl.BlockSpec(memory_space=ANY),
        scratch_shapes=[DMA, DMA((5,)), DMA((5,)), DMA((4,)), DMA((4,))],
        compiler_params=pltpu.CompilerParams(collective_id=cid, has_side_effects=True),
        name=f"plane_gather_{cid}",
    )(own)


def plane_scatter_kernel(
    part, out, mine, theirs, s1, xin, yin, t2, xin2, yin2, l_sem, c_send, c_recv, p_send, p_recv
):
    spot = Spot()
    m, d = spot.m, spot.d
    half = out.shape[0] // 2
    A, B = pl.ds(0, half), pl.ds(half, half)
    order = (spot.diag, spot.x, spot.y, d)
    loads = [pltpu.make_async_copy(part.at[who, m], mine.at[i], l_sem.at[i]) for i, who in enumerate(order)]
    for c in loads:
        c.start()
    greet(spot, 0, ("x", "y", "c"))

    def core(i):
        return remote(part.at[order[i], 1 - m], theirs.at[i], c_send.at[i], c_recv.at[i], spot.to("c"))

    for i in range(4):
        core(i).start()

    first = {
        "xdiag": remote(s1.at[0, A], xin.at[1], p_send.at[0], p_recv.at[0], spot.to("x")),
        "ydiag": remote(s1.at[0, B], yin.at[1], p_send.at[1], p_recv.at[1], spot.to("y")),
        "x": remote(s1.at[1, A], xin.at[0], p_send.at[2], p_recv.at[2], spot.to("x")),
        "y": remote(s1.at[2, B], yin.at[0], p_send.at[3], p_recv.at[3], spot.to("y")),
    }
    for i in range(4):
        loads[i].wait()
        core(i).wait_recv()
        s1[i] = (mine[i].astype(jnp.float32) + theirs[i].astype(jnp.float32)).astype(s1.dtype)
        if i == 0:
            first["xdiag"].start()
            first["ydiag"].start()
        elif i == 1:
            first["x"].start()
        elif i == 2:
            first["y"].start()
    second = (
        remote(t2.at[0], yin2, p_send.at[4], p_recv.at[4], spot.to("y")),
        remote(t2.at[1], xin2, p_send.at[5], p_recv.at[5], spot.to("x")),
    )
    first["xdiag"].wait_recv()
    t2[0] = (s1[2, A].astype(jnp.float32) + xin[1].astype(jnp.float32)).astype(t2.dtype)
    second[0].start()
    first["ydiag"].wait_recv()
    t2[1] = (s1[1, B].astype(jnp.float32) + yin[1].astype(jnp.float32)).astype(t2.dtype)
    second[1].start()
    first["x"].wait_recv()
    first["y"].wait_recv()
    second[0].wait_recv()
    out[A] = s1[3, A].astype(jnp.float32) + xin[0].astype(jnp.float32) + yin2[...].astype(jnp.float32)
    second[1].wait_recv()
    out[B] = s1[3, B].astype(jnp.float32) + yin[0].astype(jnp.float32) + xin2[...].astype(jnp.float32)
    for i in range(4):
        core(i).wait_send()
    for c in list(first.values()) + list(second):
        c.wait_send()


def plane_scatter(part, cid):
    DMA = pltpu.SemaphoreType.DMA
    r, w = part.shape[2:]
    b = jnp.bfloat16
    V = pltpu.VMEM
    return pl.pallas_call(
        plane_scatter_kernel,
        out_shape=jax.ShapeDtypeStruct((r, w), jnp.float32),
        in_specs=[pl.BlockSpec(memory_space=ANY)],
        out_specs=pl.BlockSpec(memory_space=pltpu.VMEM),
        scratch_shapes=[
            V((4, r, w), b),
            V((4, r, w), b),
            V((4, r, w), b),
            V((2, r // 2, w), b),
            V((2, r // 2, w), b),
            V((2, r // 2, w), b),
            V((r // 2, w), b),
            V((r // 2, w), b),
            DMA((4,)),
            DMA((4,)),
            DMA((4,)),
            DMA((6,)),
            DMA((6,)),
        ],
        compiler_params=pltpu.CompilerParams(collective_id=cid, has_side_effects=True, vmem_limit_bytes=40 << 20),
        name=f"plane_scatter_{cid}",
    )(part)


def line_sum_kernel(n, up, own, out, box, send, recv):
    spot = Spot()
    s = spot.s
    greet(spot, n, ("up", "dn"))
    go = "up" if up else "dn"

    def sends(t):
        return ((s - t >= 0) & (s + 1 < n)) if up else ((s + t < n) & (s > 0))

    def receives(t):
        return s - 1 - t >= 0 if up else s + 1 + t < n

    def copy(t):
        src = own if t == 0 else box.at[t - 1]
        return remote(src, box.at[t], send.at[t], recv.at[t], spot.to(go))

    @pl.when(sends(0))
    def _():
        copy(0).start()

    out[...] = jnp.zeros_like(out)
    for t in range(n - 1):

        @pl.when(receives(t))
        def _():
            copy(t).wait_recv()
            if t + 1 < n - 1:

                @pl.when(sends(t + 1))
                def _():
                    copy(t + 1).start()

            out[...] += box[t].astype(jnp.float32)

    for t in range(n - 1):

        @pl.when(sends(t))
        def _():
            copy(t).wait_send()


def line_sum(n, own, up, cid):
    DMA = pltpu.SemaphoreType.DMA
    return pl.pallas_call(
        functools.partial(line_sum_kernel, n, up),
        out_shape=jax.ShapeDtypeStruct(own.shape, jnp.float32),
        in_specs=[pl.BlockSpec(memory_space=pltpu.VMEM)],
        out_specs=pl.BlockSpec(memory_space=pltpu.VMEM),
        scratch_shapes=[pltpu.VMEM((n - 1,) + own.shape, own.dtype), DMA((n - 1,)), DMA((n - 1,))],
        compiler_params=pltpu.CompilerParams(collective_id=cid, has_side_effects=True, vmem_limit_bytes=40 << 20),
        name=f"line_sum_{cid}",
    )(own)
def plane_total_kernel(
    n, shared, part, out, mine, core_in, xin, yin, t2, xin2, yin2, line, c_send, c_recv, p_send, p_recv, z_send, z_recv, g_send, g_recv
):
    spot = Spot()
    s, d = spot.s, spot.d
    h = out.shape[1] // 2
    A, B = pl.ds(0, h), pl.ds(h, h)
    f32, b16 = jnp.float32, jnp.bfloat16
    mine[...] = part[...].astype(b16)
    greet(spot, n, ("x", "y", "c", "up", "dn"))
    core = remote(mine.at[pl.ds(0, shared)], core_in, c_send, c_recv, spot.to("c"))
    core.start()
    core.wait()
    mine[:shared] = (mine[:shared].astype(f32) + core_in[...].astype(f32)).astype(b16)

    def block(who, part):
        return mine.at[pl.ds(who * 2 * h + part * h, h)]

    def read(who, part):
        return mine[pl.ds(who * 2 * h + part * h, h)].astype(f32)

    first = (
        remote(block(spot.diag, 0), xin.at[1], p_send.at[0], p_recv.at[0], spot.to("x")),
        remote(block(spot.diag, 1), yin.at[1], p_send.at[1], p_recv.at[1], spot.to("y")),
        remote(block(spot.x, 0), xin.at[0], p_send.at[2], p_recv.at[2], spot.to("x")),
        remote(block(spot.y, 1), yin.at[0], p_send.at[3], p_recv.at[3], spot.to("y")),
    )
    for c in first:
        c.start()
    second = (
        remote(t2.at[0], yin2, p_send.at[4], p_recv.at[4], spot.to("y")),
        remote(t2.at[1], xin2, p_send.at[5], p_recv.at[5], spot.to("x")),
    )
    first[0].wait_recv()
    t2[0] = (read(spot.y, 0) + xin[1].astype(f32)).astype(b16)
    second[0].start()
    first[1].wait_recv()
    t2[1] = (read(spot.x, 1) + yin[1].astype(f32)).astype(b16)
    second[1].start()
    first[2].wait_recv()
    first[3].wait_recv()
    second[0].wait_recv()
    line[s, A] = (read(d, 0) + xin[0].astype(f32) + yin2[...].astype(f32)).astype(b16)
    second[1].wait_recv()
    line[s, B] = (read(d, 1) + yin[0].astype(f32) + xin2[...].astype(f32)).astype(b16)

    def sends(up, t):
        return ((s - t >= 0) & (s + 1 < n)) if up else ((s + t < n) & (s > 0))

    def receives(up, t):
        return s - 1 - t >= 0 if up else s + 1 + t < n

    def z_copy(up, t, sending):
        way = 0 if up else 1
        piece = (s - t if up else s + t) if sending else (s - 1 - t if up else s + 1 + t)
        return remote(line.at[piece], line.at[piece], z_send.at[way, t], z_recv.at[way, t], spot.to("up" if up else "dn"))

    for up in (True, False):

        @pl.when(sends(up, 0))
        def _():
            z_copy(up, 0, True).start()

    for t in range(n - 1):
        for up in (True, False):

            @pl.when(receives(up, t))
            def _():
                z_copy(up, t, False).wait_recv()
                if t + 1 < n - 1:

                    @pl.when(sends(up, t + 1))
                    def _():
                        z_copy(up, t + 1, True).start()

    total = line[0].astype(f32)
    for i in range(1, n):
        total = total + line[i].astype(f32)
    out[d] = total.astype(b16)

    parts = (A, B)

    def back(kind, sending):
        who = (d, d, spot.y, spot.x)[kind] if sending else (spot.x, spot.y, spot.diag, spot.diag)[kind]
        ref = out.at[who] if kind < 2 else out.at[who, parts[kind - 2]]
        return remote(ref, ref, g_send.at[kind], g_recv.at[kind], spot.to("xyxy"[kind]))

    back(0, True).start()
    back(1, True).start()
    back(0, False).wait_recv()
    back(3, True).start()
    back(1, False).wait_recv()
    back(2, True).start()
    back(2, False).wait_recv()
    back(3, False).wait_recv()
    for kind in range(4):
        back(kind, True).wait_send()
    for c in first + second:
        c.wait_send()
    for t in range(n - 1):
        for up in (True, False):

            @pl.when(sends(up, t))
            def _():
                z_copy(up, t, True).wait_send()


def plane_total(n, part, shared, cid):
    DMA = pltpu.SemaphoreType.DMA
    V = pltpu.VMEM
    b = jnp.bfloat16
    rows, w = part.shape
    h = rows // 8
    return pl.pallas_call(
        functools.partial(plane_total_kernel, n, shared),
        out_shape=jax.ShapeDtypeStruct((4, 2 * h, w), b),
        in_specs=[pl.BlockSpec(memory_space=pltpu.VMEM)],
        out_specs=pl.BlockSpec(memory_space=pltpu.VMEM),
        scratch_shapes=[
            V((rows, w), b),
            V((shared, w), b),
            V((2, h, w), b),
            V((2, h, w), b),
            V((2, h, w), b),
            V((h, w), b),
            V((h, w), b),
            V((n, 2 * h, w), b),
            DMA,
            DMA,
            DMA((6,)),
            DMA((6,)),
            DMA((2, n - 1)),
            DMA((2, n - 1)),
            DMA((4,)),
            DMA((4,)),
        ],
        compiler_params=pltpu.CompilerParams(collective_id=cid, has_side_effects=True, vmem_limit_bytes=40 << 20),
        name=f"plane_total_{cid}",
    )(part)


def key_features(key_block, feature_maps):
    logits = jnp.einsum("ekd,kdf->ekf", key_block, feature_maps, preferred_element_type=jnp.float32)
    return jnp.concatenate([jax.nn.softmax(logits, -1), jax.nn.softmax(-logits, -1)], -1)


def query_features(query_rows, feature_maps):
    logits = jnp.einsum(
        "tkgd,kgdf->tkgf", query_rows, feature_maps, preferred_element_type=jnp.float32
    )
    return jnp.concatenate([jax.nn.softmax(logits, -1), jax.nn.softmax(-logits, -1)], -1)


def state_piece(features, values, valid_mask, rows_here):
    kept_feats = jnp.where(valid_mask[:rows_here, None, None], features[:rows_here], 0.0)
    state_sum = jnp.einsum(
        "ekf,ekd->kfd", kept_feats, values[:rows_here], preferred_element_type=jnp.float32
    )
    return (state_sum, jnp.sum(kept_feats, 0))


def attend(query_rows, key_block, values, features, state_sum, totals, feature_maps, valid_mask):
    rows_here = query_rows.shape[0]
    extent = key_block.shape[0]
    reach_back = extent - rows_here
    query_feats = query_features(query_rows, feature_maps)
    scores = jnp.einsum(
        "tkgd,ekd->kgte", query_rows, key_block, preferred_element_type=jnp.float32
    ) / math.sqrt(query_rows.shape[-1])
    rowpos = jnp.arange(rows_here, dtype=jnp.int32)[:, None]
    colpos = jnp.arange(extent, dtype=jnp.int32)[None, :]
    inside = (colpos > rowpos) & (colpos <= rowpos + reach_back) & valid_mask[None, :]
    older_mask = (colpos <= rowpos) & valid_mask[None, :]
    window_part = jnp.where(inside, jnp.exp(jnp.where(inside, scores, 0.0)), 0.0)
    linear_part = jnp.where(
        older_mask,
        jnp.einsum("tkgf,ekf->kgte", query_feats, features, preferred_element_type=jnp.float32),
        0.0,
    )
    weights = window_part + linear_part
    numerator = jnp.einsum("kgte,ekd->tkgd", weights, values, preferred_element_type=jnp.float32)
    numerator = numerator + jnp.einsum(
        "tkgf,kfd->tkgd", query_feats, state_sum, preferred_element_type=jnp.float32
    )
    denominator = jnp.transpose(jnp.sum(weights, -1), (2, 0, 1))
    denominator = denominator + jnp.einsum(
        "tkgf,kf->tkg", query_feats, totals, preferred_element_type=jnp.float32
    )
    return numerator / denominator[..., None]


f32, b16 = jnp.float32, jnp.bfloat16


def dot(left, right):
    return jnp.dot(left, right, preferred_element_type=f32)


def dot_t(left, right):
    return lax.dot_general(left, right, (((1,), (1,)), ((), ())), preferred_element_type=f32)


def t_dot(left, right):
    return lax.dot_general(left, right, (((0,), (0,)), ((), ())), preferred_element_type=f32)


def norm_back(inputs, inv_rms, gain, dnormed):
    return inv_rms * gain * dnormed - inputs * inv_rms**3 * jnp.mean(
        gain * dnormed * inputs, -1, keepdims=True
    )


def from_behind(value, axis, steps):
    count = lax.axis_size(axis)
    first, last = (max(0, -steps), min(count, count - steps))
    return lax.ppermute(value, axis, [(source, source + steps) for source in range(first, last)])


def swap_core(value):
    return lax.ppermute(value, "mp", [(0, 1), (1, 0)])


def per_device(
    tokens,
    cotangent,
    attention_norm_gain,
    feedforward_norm_gain,
    query_weight,
    key_weight,
    value_weight,
    output_weight,
    gate_weight,
    up_weight,
    down_weight,
    query_adapter_down,
    query_adapter_up,
    key_adapter_down,
    key_adapter_up,
    value_adapter_down,
    value_adapter_up,
    output_adapter_down,
    output_adapter_up,
    query_feature_matrix,
    key_feature_matrix,
):
    n = lax.axis_size("seq")
    position, m, d = (lax.axis_index(a) for a in ("seq", "mp", "dp"))
    seq_count, rows_here, width = tokens.shape
    total_rows = seq_count * rows_here
    half = total_rows // 2
    heads_kv = key_feature_matrix.shape[0]
    head_size = key_feature_matrix.shape[1]
    groups = query_feature_matrix.shape[0] // heads_kv
    extent = rows_here + SOFTMAX_SPAN

    units = gate_weight.shape[1] // 4
    gate_w = lax.all_gather(lax.dynamic_slice_in_dim(gate_weight, d * units, units, 1), "seq", axis=0, tiled=True)
    up_w = lax.all_gather(lax.dynamic_slice_in_dim(up_weight, d * units, units, 1), "seq", axis=0, tiled=True)
    down_w = lax.all_gather(lax.dynamic_slice_in_dim(down_weight, d * units, units, 0), "seq", axis=1, tiled=True)

    qkv_own = jnp.concatenate([query_weight, key_weight, value_weight], 1)
    qkv_g, out_g = gather_weights(n, [qkv_own, output_weight], 1)
    qkv_w = qkv_g.reshape(width, -1)
    wide = query_weight.shape[1]
    kv_wide = key_weight.shape[1]

    def my_half(a):
        return lax.dynamic_slice_in_dim(a, m * half, half, 0)

    def both_halves(own):
        other = swap_core(own)
        return jnp.concatenate([jnp.where(m == 0, own, other), jnp.where(m == 0, other, own)], 0)

    tok2 = tokens.reshape(total_rows, width)
    inputs = tok2.astype(f32)
    gain_attn = attention_norm_gain.astype(f32)
    rms_attn = lax.rsqrt(jnp.mean(inputs * inputs, -1, keepdims=True) + epsilon)
    normed = (inputs * rms_attn * gain_attn).astype(b16)

    cot2 = cotangent.reshape(total_rows, width)
    cot_all = plane_gather(my_half(cot2), 2).reshape(8 * half, width)

    downs = jnp.concatenate([query_adapter_down, key_adapter_down, value_adapter_down], 1)
    inner = dot(normed, downs)
    rank = query_adapter_down.shape[1]
    full = dot(normed, qkv_w)

    def project(index, first, last, second):
        return (
            full[:, first:last] + dot(inner[:, index * rank : (index + 1) * rank].astype(b16), second)
        ).astype(b16)

    query_half = project(0, 0, wide, query_adapter_up)
    key_half = project(1, wide, wide + kv_wide, key_adapter_up)
    value_half = project(2, wide + kv_wide, wide + 2 * kv_wide, value_adapter_up)
    key3 = key_half.reshape(seq_count, rows_here, heads_kv * head_size)
    value3 = value_half.reshape(seq_count, rows_here, heads_kv * head_size)
    kv3 = jnp.concatenate([key3, value3], -1)
    kv_prev = from_behind(kv3[:, rows_here - SOFTMAX_SPAN :], "seq", 1)
    kv_ext = jnp.concatenate([kv_prev, kv3], 1).astype(f32)
    key_ext = kv_ext[..., :kv_wide].reshape(seq_count, extent, heads_kv, head_size)
    value_ext = kv_ext[..., kv_wide:].reshape(seq_count, extent, heads_kv, head_size)
    valid_mask = position * rows_here - SOFTMAX_SPAN + jnp.arange(extent, dtype=jnp.int32) >= 0
    kmaps = key_feature_matrix.astype(f32)
    qmaps = query_feature_matrix.astype(f32).reshape(heads_kv, groups, head_size, head_size)

    def features_all(key_in, maps_in):
        return jax.vmap(key_features, (0, None))(key_in, maps_in)

    features, features_back = jax.vjp(features_all, key_ext, kmaps)

    def pieces_all(feats_in, values_in):
        return jax.vmap(state_piece, (0, 0, None, None))(feats_in, values_in, valid_mask, rows_here)

    (piece_state, piece_totals), pieces_back = jax.vjp(pieces_all, features, value_ext)

    def line_totals(state, totals, up, cid):
        flat = jnp.concatenate([state.reshape(-1, 128), totals.reshape(-1, 128)], 0)
        flat = jnp.pad(flat, ((0, -flat.shape[0] % 16), (0, 0))).astype(b16)
        summed = line_sum(n, flat, up, cid)
        rows = state.size // 128
        return summed[:rows].reshape(state.shape), summed[rows : rows + totals.size // 128].reshape(totals.shape)

    state_sum, totals = line_totals(piece_state, piece_totals, True, 3)
    queries5 = query_half.reshape(seq_count, rows_here, heads_kv, groups, head_size).astype(f32)

    def attend_all(query_in, key_in, value_in, feats_in, state_in, totals_in, maps_in):
        return jax.vmap(attend, (0, 0, 0, 0, 0, 0, None, None))(
            query_in, key_in, value_in, feats_in, state_in, totals_in, maps_in, valid_mask
        )

    attn5, attend_back = jax.vjp(
        attend_all, queries5, key_ext, value_ext, features, state_sum, totals, qmaps
    )
    attn16 = attn5.reshape(total_rows, -1).astype(b16)
    inner_output = dot(attn16, output_adapter_down)
    branch = jnp.concatenate([dot(attn16, out_g[i]) for i in range(n)], 1) + dot(
        inner_output.astype(b16), output_adapter_up
    )
    branch16 = branch.astype(b16)
    from_other = swap_core(lax.dynamic_slice_in_dim(branch16, (1 - m) * half, half, 0))
    resid = my_half(inputs) + my_half(branch) + from_other.astype(f32)
    gain_mlp = feedforward_norm_gain.astype(f32)
    rms_mlp = lax.rsqrt(jnp.mean(resid * resid, -1, keepdims=True) + epsilon)
    normed_mlp = (resid * rms_mlp * gain_mlp).astype(b16)
    normed_all = plane_gather(normed_mlp, 4).reshape(8 * half, width)

    gate = dot(normed_all, gate_w)
    up_vals = dot(normed_all, up_w)
    dhidden = dot_t(cot_all, down_w)
    sig = jax.nn.sigmoid(gate)
    act = gate * sig
    hidden = (act * up_vals).astype(b16)
    dgate = (dhidden * up_vals * sig * (1.0 + gate * (1.0 - sig))).astype(b16)
    dup = (dhidden * act).astype(b16)
    dn_part = (dot_t(dgate, gate_w) + dot_t(dup, up_w)).astype(b16)
    out_part = dot(hidden, down_w).astype(b16)
    dnormed_mlp = plane_scatter(dn_part.reshape(4, 2, half, width), 5)
    mlp_out = plane_scatter(out_part.reshape(4, 2, half, width), 6)
    output = both_halves((resid + mlp_out).astype(b16)).reshape(seq_count, rows_here, width)

    mlp_gain_term = jnp.sum(dnormed_mlp * resid * rms_mlp, 0)
    dresid = my_half(cot2).astype(f32) + norm_back(resid, rms_mlp, gain_mlp, dnormed_mlp)
    dresid16 = both_halves(dresid.astype(b16))
    du_o = dot_t(dresid16, output_adapter_up)
    oup_term = t_dot(inner_output.astype(b16), dresid16)
    odown_term = t_dot(du_o.astype(b16), attn16)
    dattn = dot_t(du_o.astype(b16), output_adapter_down)
    step = output_weight.shape[1]
    for i in range(n):
        dattn = dattn + dot_t(dresid16[:, i * step : (i + 1) * step], out_g[i])
    dattn16 = dattn.astype(b16).astype(f32).reshape(attn5.shape)
    dqueries, dkey_ext, dvalue_ext, dfeatures, dstate, dtotals, dqmaps = attend_back(dattn16)
    later_state, later_totals = line_totals(dstate, dtotals, False, 7)
    dfeatures_more, dvalue_more = pieces_back((later_state, later_totals))
    dkey_more, dkmaps = features_back(dfeatures + dfeatures_more)
    dkey_ext = (dkey_ext + dkey_more).reshape(seq_count, extent, heads_kv * head_size)
    dvalue_ext = (dvalue_ext + dvalue_more).reshape(seq_count, extent, heads_kv * head_size)
    dkv_ext = jnp.concatenate([dkey_ext, dvalue_ext], -1)
    back = from_behind(dkv_ext[:, :SOFTMAX_SPAN].astype(b16), "seq", -1).astype(f32)
    dkv = dkv_ext[:, SOFTMAX_SPAN:]
    dkv = jnp.concatenate(
        [dkv[:, : rows_here - SOFTMAX_SPAN], dkv[:, rows_here - SOFTMAX_SPAN :] + back], 1
    )
    dqkv16 = jnp.concatenate(
        [dqueries.reshape(total_rows, -1).astype(b16), dkv.reshape(total_rows, -1).astype(b16)], 1
    )
    bounds = ((0, wide), (wide, wide + kv_wide), (wide + kv_wide, wide + 2 * kv_wide))
    seconds = (query_adapter_up, key_adapter_up, value_adapter_up)
    dinner = jnp.concatenate(
        [dot_t(dqkv16[:, a:b], second) for (a, b), second in zip(bounds, seconds)], 1
    ).astype(b16)
    dnormed = (dot_t(dqkv16, qkv_w) + dot_t(dinner, downs)).astype(b16)
    down_terms = t_dot(dinner, normed)
    inner16 = inner.astype(b16)
    up_terms = [
        t_dot(inner16[:, i * rank : (i + 1) * rank], dqkv16[:, a:b]) for i, (a, b) in enumerate(bounds)
    ]
    from_other = swap_core(lax.dynamic_slice_in_dim(dnormed, (1 - m) * half, half, 0))
    dnormed = my_half(dnormed).astype(f32) + from_other.astype(f32)
    x_half, r_half = my_half(inputs), my_half(rms_attn)
    attn_gain_term = jnp.sum(dnormed * x_half * r_half, 0)
    tokens_grad = both_halves(dresid + norm_back(x_half, r_half, gain_attn, dnormed)).reshape(
        seq_count, rows_here, width
    )

    shared = [attn_gain_term, mlp_gain_term, down_terms, oup_term]
    split = up_terms + [odown_term, dqmaps, dkmaps]
    flat = [a.reshape(-1, 128) for a in shared + split]
    sizes = [a.shape[0] for a in flat]
    shared_rows = sum(sizes[:4])
    flat = jnp.concatenate(flat, 0)
    flat = jnp.pad(flat, ((0, -flat.shape[0] % 128), (0, 0)))
    summed = plane_total(n, flat, shared_rows, 8).reshape(-1, 128).astype(f32)
    parts, at = [], 0
    for term, size in zip(shared + split, sizes):
        parts.append(summed[at : at + size].reshape(term.shape))
        at += size
    attn_gain, mlp_gain, downs_g, oup, qup, kup, vup, odown, qmaps_g, kmaps_g = parts
    downs_g = downs_g.T
    return (
        output,
        tokens_grad,
        attn_gain,
        mlp_gain,
        downs_g[:, :rank],
        qup,
        downs_g[:, rank : 2 * rank],
        kup,
        downs_g[:, 2 * rank :],
        vup,
        odown.T,
        oup,
        qmaps_g.reshape(query_feature_matrix.shape),
        kmaps_g,
    )


def solution(mesh):
    placed = (
        P("dp", "seq", None),
        P("dp", "seq", None),
        P(),
        P(),
        P("seq", "mp"),
        P("seq", "mp"),
        P("seq", "mp"),
        P("mp", "seq"),
        P("seq", "mp"),
        P("seq", "mp"),
        P("mp", "seq"),
        P(),
        P(None, "mp"),
        P(),
        P(None, "mp"),
        P(),
        P(None, "mp"),
        P("mp", None),
        P(),
        P("mp", None, None),
        P("mp", None, None),
    )
    return jax.shard_map(
        per_device,
        mesh=mesh,
        in_specs=placed,
        out_specs=(
            P("dp", "seq", None),
            P("dp", "seq", None),
            P(),
            P(),
            P(),
            P(None, "mp"),
            P(),
            P(None, "mp"),
            P(),
            P(None, "mp"),
            P("mp", None),
            P(),
            P("mp", None, None),
            P("mp", None, None),
        ),
        check_vma=False,
    )
```

time: 1780 us -> 759 us (0.43)
  waiting for transfers between devices: 1340 us -> 0.09 us
  Pallas kernels: 0 us -> 382 us
  blocking collectives: 62.7 us -> 0 us
  matrix products: 234 us -> 212 us
  local copies, waits for them, and re-layouts: 60.5 us -> 79.2 us
    all_gather x7 -> x3, waiting for transfers between devices: 949 us -> 0.02 us  [the longest x1 0.02 us: per_device(): lax.all_gather(lax.dynamic_slice_in_dim(up_weight, d * units, units, 1),...]
    pallas_call x0 -> x8, Pallas kernels: none -> 382 us  [the longest x1 137 us: gather_weights(): pl.pallas_call(functools.partial(gather_weights_kernel, n, k), out_shape=...]
    psum x6 -> x0, waiting for transfers between devices: 382 us -> none  [the longest x2 229 us: per_device(): lax.psum((qup_term, key_up_product, vup_term, odown_term, dqmaps.reshape(...]
    all_gather x4 -> x0, blocking collectives: 62.7 us -> none  [the longest x2 34 us: entering(): lax.all_gather(a.astype(kind), axis)]
    dot_general x38 -> x34, matrix products: 158 us -> 128 us  [the longest x14 70 us: dot_t(): lax.dot_general(left, right, (((1,), (1,)), ((), ())), preferred_element_...]
  transfers between devices with their start and end apart: 17 -> 10, of which waited for: 13 -> 0; matrix products, arithmetic and copies ran while one was open for 12% -> 30% of each run, Pallas kernels for 0% -> 40%
where the time goes in v1:
time: 759 us; the launch traced here: 749 us
  Pallas kernels  382 us (50%)
  matrix products  212 us (28%)
  local copies, waits for them, and re-layouts  79.2 us (10%)
  other arithmetic  55.6 us (7%)
  between operations  16 us (2%)
    pallas_call x1, Pallas kernels, gather_weights(): pl.pallas_call(functools.partial(gather_weights_kernel, n, k), out_shape=...  137 us
    pallas_call x2, Pallas kernels, plane_gather(): pl.pallas_call(plane_gather_kernel, out_shape=jax.ShapeDtypeStruct((4, 2)...  84.3 us
    pallas_call x2, Pallas kernels, plane_scatter(): pl.pallas_call(plane_scatter_kernel, out_shape=jax.ShapeDtypeStruct((r, w...  80.8 us
    dot_general x14, matrix products, dot_t(): lax.dot_general(left, right, (((1,), (1,)), ((), ())), preferred_element_...  70 us
    dot_general x14, matrix products, dot(): return jnp.dot(left, right, preferred_element_type=f32)  53.7 us
    pallas_call x2, Pallas kernels, line_sum(): pl.pallas_call(functools.partial(line_sum_kernel, n, up), out_shape=jax.S...  50.4 us
    pallas_call x1, Pallas kernels, plane_total(): pl.pallas_call(functools.partial(plane_total_kernel, n, shared), out_shap...  29.6 us
    dot_general x3, matrix products, attend(): jnp.einsum('tkgd,ekd->kgte', query_rows, key_block, preferred_element_typ...  27.5 us
  transfers between devices with their start and end apart: 10, of which 0 were waited for; matrix products, arithmetic and copies ran while one was open for 30% of the time, Pallas kernels for 40%

profile of v1, /device:TPU:0, one launch (start us, length us, event | category | flops | bytes accessed | tf_op | source)
XLA Modules:
  0.0 749.2 jit_solution(14484612229378446172)
XLA Ops:
  12.3 137.3 %gather_weights.1 = (bf16[4,512,1536]{2,1,0:T(8,128)(2,1)}, bf16[4,1024,512]{2,1,0:T(8,128)(2,1)}) custom-call(bf16[512,1536]{1,0:T(8,128)(2,1)} %pad_maximum_fusion.5.refs_0_, bf16[1024,512]{1,0:T(8,128)(2,1)} %refs_1_.1), custom_call_target="tpu_custom_call" | custom-call | tf_op jit(solution)/shard_map/gather_weights/pallas_call | solution.py:166
  153.9 3.4 fusion.224
  173.5 4.2 fusion.212
  177.8 4.2 broadcast_divide_fusion.1
  199.0 6.2 line_sum_3.1
  205.8 4.4 fusion.19
  210.2 3.4 copy.290
  217.4 4.1 fusion.223
  242.2 43.3 %plane_gather_2.1 = bf16[4,2,256,2048]{3,2,1,0:T(8,128)(2,1)} custom-call(bf16[256,2048]{1,0:T(8,128)(2,1)} %constant_dynamic-slice_fusion.2.own), custom_call_target="tpu_custom_call" | custom-call | tf_op jit(solution)/shard_map/plane_gather_2/pallas_call | solution.py:230
  291.0 41.0 %plane_gather_4.1 = bf16[4,2,256,2048]{3,2,1,0:T(8,128)(2,1)} custom-call(bf16[256,2048]{1,0:T(8,128)(2,1)} %multiply_convert_fusion.8.own), custom_call_target="tpu_custom_call" | custom-call | tf_op jit(solution)/shard_map/plane_gather_4/pallas_call | solution.py:230
  332.1 14.8 %fusion.227 = f32[2048,1024]{1,0:T(8,128)} fusion(bf16[2048,2048]{1,0:T(8,128)(2,1)} %bitcast.341, bf16[2048,1024]{1,0:T(8,128)(2,1)} %all-gather.6.cloned.1.call-done), kind=kOutput, calls=%fused_computation.320 | convolution fusion | flops 8589934592 | bytes 20971520 | tf_op jit(solution)/shard_map/dot_general | solution.py:576
  346.8 14.5 %fusion.226 = f32[2048,1024]{1,0:T(8,128)} fusion(bf16[2048,2048]{1,0:T(8,128)(2,1)} %bitcast.342, bf16[2048,1024]{1,0:T(8,128)(2,1)} %all-gather.4.cloned.1.call-done), kind=kOutput, calls=%fused_computation.319 | convolution fusion | flops 8589934592 | bytes 20971520 | tf_op jit(solution)/shard_map/dot_general | solution.py:576
  361.3 13.8 %convolution_convert_fusion = bf16[2048,2048]{1,0:T(8,128)(2,1)S(1)} fusion(bf16[1024,2048]{1,0:T(8,128)(2,1)} %all-gather.8.cloned.1.call-done, f32[2048,1024]{1,0:T(8,128)} %fusion.227, f32[2048,1024]{1,0:T(8,128)} %fusion.226), kind=kOutput, calls=%fused_computation.22 | convolution fusion | flops 8606711808 | bytes 29360128 | tf_op jit(solution)/shard_map/dot_general | solution.py:576
  375.1 40.4 %plane_scatter_6.1 = f32[256,2048]{1,0:T(8,128)S(1)} custom-call(bf16[4,2,256,2048]{3,2,1,0:T(8,128)(2,1)S(1)} %bitcast.328), custom_call_target="tpu_custom_call" | custom-call | tf_op jit(solution)/shard_map/plane_scatter_6/pallas_call | solution.py:304
  415.6 13.5 %fusion.228 = f32[2048,1024]{1,0:T(8,128)} fusion(bf16[2048,2048]{1,0:T(8,128)(2,1)} %bitcast.340, bf16[1024,2048]{1,0:T(8,128)(2,1)S(1)} %copy-done.131), kind=kOutput, calls=%fused_computation.321 | convolution fusion | flops 8589934592 | bytes 20971520 | tf_op jit(solution)/shard_map/dot_general | solution.py:580
  429.0 22.9 %fusion.14 = f32[2048,2048]{1,0:T(8,128)} fusion(bf16[2048,1024]{1,0:T(8,128)(2,1)} %all-gather.4.cloned.1.call-done, f32[2048,1024]{1,0:T(8,128)} %fusion.226, f32[2048,1024]{1,0:T(8,128)} %fusion.228, f32[2048,1024]{1,0:T(8,128)} %fusion.227), kind=kOutput, calls=%fused_computation.32 | convolution fusion | flops 8610906112 | bytes 46137344 | tf_op jit(solution)/shard_map/dot_general | solution.py:580
  451.9 21.1 %add_convert_fusion = bf16[2048,2048]{1,0:T(8,128)(2,1)} fusion(f32[2048,2048]{1,0:T(8,128)} %fusion.14, bf16[2048,1024]{1,0:T(8,128)(2,1)} %all-gather.6.cloned.1.call-done, f32[2048,1024]{1,0:T(8,128)} %fusion.228, f32[2048,1024]{1,0:T(8,128)} %fusion.226), kind=kOutput, calls=%fused_computation.4 | convolution fusion | flops 8610906112 | bytes 46137344 | tf_op jit(solution)/shard_map/dot_general | solution.py:580
  473.0 3.4 copy-done.1
  476.4 40.4 %plane_scatter_5.1 = f32[256,2048]{1,0:T(8,128)S(1)} custom-call(bf16[4,2,256,2048]{3,2,1,0:T(8,128)(2,1)S(1)} %bitcast.327), custom_call_target="tpu_custom_call" | custom-call | tf_op jit(solution)/shard_map/plane_scatter_5/pallas_call | solution.py:304
  535.4 6.1 reshape.385
  541.5 4.8 copy.246
  546.3 4.5 fusion.34
  555.8 44.2 %line_sum_7.1 = f32[528,128]{1,0:T(8,128)S(1)} custom-call(bf16[528,128]{1,0:T(8,128)(2,1)S(1)} %fusion.151.own), custom_call_target="tpu_custom_call" | custom-call | tf_op jit(solution)/shard_map/line_sum_7/pallas_call | solution.py:372
  600.8 6.1 fusion.11
  607.0 5.1 add_bitcast_fusion
  618.0 12.2 %convolution_bitcast_fusion.1 = f32[2,320,4,64]{1,3,2,0:T(8,128)} fusion(bf16[2,256,4,4,64]{1,0,4,3,2:T(2,128)(2,1)} %copy-done.14, f32[2,4,4,256,320]{3,4,2,1,0:T(8,128)} %get-tuple-element.78, f32[2,4,320,256,4]{3,2,4,1,0:T(8,128)} %copy-done.18, f32[2,4,256,4]{2,3,1,0:T(4,128)S(1)} %negate_bitcast_fusion.1, pred[320,256]{1,0:T(8,128)(4,1)S(1)} %copy-done.93), kind=kOutput, calls=%fused_computation.118 | convolution fusion | flops 353894400 | bytes 22790144 | tf_op jit(solution)/shard_map/transpose(jvp(vmap(tkgd,ekd->kgte)))/dot_general | solution.py:547
  630.2 12.5 %fusion.27 = bf16[2,256,4,4,64]{1,4,3,2,0:T(8,128)(2,1)} fusion(f32[4,4,2,256,64]{3,4,1,0,2:T(8,128)} %fusion.36, bf16[2,320,4,64,1]{1,3,4,2,0:T(8,128)(2,1)S(1)} %bitcast.358, f32[2,4,4,256,320]{3,4,2,1,0:T(8,128)} %get-tuple-element.78, f32[2,4,320,256,4]{3,2,4,1,0:T(8,128)} %copy-done.18, f32[2,4,256,4]{2,3,1,0:T(4,128)} %copy-done.71, ...), kind=kOutput, calls=%fused_computation.56 | convolution fusion | flops 354942976 | bytes 24559616 | tf_op jit(solution)/shard_map/transpose(jvp(vmap(tkgd,ekd->kgte)))/dot_general | solution.py:547
  644.1 5.7 fusion.70
  652.6 5.1 bitcast_add_fusion.3
  676.7 5.6 fusion.43
  697.5 4.0 subtract_add_fusion
  701.9 29.6 %plane_total_8.1 = bf16[4,352,128]{2,1,0:T(8,128)(2,1)S(1)} custom-call(f32[1408,128]{1,0:T(8,128)S(1)} %pad.23.part), custom_call_target="tpu_custom_call" | custom-call | tf_op jit(solution)/shard_map/plane_total_8/pallas_call | solution.py:494
  (456 shorter events, 151.5 us)
Async XLA Ops:
  7.2 162.3 %copy-start = (bf16[16,64,64]{2,1,0:T(8,128)(2,1)S(1)}, bf16[16,64,64]{2,1,0:T(8,128)(2,1)}, u32[]{:S(2)}) copy-start(bf16[16,64,64]{2,1,0:T(8,128)(2,1)} %param.40) | copy-start | bytes 393220
  7.2 324.8 %all-gather.6.cloned.1.call-start = ((), (), s32[]{:S(2)}) async-start(), calls=%async_computation.1 | async-start | bytes 5242880 | tf_op jit(solution)/shard_map/all_gather | solution.py:638
  9.7 337.1 %all-gather.4.cloned.1.call-start = ((), (), s32[]{:S(2)}) async-start(), calls=%async_computation | async-start | bytes 5242880 | tf_op jit(solution)/shard_map/all_gather | solution.py:637
  9.8 141.2 %copy-start.79 = (f32[2048]{0:T(1024)}, f32[2048]{0:T(1024)S(1)}, u32[]{:S(2)}) copy-start(f32[2048]{0:T(1024)S(1)} %convert_element_type.136) | copy-start | bytes 24580
  11.0 138.6 %copy-start.114 = (bf16[2048,8]{0,1:T(8,128)(2,1)S(1)}, bf16[2048,8]{0,1:T(8,128)(2,1)}, u32[]{:S(2)}) copy-start(bf16[2048,8]{0,1:T(8,128)(2,1)} %param.32) | copy-start | bytes 98308
  12.3 137.4 %copy-start.115 = (bf16[2048,8]{0,1:T(8,128)(2,1)S(1)}, bf16[2048,8]{0,1:T(8,128)(2,1)}, u32[]{:S(2)}) copy-start(bf16[2048,8]{0,1:T(8,128)(2,1)} %param.34) | copy-start | bytes 98308
  12.3 137.4 %copy-start.116 = (bf16[2048,8]{0,1:T(8,128)(2,1)S(1)}, bf16[2048,8]{0,1:T(8,128)(2,1)}, u32[]{:S(2)}) copy-start(bf16[2048,8]{0,1:T(8,128)(2,1)} %param.36) | copy-start | bytes 98308
  151.0 13.7 %copy-start.77 = (bf16[512,24]{0,1:T(8,128)(2,1)}, bf16[512,24]{0,1:T(8,128)(2,1)S(1)}, u32[]{:S(2)}) copy-start(bf16[512,24]{0,1:T(8,128)(2,1)S(1)} %convolution_convert_fusion.2) | copy-start | bytes 73732
  160.4 22.4 %collective-permute-start = (bf16[2,64,512]{2,1,0:T(8,128)(2,1)}, bf16[2,64,512]{2,1,0:T(8,128)(2,1)}, u32[]{:S(2)}, u32[]{:S(2)}) collective-permute-start(bf16[2,64,512]{2,1,0:T(8,128)(2,1)} %pad_maximum_fusion.13), channel_id=1, source_target_pairs={{0,8},{8,16},{16,24},{1,9},{9,17},{17,25},{2,10},{10,18},{18,26},{... | collective-permute-start | bytes 393224 | tf_op jit(solution)/shard_map/ppermute | solution.py:596
  164.6 196.7 %all-gather.8.cloned.1.call-start = ((), (), s32[]{:S(2)}) async-start(), calls=%async_computation.2 | async-start | bytes 5242880 | tf_op jit(solution)/shard_map/all_gather | solution.py:639
  169.4 45.1 %copy-start.14 = (bf16[2,256,4,4,64]{1,0,4,3,2:T(2,128)(2,1)}, bf16[2,256,4,4,64]{1,0,4,3,2:T(2,128)(2,1)S(1)}, u32[]{:S(2)}) copy-start(bf16[2,256,4,4,64]{1,0,4,3,2:T(2,128)(2,1)S(1)} %reshape.321) | copy-start | bytes 3145732
  173.5 8.5 %copy-start.126 = (s32[256]{0:T(256)}, s32[256]{0:T(256)S(1)}, u32[]{:S(2)}) copy-start(s32[256]{0:T(256)S(1)} %iota_add_fusion) | copy-start | bytes 3076
  177.8 17.0 %copy-start.120 = (pred[320]{0:T(512)(128)(4,1)}, pred[320]{0:T(512)(128)(4,1)S(1)}, u32[]{:S(2)}) copy-start(pred[320]{0:T(512)(128)(4,1)S(1)} %add_compare_fusion) | copy-start | bytes 964
  235.0 50.5 %collective-permute-start.1 = (bf16[256,2048]{1,0:T(8,128)(2,1)S(1)}, bf16[256,2048]{1,0:T(8,128)(2,1)}, u32[]{:S(2)}, u32[]{:S(2)}) collective-permute-start(bf16[256,2048]{1,0:T(8,128)(2,1)S(1)} %dynamic-slice_convert_fusion), channel_id=1, source_target_pairs={{0,4},{4,0},{1,5},{5,1},{2,6},{6,2},{3,7},{7,3},{8,12},{12,8},{9,1... | collective-permute-start | bytes 3145736 | tf_op jit(solution)/shard_map/ppermute | solution.py:600
  375.1 40.5 %copy-start.131 = (bf16[1024,2048]{1,0:T(8,128)(2,1)S(1)}, bf16[1024,2048]{1,0:T(8,128)(2,1)}, u32[]{:S(2)}) copy-start(bf16[1024,2048]{1,0:T(8,128)(2,1)} %all-gather.8.cloned.1.call-done) | copy-start | bytes 12582916
  476.4 40.4 %copy-start.6 = (f32[256,2048]{1,0:T(8,128)S(1)}, f32[256,2048]{1,0:T(8,128)}, u32[]{:S(2)}) copy-start(f32[256,2048]{1,0:T(8,128)} %copy-done.5) | copy-start | bytes 6291460
  520.8 6.5 copy-start.37
  520.8 6.5 collective-permute-start.3
  526.8 144.5 %collective-permute-start.2 = (bf16[256,2048]{1,0:T(8,128)(2,1)}, bf16[256,2048]{1,0:T(8,128)(2,1)}, u32[]{:S(2)}, u32[]{:S(2)}) collective-permute-start(bf16[256,2048]{1,0:T(8,128)(2,1)} %get-tuple-element.40), channel_id=1, source_target_pairs={{0,4},{4,0},{1,5},{5,1},{2,6},{6,2},{3,7},{7,3},{8,12},{12,8},{9,1... | collective-permute-start | bytes 3145736 | tf_op jit(solution)/shard_map/ppermute | solution.py:600
  553.0 64.9 %copy-start.71 = (f32[2,4,256,4]{2,3,1,0:T(4,128)}, f32[2,4,256,4]{2,3,1,0:T(4,128)S(1)}, u32[]{:S(2)}) copy-start(f32[2,4,256,4]{2,3,1,0:T(4,128)S(1)} %negate_bitcast_fusion.1) | copy-start | bytes 98308
  553.4 47.4 %copy-start.10 = (f32[2,256,4,4,64]{1,4,3,2,0:T(8,128)S(1)}, f32[2,256,4,4,64]{1,4,3,2,0:T(8,128)}, u32[]{:S(2)}) copy-start(f32[2,256,4,4,64]{1,4,3,2,0:T(8,128)} %copy.246) | copy-start | bytes 6291460
  553.4 47.4 %copy-start.36 = (bf16[2,320,256]{1,2,0:T(8,128)(2,1)S(1)}, bf16[2,320,256]{1,2,0:T(8,128)(2,1)}, u32[]{:S(2)}) copy-start(bf16[2,320,256]{1,2,0:T(8,128)(2,1)} %copy.225) | copy-start | bytes 983044
  600.0 6.9 copy-start.2
  600.8 6.1 copy-start.27
  600.8 6.1 copy-start.30
  618.0 12.2 %copy-start.46 = (bf16[2,320,256]{1,2,0:T(8,128)(2,1)S(1)}, bf16[2,320,256]{1,2,0:T(8,128)(2,1)}, u32[]{:S(2)}) copy-start(bf16[2,320,256]{1,2,0:T(8,128)(2,1)} %copy.226) | copy-start | bytes 983044
  630.2 13.6 %copy-start.60 = (bf16[2,256,4,128]{1,3,0,2:T(8,128)(2,1)S(1)}, bf16[2,256,4,128]{1,3,0,2:T(8,128)(2,1)}, u32[]{:S(2)}) copy-start(bf16[2,256,4,128]{1,3,0,2:T(8,128)(2,1)} %copy-done.59) | copy-start | bytes 1572868
  644.1 7.1 slice-start
  644.1 7.1 copy-start.121
  665.7 9.7 %collective-permute-start.4 = (bf16[2,64,512]{2,1,0:T(8,128)(2,1)S(1)}, bf16[2,64,512]{2,1,0:T(8,128)(2,1)S(1)}, u32[]{:S(2)}, u32[]{:S(2)}) collective-permute-start(bf16[2,64,512]{2,1,0:T(8,128)(2,1)S(1)} %slice.207), channel_id=1, source_target_pairs={{8,0},{16,8},{24,16},{9,1},{17,9},{25,17},{10,2},{18,10},{26,18},{... | collective-permute-start | bytes 393224 | tf_op jit(solution)/shard_map/ppermute | solution.py:596
  684.2 10.1 %collective-permute-start.5 = (bf16[256,2048]{1,0:T(8,128)(2,1)}, bf16[256,2048]{1,0:T(8,128)(2,1)}, u32[]{:S(2)}, u32[]{:S(2)}) collective-permute-start(bf16[256,2048]{1,0:T(8,128)(2,1)} %constant_dynamic-slice_fusion), channel_id=1, source_target_pairs={{0,4},{4,0},{1,5},{5,1},{2,6},{6,2},{3,7},{7,3},{8,12},{12,8},{9,1... | collective-permute-start | bytes 3145736 | tf_op jit(solution)/shard_map/ppermute | solution.py:600
  701.4 36.4 %collective-permute-start.6 = (f32[256,2048]{1,0:T(8,128)}, f32[256,2048]{1,0:T(8,128)S(1)}, u32[]{:S(2)}, u32[]{:S(2)}) collective-permute-start(f32[256,2048]{1,0:T(8,128)} %subtract_add_fusion), channel_id=1, source_target_pairs={{0,4},{4,0},{1,5},{5,1},{2,6},{6,2},{3,7},{7,3},{8,12},{12,8},{9,1... | collective-permute-start | bytes 6291464 | tf_op jit(solution)/shard_map/ppermute | solution.py:600
  (112 other events, 330.3 us)
Sparse Core Ops, SparseCore 0:
  9.8 115.2 all-gather.5
  164.7 80.3 all-gather.3
  246.7 101.3 all-gather.7

commit v2 on v1

--- a/solution.py
+++ b/solution.py
@@ -519,54 +519,662 @@
     )(part)
 
 
-def key_features(key_block, feature_maps):
-    logits = jnp.einsum("ekd,kdf->ekf", key_block, feature_maps, preferred_element_type=jnp.float32)
-    return jnp.concatenate([jax.nn.softmax(logits, -1), jax.nn.softmax(-logits, -1)], -1)
-
-
-def query_features(query_rows, feature_maps):
-    logits = jnp.einsum(
-        "tkgd,kgdf->tkgf", query_rows, feature_maps, preferred_element_type=jnp.float32
-    )
-    return jnp.concatenate([jax.nn.softmax(logits, -1), jax.nn.softmax(-logits, -1)], -1)
-
-
-def state_piece(features, values, valid_mask, rows_here):
-    kept_feats = jnp.where(valid_mask[:rows_here, None, None], features[:rows_here], 0.0)
-    state_sum = jnp.einsum(
-        "ekf,ekd->kfd", kept_feats, values[:rows_here], preferred_element_type=jnp.float32
-    )
-    return (state_sum, jnp.sum(kept_feats, 0))
-
-
-def attend(query_rows, key_block, values, features, state_sum, totals, feature_maps, valid_mask):
-    rows_here = query_rows.shape[0]
-    extent = key_block.shape[0]
-    reach_back = extent - rows_here
-    query_feats = query_features(query_rows, feature_maps)
-    scores = jnp.einsum(
-        "tkgd,ekd->kgte", query_rows, key_block, preferred_element_type=jnp.float32
-    ) / math.sqrt(query_rows.shape[-1])
-    rowpos = jnp.arange(rows_here, dtype=jnp.int32)[:, None]
-    colpos = jnp.arange(extent, dtype=jnp.int32)[None, :]
-    inside = (colpos > rowpos) & (colpos <= rowpos + reach_back) & valid_mask[None, :]
-    older_mask = (colpos <= rowpos) & valid_mask[None, :]
-    window_part = jnp.where(inside, jnp.exp(jnp.where(inside, scores, 0.0)), 0.0)
-    linear_part = jnp.where(
-        older_mask,
-        jnp.einsum("tkgf,ekf->kgte", query_feats, features, preferred_element_type=jnp.float32),
-        0.0,
-    )
-    weights = window_part + linear_part
-    numerator = jnp.einsum("kgte,ekd->tkgd", weights, values, preferred_element_type=jnp.float32)
-    numerator = numerator + jnp.einsum(
-        "tkgf,kfd->tkgd", query_feats, state_sum, preferred_element_type=jnp.float32
-    )
-    denominator = jnp.transpose(jnp.sum(weights, -1), (2, 0, 1))
-    denominator = denominator + jnp.einsum(
-        "tkgf,kf->tkg", query_feats, totals, preferred_element_type=jnp.float32
-    )
-    return numerator / denominator[..., None]
+SPAN, TILE = 64, 128
+REACH = TILE + SPAN
+
+
+def mm(left, right, contract=((1,), (0,))):
+    return lax.dot_general(left, right, (contract, ((), ())), preferred_element_type=jnp.float32)
+
+
+def halves(shape, value):
+    r = lax.broadcasted_iota(jnp.int32, shape, 0) // 64
+    c = lax.broadcasted_iota(jnp.int32, shape, 1) // 64
+    return jnp.where(r == c, value, 0.0).astype(jnp.bfloat16)
+
+
+def signed_map(matrix):
+    return jnp.concatenate([matrix, -matrix], 1)
+
+
+def maps_of(logits):
+    left = lax.broadcasted_iota(jnp.int32, logits.shape, 1) < 64
+    low = jnp.max(jnp.where(left, logits, -jnp.inf), -1, keepdims=True)
+    high = jnp.max(jnp.where(left, -jnp.inf, logits), -1, keepdims=True)
+    e = jnp.exp(logits - jnp.where(left, low, high))
+    sums = mm(e.astype(jnp.bfloat16), halves((128, 128), 1.0))
+    return e / sums
+
+
+def maps_back(maps, dmaps):
+    p = (maps * dmaps).astype(jnp.bfloat16)
+    return maps * (dmaps - mm(p, halves((128, 128), 1.0)))
+
+
+def with_ones(values, first):
+    rows = values.shape[0]
+    r = lax.broadcasted_iota(jnp.int32, (rows, 64), 0)
+    c = lax.broadcasted_iota(jnp.int32, (rows, 64), 1)
+    ones = jnp.where((c == 0) & (r >= first), 1.0, 0.0).astype(jnp.bfloat16)
+    return jnp.concatenate([values, ones], 1)
+
+
+def pick(column):
+    r = lax.broadcasted_iota(jnp.int32, (8, 128), 0)
+    c = lax.broadcasted_iota(jnp.int32, (8, 128), 1)
+    return jnp.where((r == 0) & (c == column), 1.0, 0.0).astype(jnp.bfloat16)
+
+
+def identity():
+    r = lax.broadcasted_iota(jnp.int32, (128, 128), 0)
+    c = lax.broadcasted_iota(jnp.int32, (128, 128), 1)
+    return jnp.where(r == c, 1.0, 0.0).astype(jnp.bfloat16)
+
+
+def start_row():
+    return jnp.where(lax.axis_index("seq") == 0, SPAN, 0)
+
+
+def key_state_kernel(kv, kmaps, out):
+    first = start_row()
+    b16 = jnp.bfloat16
+    out[512:] = jnp.zeros((16, 128), b16)
+    for e in range(2):
+        for gp in range(2):
+            parts = []
+            for j in range(2):
+                g = 2 * gp + j
+                keys = kv[e, :256, g * 64 : g * 64 + 64]
+                values = with_ones(kv[e, :256, 256 + g * 64 : 320 + g * 64], first)
+                feats = maps_of(mm(keys, signed_map(kmaps[g]))).astype(b16)
+                state = mm(feats, values, ((0,), (0,)))
+                parts.append(state[:, :64])
+                total = mm(pick(64), state.astype(b16), ((1,), (1,)))
+                out[512 + e * 4 + g : 513 + e * 4 + g] = total[:1].astype(b16)
+            block = jnp.concatenate(parts, 1).astype(b16)
+            out[(e * 2 + gp) * 128 : (e * 2 + gp) * 128 + 128] = block
+
+
+def key_state(kv_ext, kmaps):
+    return pl.pallas_call(
+        key_state_kernel,
+        out_shape=jax.ShapeDtypeStruct((528, 128), jnp.bfloat16),
+        in_specs=[pl.BlockSpec(memory_space=pltpu.VMEM)] * 2,
+        out_specs=pl.BlockSpec(memory_space=pltpu.VMEM),
+        compiler_params=pltpu.CompilerParams(vmem_limit_bytes=40 << 20),
+        name="key_state",
+    )(kv_ext, kmaps)
+
+
+def masks():
+    r = lax.broadcasted_iota(jnp.int32, (TILE, REACH), 0)
+    c = lax.broadcasted_iota(jnp.int32, (TILE, REACH), 1)
+    return (c > r) & (c <= r + SPAN), c <= r
+
+
+def state_of(states, totals, e, gp, j):
+    b16 = jnp.bfloat16
+    column = mm(identity(), totals[...].astype(b16), ((1,), (1,)))
+    row = e * 4 + 2 * gp + j
+    pickcol = lax.broadcasted_iota(jnp.int32, column.shape, 1) == row
+    one = jnp.sum(jnp.where(pickcol, column, 0.0), -1, keepdims=True)
+    c = lax.broadcasted_iota(jnp.int32, (128, 64), 1)
+    return jnp.concatenate([states[:, j * 64 : j * 64 + 64], jnp.where(c == 0, one, 0.0)], 1)
+
+
+def attend_kernel(q, k, v, st, tot, qmaps, kmaps, out):
+    gp, e = pl.program_id(0), pl.program_id(1)
+    first = start_row()
+    b16 = jnp.bfloat16
+    window, older = masks()
+    for j in range(2):
+        keys = k[0, :, j * 64 : j * 64 + 64]
+        values = with_ones(v[0, :, j * 64 : j * 64 + 64], first)
+        kfeats = maps_of(mm(keys, signed_map(kmaps[j]))).astype(b16)
+        keys8 = keys * jnp.asarray(0.125, b16)
+        state = state_of(st, tot, e, gp, j)
+        for i in range(2):
+            if i:
+                state = state + mm(kfeats[:TILE], values[:TILE], ((0,), (0,)))
+            state16 = state.astype(b16)
+            reach = slice(i * TILE, i * TILE + REACH)
+            for h in range(0, 4, 2):
+                pair = []
+                for hh in (h, h + 1):
+                    col = (j * 4 + hh) * 64
+                    query = q[i * TILE : (i + 1) * TILE, col : col + 64]
+                    qfeats = maps_of(mm(query, signed_map(qmaps[j * 4 + hh]))).astype(b16)
+                    near = mm(query, keys8[reach], ((1,), (1,)))
+                    far = mm(qfeats, kfeats[reach], ((1,), (1,)))
+                    weights = jnp.where(window, jnp.exp(jnp.where(window, near, 0.0)), jnp.where(older, far, 0.0))
+                    both = mm(weights.astype(b16), values[reach]) + mm(qfeats, state16)
+                    pair.append(both[:, :64] / both[:, 64:65])
+                col = (j * 4 + h) * 64
+                out[i * TILE : (i + 1) * TILE, col : col + 128] = jnp.concatenate(pair, 1).astype(b16)
+
+
+def attend(q, kv_ext, st, qmaps, kmaps):
+    return pl.pallas_call(
+        attend_kernel,
+        grid=(2, 2),
+        out_shape=jax.ShapeDtypeStruct(q.shape, jnp.bfloat16),
+        in_specs=[
+            pl.BlockSpec((256, 512), lambda g, e: (e, g)),
+            pl.BlockSpec((1, 320, 128), lambda g, e: (e, 0, g)),
+            pl.BlockSpec((1, 320, 128), lambda g, e: (e, 0, 2 + g)),
+            pl.BlockSpec((128, 128), lambda g, e: (e * 2 + g, 0)),
+            pl.BlockSpec((16, 128), lambda g, e: (32, 0)),
+            pl.BlockSpec((8, 64, 64), lambda g, e: (g, 0, 0)),
+            pl.BlockSpec((2, 64, 64), lambda g, e: (g, 0, 0)),
+        ],
+        out_specs=pl.BlockSpec((256, 512), lambda g, e: (e, g)),
+        compiler_params=pltpu.CompilerParams(vmem_limit_bytes=40 << 20),
+        name="attend",
+    )(q, kv_ext, kv_ext, st, st, qmaps, kmaps)
+
+
+def attend_back_kernel(q, k, v, st, tot, qmaps, kmaps, dattn, dq, dk, dv, dkf, dst, dtot, dqm):
+    gp, e = pl.program_id(0), pl.program_id(1)
+    first = start_row()
+    b16, f32 = jnp.bfloat16, jnp.float32
+    window, older = masks()
+    eighth = jnp.asarray(0.125, b16)
+    dk[...] = jnp.zeros_like(dk)
+    dv[...] = jnp.zeros_like(dv)
+    dkf[...] = jnp.zeros_like(dkf)
+
+    @pl.when(e == 0)
+    def _():
+        dqm[...] = jnp.zeros_like(dqm)
+
+    dstates = []
+    for j in range(2):
+        keys = k[0, :, j * 64 : j * 64 + 64]
+        values = with_ones(v[0, :, j * 64 : j * 64 + 64], first)
+        kfeats = maps_of(mm(keys, signed_map(kmaps[j]))).astype(b16)
+        keys8 = keys * eighth
+        state = state_of(st, tot, e, gp, j)
+        gsum = None
+        for i in range(2):
+            if i:
+                state = state + mm(kfeats[:TILE], values[:TILE], ((0,), (0,)))
+            state16 = state.astype(b16)
+            reach = slice(i * TILE, i * TILE + REACH)
+            rows = slice(i * TILE, (i + 1) * TILE)
+            dvalue = dkey = dkfeat = g = None
+            for h in range(0, 4, 2):
+                dqs = []
+                for hh in (h, h + 1):
+                    head = j * 4 + hh
+                    query = q[rows, head * 64 : head * 64 + 64]
+                    grad = dattn[rows, head * 64 : head * 64 + 64].astype(f32)
+                    signed = signed_map(qmaps[head])
+                    qmap = maps_of(mm(query, signed))
+                    qfeats = qmap.astype(b16)
+                    near = mm(query, keys8[reach], ((1,), (1,)))
+                    far = mm(qfeats, kfeats[reach], ((1,), (1,)))
+                    close = jnp.where(window, jnp.exp(jnp.where(window, near, 0.0)), 0.0)
+                    weights = (close + jnp.where(older, far, 0.0)).astype(b16)
+                    both = mm(weights, values[reach]) + mm(qfeats, state16)
+                    inv = 1.0 / both[:, 64:65]
+                    grad = grad * inv
+                    c = jnp.sum(grad * both[:, :64], -1, keepdims=True) * inv
+                    lane = lax.broadcasted_iota(jnp.int32, (TILE, 64), 1)
+                    grad1 = jnp.concatenate([grad, jnp.where(lane == 0, -c, 0.0)], 1).astype(b16)
+                    dweights = mm(grad1, values[reach], ((1,), (1,)))
+                    ds = (close * dweights).astype(b16)
+                    dl = jnp.where(older, dweights, 0.0).astype(b16)
+                    dqmap = mm(dl, kfeats[reach]) + mm(grad1, state16, ((1,), (1,)))
+                    da = maps_back(qmap, dqmap).astype(b16)
+                    dqs.append(mm(ds, keys8[reach]) + mm(da, signed, ((1,), (1,))))
+                    x = mm(query, da, ((0,), (0,)))
+                    dqm[head] += x[:, :64] - x[:, 64:]
+                    a1 = mm(weights, grad1, ((0,), (0,)))
+                    a2 = mm(ds, query * eighth, ((0,), (0,)))
+                    a3 = mm(dl, qfeats, ((0,), (0,)))
+                    a4 = mm(qfeats, grad1, ((0,), (0,)))
+                    if dvalue is None:
+                        dvalue, dkey, dkfeat, g = a1, a2, a3, a4
+                    else:
+                        dvalue, dkey, dkfeat, g = dvalue + a1, dkey + a2, dkfeat + a3, g + a4
+                col = (j * 4 + h) * 64
+                dq[rows, col : col + 128] = jnp.concatenate(dqs, 1).astype(b16)
+            dv[0, reach, j * 64 : j * 64 + 64] += dvalue[:, :64]
+            dk[0, reach, j * 64 : j * 64 + 64] += dkey
+            dkf[0, j, reach] += dkfeat
+            if i:
+                g16 = g.astype(b16)
+                dkf[0, j, :TILE] += mm(values[:TILE], g16, ((1,), (1,)))
+                dv[0, :TILE, j * 64 : j * 64 + 64] += mm(kfeats[:TILE], g16)[:, :64]
+            gsum = g if gsum is None else gsum + g
+        dstates.append(gsum[:, :64])
+        dtot[0, 0, j * 8 : j * 8 + 8] = mm(pick(64), gsum.astype(b16), ((1,), (1,))).astype(b16)
+    dst[...] = jnp.concatenate(dstates, 1).astype(b16)
+
+
+def attend_back(q, kv_ext, st, qmaps, kmaps, dattn):
+    f32, b16 = jnp.float32, jnp.bfloat16
+    e2, ext = kv_ext.shape[:2]
+    return pl.pallas_call(
+        attend_back_kernel,
+        grid=(2, 2),
+        out_shape=[
+            jax.ShapeDtypeStruct(q.shape, b16),
+            jax.ShapeDtypeStruct((e2, ext, 256), f32),
+            jax.ShapeDtypeStruct((e2, ext, 256), f32),
+            jax.ShapeDtypeStruct((e2, 4, ext, 128), f32),
+            jax.ShapeDtypeStruct((512, 128), b16),
+            jax.ShapeDtypeStruct((2, 2, 16, 128), b16),
+            jax.ShapeDtypeStruct((16, 64, 64), f32),
+        ],
+        in_specs=[
+            pl.BlockSpec((256, 512), lambda g, e: (e, g)),
+            pl.BlockSpec((1, 320, 128), lambda g, e: (e, 0, g)),
+            pl.BlockSpec((1, 320, 128), lambda g, e: (e, 0, 2 + g)),
+            pl.BlockSpec((128, 128), lambda g, e: (e * 2 + g, 0)),
+            pl.BlockSpec((16, 128), lambda g, e: (32, 0)),
+            pl.BlockSpec((8, 64, 64), lambda g, e: (g, 0, 0)),
+            pl.BlockSpec((2, 64, 64), lambda g, e: (g, 0, 0)),
+            pl.BlockSpec((256, 512), lambda g, e: (e, g)),
+        ],
+        out_specs=[
+            pl.BlockSpec((256, 512), lambda g, e: (e, g)),
+            pl.BlockSpec((1, 320, 128), lambda g, e: (e, 0, g)),
+            pl.BlockSpec((1, 320, 128), lambda g, e: (e, 0, g)),
+            pl.BlockSpec((1, 2, 320, 128), lambda g, e: (e, g, 0, 0)),
+            pl.BlockSpec((128, 128), lambda g, e: (e * 2 + g, 0)),
+            pl.BlockSpec((1, 1, 16, 128), lambda g, e: (e, g, 0, 0)),
+            pl.BlockSpec((8, 64, 64), lambda g, e: (g, 0, 0)),
+        ],
+        compiler_params=pltpu.CompilerParams(vmem_limit_bytes=40 << 20),
+        name="attend_back",
+    )(q, kv_ext, kv_ext, st, st, qmaps, kmaps, dattn)
+
+
+def key_back_kernel(k, v, later, tot, kmaps, dk_in, dv_in, dkf, dk, dv, dkm):
+    gp, e = pl.program_id(0), pl.program_id(1)
+    first = start_row()
+    b16 = jnp.bfloat16
+
+    @pl.when(e == 0)
+    def _():
+        dkm[...] = jnp.zeros_like(dkm)
+
+    dks, dvs = [], []
+    for j in range(2):
+        cols = slice(j * 64, j * 64 + 64)
+        keys = k[0, :, cols]
+        values = with_ones(v[0, :, cols], first)
+        signed = signed_map(kmaps[j])
+        kmap = maps_of(mm(keys, signed))
+        g = state_of(later, tot, e, gp, j).astype(b16)
+        more = mm(values[:256], g, ((1,), (1,)))
+        dmap = jnp.concatenate([dkf[0, j, :256] + more, dkf[0, j, 256:]], 0)
+        da = maps_back(kmap, dmap).astype(b16)
+        dks.append(dk_in[0, :, cols] + mm(da, signed, ((1,), (1,))))
+        moved = mm(kmap[:256].astype(b16), g)[:, :64]
+        dvs.append(jnp.concatenate([dv_in[0, :256, cols] + moved, dv_in[0, 256:, cols]], 0))
+        x = mm(keys, da, ((0,), (0,)))
+        dkm[j] += x[:, :64] - x[:, 64:]
+    dk[0] = jnp.concatenate(dks, 1)
+    dv[0] = jnp.concatenate(dvs, 1)
+
+
+def key_back(kv_ext, later, kmaps, dk, dv, dkf):
+    f32 = jnp.float32
+    piece = pl.BlockSpec((1, 320, 128), lambda g, e: (e, 0, g))
+    return pl.pallas_call(
+        key_back_kernel,
+        grid=(2, 2),
+        out_shape=[
+            jax.ShapeDtypeStruct(dk.shape, f32),
+            jax.ShapeDtypeStruct(dv.shape, f32),
+            jax.ShapeDtypeStruct((4, 64, 64), f32),
+        ],
+        in_specs=[
+            piece,
+            pl.BlockSpec((1, 320, 128), lambda g, e: (e, 0, 2 + g)),
+            pl.BlockSpec((128, 128), lambda g, e: (e * 2 + g, 0)),
+            pl.BlockSpec((16, 128), lambda g, e: (32, 0)),
+            pl.BlockSpec((2, 64, 64), lambda g, e: (g, 0, 0)),
+            piece,
+            piece,
+            pl.BlockSpec((1, 2, 320, 128), lambda g, e: (e, g, 0, 0)),
+        ],
+        out_specs=[piece, piece, pl.BlockSpec((2, 64, 64), lambda g, e: (g, 0, 0))],
+        compiler_params=pltpu.CompilerParams(vmem_limit_bytes=40 << 20),
+        name="key_back",
+    )(kv_ext, kv_ext, later, later, kmaps, dk, dv, dkf)
+
+
+CHUNKS = 4
+
+
+def feed_kernel(n, k, early, xn_own, ct_own, packed, gate, up, down, dxn, out_part, *scratch):
+    (xn, ct, gw, uw, dw, da, oa, xin, yin, t2, xin2, yin2) = scratch[:12]
+    (o_sem, a_send, a_recv, w_sem, w_send, w_recv, z_sem, z_send, z_recv, c_send, c_recv, p_send, p_recv, st_sem) = scratch[12:]
+    spot = Spot()
+    s, m, d = spot.s, spot.m, spot.d
+    f32, b16 = jnp.float32, jnp.bfloat16
+    unit = gw.shape[3] // 2
+    wd = min(unit, k)
+    gs, ds = unit // wd, k // wd
+    half = xn.shape[1] // 2
+    A, B = pl.ds(0, half), pl.ds(half, half)
+
+    own = [pltpu.make_async_copy(xn_own, xn.at[3], o_sem.at[0]), pltpu.make_async_copy(ct_own, ct.at[3], o_sem.at[1])]
+    for c in own:
+        c.start()
+
+    lanes = pl.ds(pl.multiple_of(m * unit, unit), unit)
+
+    def own_piece(q):
+        start = pl.multiple_of(d * (CHUNKS * unit) + q * unit, unit)
+        return (
+            (gate.at[:, pl.ds(start, unit)], gw.at[q, s, :, lanes]),
+            (up.at[:, pl.ds(start, unit)], uw.at[q, s, :, lanes]),
+            (down.at[pl.ds(start, unit)], dw.at[q, s, lanes]),
+        )
+
+    def piece(q, w, who):
+        return (gw.at[q, who, :, lanes], uw.at[q, who, :, lanes], dw.at[q, who, lanes])[w]
+
+    late = tuple(range(early, CHUNKS))
+    own_weights = [
+        pltpu.make_async_copy(src, dst, z_sem.at[i, w])
+        for i, q in enumerate(late)
+        for w, (src, dst) in enumerate(own_piece(q))
+    ]
+    for c in own_weights:
+        c.start()
+
+    def early_parts(q):
+        parts = []
+        at = 0
+        for ref in (gw, uw):
+            for i in range(gs):
+                cols = pl.ds(pl.multiple_of(m * unit + i * wd, wd), wd)
+                parts.append((packed.at[:, q, pl.ds(at, k)], ref.at[q, :, :, cols]))
+                at += k
+        for i in range(ds):
+            parts.append((packed.at[:, q, pl.ds(at, unit)], dw.at[q, :, lanes, pl.ds(i * wd, wd)]))
+            at += unit
+        return parts
+
+    early_own = [
+        [pltpu.make_async_copy(src, dst, w_sem.at[q, i]) for i, (src, dst) in enumerate(early_parts(q))]
+        for q in range(early)
+    ]
+    for copies in early_own:
+        for c in copies:
+            c.start()
+
+    greet(spot, n, ("x", "y", "c", "up", "dn"))
+
+    def block_copy(a, kind, sending):
+        ref, src_own = ((xn, xn_own), (ct, ct_own))[a]
+        if kind < 2:
+            dst = ref.at[kind + 1]
+            src = src_own if sending else dst
+        else:
+            rows = (A, B)[kind - 2]
+            dst = ref.at[0, rows]
+            src = ref.at[(2, 1)[kind - 2], rows] if sending else dst
+        return remote(src, dst, a_send.at[a, kind], a_recv.at[a, kind], spot.to("xyxy"[kind]))
+
+    for a in range(2):
+        block_copy(a, 0, True).start()
+        block_copy(a, 1, True).start()
+
+    def sends(upward, t):
+        return ((s - t >= 0) & (s + 1 < n)) if upward else ((s + t < n) & (s > 0))
+
+    def receives(upward, t):
+        return s - 1 - t >= 0 if upward else s + 1 + t < n
+
+    def z_copy(i, w, upward, t, sending):
+        q = late[i]
+        way = 0 if upward else 1
+        who = (s - t if upward else s + t) if sending else (s - 1 - t if upward else s + 1 + t)
+        dst = piece(q, w, who)
+        src = own_piece(q)[w][0] if (t == 0 and sending) else dst
+        return remote(src, dst, z_send.at[i, w, way, t], z_recv.at[i, w, way, t], spot.to("up" if upward else "dn"))
+
+    for i in range(len(late)):
+        for w in range(3):
+            for upward in (True, False):
+
+                @pl.when(sends(upward, 0))
+                def _():
+                    z_copy(i, w, upward, 0, True).start()
+
+    def early_core(q):
+        return [
+            remote(src, dst, w_send.at[q, i], w_recv.at[q, i], spot.to("c")) for i, (src, dst) in enumerate(early_parts(q))
+        ]
+
+    def theirs(q, w, who):
+        other = pl.ds(pl.multiple_of((1 - m) * unit, unit), unit)
+        return (gw.at[q, who, :, other], uw.at[q, who, :, other], dw.at[q, who, other])[w]
+
+    def core_copy(i, w, who, sending):
+        q = late[i]
+        ref = piece(q, w, who) if sending else theirs(q, w, who)
+        return remote(ref, ref, c_send.at[i, w, who], c_recv.at[i, w, who], spot.to("c"))
+
+    for q in range(early):
+        for c in early_core(q):
+            c.start()
+
+    def relay(i, t):
+        for w in range(3):
+            for upward in (True, False):
+
+                @pl.when(receives(upward, t))
+                def _():
+                    z_copy(i, w, upward, t, False).wait_recv()
+                    if t + 1 < n - 1:
+
+                        @pl.when(sends(upward, t + 1))
+                        def _():
+                            z_copy(i, w, upward, t + 1, True).start()
+
+                    core_copy(i, w, s - 1 - t if upward else s + 1 + t, True).start()
+
+    for i in range(len(late)):
+        for w in range(3):
+            own_weights[3 * i + w].wait()
+            core_copy(i, w, s, True).start()
+
+    for c in own:
+        c.wait()
+
+    first = (
+        remote(xn.at[0, A], xin.at[1], p_send.at[0], p_recv.at[0], spot.to("x")),
+        remote(xn.at[0, B], yin.at[1], p_send.at[1], p_recv.at[1], spot.to("y")),
+        remote(xn.at[1, A], xin.at[0], p_send.at[2], p_recv.at[2], spot.to("x")),
+        remote(xn.at[2, B], yin.at[0], p_send.at[3], p_recv.at[3], spot.to("y")),
+    )
+    stores = [pltpu.make_async_copy(ct.at[i], out_part.at[i], st_sem.at[i]) for i in range(4)]
+
+    steps = 4 * CHUNKS
+    turns = {}
+    total = len(late) * (n - 1)
+    for j in range(total):
+        i, t = j // (n - 1), j % (n - 1)
+        at = min(4 * late[i], 2 + (4 * late[i] - 2) * (j + 1) // (i * (n - 1) + n - 1))
+        turns.setdefault(at, []).append((i, t))
+
+    @pl.loop(0, steps)
+    def _(step):
+        c = step // 4
+        last = step >= steps - 4
+        t = jnp.where(last, step % 4, 3 - step % 4)
+
+        for q in range(early):
+
+            @pl.when(step == 4 * q)
+            def _():
+                for copy in early_own[q]:
+                    copy.wait()
+                for copy in early_core(q):
+                    copy.wait_recv()
+
+        for at, jobs in turns.items():
+
+            @pl.when(step == at)
+            def _():
+                for i, t in jobs:
+                    relay(i, t)
+
+        for i, q in enumerate(late):
+
+            @pl.when(step == 4 * q)
+            def _():
+                for w in range(3):
+                    for who in range(n):
+                        core_copy(i, w, who, False).wait_recv()
+
+        @pl.when(step == 1)
+        def _():
+            for a in range(2):
+                block_copy(a, 1, False).wait_recv()
+                block_copy(a, 2, True).start()
+                block_copy(a, 0, False).wait_recv()
+                block_copy(a, 3, True).start()
+
+        @pl.when(step == 3)
+        def _():
+            for a in range(2):
+                for kind in (2, 3):
+                    block_copy(a, kind, False).wait_recv()
+                for kind in range(4):
+                    block_copy(a, kind, True).wait_send()
+
+        x, cot = xn[t], ct[t]
+        g_all = gw[c].reshape(n * k, 2 * unit)
+        u_all = uw[c].reshape(n * k, 2 * unit)
+        g = mm(x, g_all)
+        u = mm(x, u_all)
+        dh = mm(cot[:, :k], dw[c, 0], ((1,), (1,)))
+        for i in range(1, n):
+            dh = dh + mm(cot[:, i * k : (i + 1) * k], dw[c, i], ((1,), (1,)))
+        sig = 1.0 / (1.0 + jnp.exp(-g))
+        act = g * sig
+        hid = (act * u).astype(b16)
+        dg = (dh * u * sig * (1.0 + g * (1.0 - sig))).astype(b16)
+        du = (dh * act).astype(b16)
+        for i in range(n):
+            cols = slice(i * k, (i + 1) * k)
+            o = mm(hid, dw[c, i])
+            e = mm(dg, gw[c, i], ((1,), (1,))) + mm(du, uw[c, i], ((1,), (1,)))
+
+            @pl.when(step < 4)
+            def _():
+                oa[t, :, cols] = o
+                da[t, :, cols] = e
+
+            @pl.when(step >= 4)
+            def _():
+                oa[t, :, cols] += o
+                da[t, :, cols] += e
+
+        @pl.when(last)
+        def _():
+            xn[t] = da[t].astype(b16)
+            ct[t] = oa[t].astype(b16)
+
+        for i in range(4):
+
+            @pl.when(step == steps - 4 + i)
+            def _():
+                stores[i].start()
+                if i == 0:
+                    first[0].start()
+                    first[1].start()
+                elif i < 3:
+                    first[i + 1].start()
+
+    second = (
+        remote(t2.at[0], yin2, p_send.at[4], p_recv.at[4], spot.to("y")),
+        remote(t2.at[1], xin2, p_send.at[5], p_recv.at[5], spot.to("x")),
+    )
+    first[0].wait_recv()
+    t2[0] = (xn[2, A].astype(f32) + xin[1].astype(f32)).astype(b16)
+    second[0].start()
+    first[1].wait_recv()
+    t2[1] = (xn[1, B].astype(f32) + yin[1].astype(f32)).astype(b16)
+    second[1].start()
+    first[2].wait_recv()
+    first[3].wait_recv()
+    second[0].wait_recv()
+    dxn[A] = da[3, A] + xin[0].astype(f32) + yin2[...].astype(f32)
+    second[1].wait_recv()
+    dxn[B] = da[3, B] + yin[0].astype(f32) + xin2[...].astype(f32)
+
+    for c in stores:
+        c.wait()
+    for c in first + second:
+        c.wait_send()
+    for q in range(early):
+        for c in early_core(q):
+            c.wait_send()
+    for i in range(len(late)):
+        for w in range(3):
+            for who in range(n):
+                core_copy(i, w, who, True).wait_send()
+            for t in range(n - 1):
+                for upward in (True, False):
+
+                    @pl.when(sends(upward, t))
+                    def _():
+                        z_copy(i, w, upward, t, True).wait_send()
+
+
+def feed(n, early, xn_own, ct_own, packed, gate, up, down, cid):
+    DMA, V = pltpu.SemaphoreType.DMA, pltpu.VMEM
+    b, f32 = jnp.bfloat16, jnp.float32
+    r, w = xn_own.shape
+    k = gate.shape[0]
+    unit = gate.shape[1] // (4 * CHUNKS)
+    wd = min(unit, k)
+    pieces = 2 * (unit // wd) + k // wd
+    late = CHUNKS - early
+    scratch = [V((4, r, w), b), V((4, r, w), b)]
+    scratch += [V((CHUNKS, n, k, 2 * unit), b), V((CHUNKS, n, k, 2 * unit), b), V((CHUNKS, n, 2 * unit, k), b)]
+    scratch += [V((4, r, w), f32), V((4, r, w), f32)]
+    scratch += [V((2, r // 2, w), b), V((2, r // 2, w), b), V((2, r // 2, w), b), V((r // 2, w), b), V((r // 2, w), b)]
+    scratch += [DMA((2,)), DMA((2, 4)), DMA((2, 4))]
+    scratch += [DMA((max(early, 1), pieces))] * 3
+    scratch += [DMA((late, 3)), DMA((late, 3, 2, n - 1)), DMA((late, 3, 2, n - 1)), DMA((late, 3, n)), DMA((late, 3, n))]
+    scratch += [DMA((6,)), DMA((6,)), DMA((4,))]
+    return pl.pallas_call(
+        functools.partial(feed_kernel, n, k, early),
+        out_shape=[jax.ShapeDtypeStruct((r, w), f32), jax.ShapeDtypeStruct((4, r, w), b)],
+        in_specs=[pl.BlockSpec(memory_space=ANY)] * 6,
+        out_specs=[pl.BlockSpec(memory_space=pltpu.VMEM), pl.BlockSpec(memory_space=ANY)],
+        scratch_shapes=scratch,
+        compiler_params=pltpu.CompilerParams(collective_id=cid, has_side_effects=True, vmem_limit_bytes=62 << 20),
+        name="feed",
+    )(xn_own, ct_own, packed, gate, up, down)
+
+
+def pack_early(k, early, gate, up, down, d):
+    unit = gate.shape[1] // (4 * CHUNKS)
+    wd = min(unit, k)
+    at = d * (CHUNKS * unit)
+    g = lax.dynamic_slice_in_dim(gate, at, early * unit, 1)
+    u = lax.dynamic_slice_in_dim(up, at, early * unit, 1)
+    dn = lax.dynamic_slice_in_dim(down, at, early * unit, 0)
+    chunks = []
+    for q in range(early):
+        rows = [a[:, q * unit + i : q * unit + i + wd] for a in (g, u) for i in range(0, unit, wd)]
+        rows += [dn[q * unit : (q + 1) * unit, i : i + wd] for i in range(0, k, wd)]
+        chunks.append(jnp.concatenate(rows, 0))
+    return jnp.stack(chunks)
+
+
+EARLY = 3
 
 
 f32, b16 = jnp.float32, jnp.bfloat16
@@ -633,11 +1241,9 @@
     groups = query_feature_matrix.shape[0] // heads_kv
     extent = rows_here + SOFTMAX_SPAN
 
-    units = gate_weight.shape[1] // 4
-    gate_w = lax.all_gather(lax.dynamic_slice_in_dim(gate_weight, d * units, units, 1), "seq", axis=0, tiled=True)
-    up_w = lax.all_gather(lax.dynamic_slice_in_dim(up_weight, d * units, units, 1), "seq", axis=0, tiled=True)
-    down_w = lax.all_gather(lax.dynamic_slice_in_dim(down_weight, d * units, units, 0), "seq", axis=1, tiled=True)
-
+    packed = lax.all_gather(
+        pack_early(gate_weight.shape[0], EARLY, gate_weight, up_weight, down_weight, d), "seq"
+    )
     qkv_own = jnp.concatenate([query_weight, key_weight, value_weight], 1)
     qkv_g, out_g = gather_weights(n, [qkv_own, output_weight], 1)
     qkv_w = qkv_g.reshape(width, -1)
@@ -658,7 +1264,7 @@
     normed = (inputs * rms_attn * gain_attn).astype(b16)
 
     cot2 = cotangent.reshape(total_rows, width)
-    cot_all = plane_gather(my_half(cot2), 2).reshape(8 * half, width)
+    cot_half = my_half(cot2)
 
     downs = jnp.concatenate([query_adapter_down, key_adapter_down, value_adapter_down], 1)
     inner = dot(normed, downs)
@@ -677,42 +1283,9 @@
     value3 = value_half.reshape(seq_count, rows_here, heads_kv * head_size)
     kv3 = jnp.concatenate([key3, value3], -1)
     kv_prev = from_behind(kv3[:, rows_here - SOFTMAX_SPAN :], "seq", 1)
-    kv_ext = jnp.concatenate([kv_prev, kv3], 1).astype(f32)
-    key_ext = kv_ext[..., :kv_wide].reshape(seq_count, extent, heads_kv, head_size)
-    value_ext = kv_ext[..., kv_wide:].reshape(seq_count, extent, heads_kv, head_size)
-    valid_mask = position * rows_here - SOFTMAX_SPAN + jnp.arange(extent, dtype=jnp.int32) >= 0
-    kmaps = key_feature_matrix.astype(f32)
-    qmaps = query_feature_matrix.astype(f32).reshape(heads_kv, groups, head_size, head_size)
-
-    def features_all(key_in, maps_in):
-        return jax.vmap(key_features, (0, None))(key_in, maps_in)
-
-    features, features_back = jax.vjp(features_all, key_ext, kmaps)
-
-    def pieces_all(feats_in, values_in):
-        return jax.vmap(state_piece, (0, 0, None, None))(feats_in, values_in, valid_mask, rows_here)
-
-    (piece_state, piece_totals), pieces_back = jax.vjp(pieces_all, features, value_ext)
-
-    def line_totals(state, totals, up, cid):
-        flat = jnp.concatenate([state.reshape(-1, 128), totals.reshape(-1, 128)], 0)
-        flat = jnp.pad(flat, ((0, -flat.shape[0] % 16), (0, 0))).astype(b16)
-        summed = line_sum(n, flat, up, cid)
-        rows = state.size // 128
-        return summed[:rows].reshape(state.shape), summed[rows : rows + totals.size // 128].reshape(totals.shape)
-
-    state_sum, totals = line_totals(piece_state, piece_totals, True, 3)
-    queries5 = query_half.reshape(seq_count, rows_here, heads_kv, groups, head_size).astype(f32)
-
-    def attend_all(query_in, key_in, value_in, feats_in, state_in, totals_in, maps_in):
-        return jax.vmap(attend, (0, 0, 0, 0, 0, 0, None, None))(
-            query_in, key_in, value_in, feats_in, state_in, totals_in, maps_in, valid_mask
-        )
-
-    attn5, attend_back = jax.vjp(
-        attend_all, queries5, key_ext, value_ext, features, state_sum, totals, qmaps
-    )
-    attn16 = attn5.reshape(total_rows, -1).astype(b16)
+    kv_ext = jnp.concatenate([kv_prev, kv3], 1)
+    states = line_sum(n, key_state(kv_ext, key_feature_matrix), True, 3)
+    attn16 = attend(query_half, kv_ext, states, query_feature_matrix, key_feature_matrix)
     inner_output = dot(attn16, output_adapter_down)
     branch = jnp.concatenate([dot(attn16, out_g[i]) for i in range(n)], 1) + dot(
         inner_output.astype(b16), output_adapter_up
@@ -723,24 +1296,29 @@
     gain_mlp = feedforward_norm_gain.astype(f32)
     rms_mlp = lax.rsqrt(jnp.mean(resid * resid, -1, keepdims=True) + epsilon)
     normed_mlp = (resid * rms_mlp * gain_mlp).astype(b16)
-    normed_all = plane_gather(normed_mlp, 4).reshape(8 * half, width)
-
-    gate = dot(normed_all, gate_w)
-    up_vals = dot(normed_all, up_w)
-    dhidden = dot_t(cot_all, down_w)
-    sig = jax.nn.sigmoid(gate)
-    act = gate * sig
-    hidden = (act * up_vals).astype(b16)
-    dgate = (dhidden * up_vals * sig * (1.0 + gate * (1.0 - sig))).astype(b16)
-    dup = (dhidden * act).astype(b16)
-    dn_part = (dot_t(dgate, gate_w) + dot_t(dup, up_w)).astype(b16)
-    out_part = dot(hidden, down_w).astype(b16)
-    dnormed_mlp = plane_scatter(dn_part.reshape(4, 2, half, width), 5)
-    mlp_out = plane_scatter(out_part.reshape(4, 2, half, width), 6)
+    dnormed_mlp, out_part = feed(
+        n, EARLY, normed_mlp, cot_half, packed, gate_weight, up_weight, down_weight, 4
+    )
+
+    def swap_chip(value, bit):
+        return lax.ppermute(value, "dp", [(i, i ^ bit) for i in range(4)])
+
+    cut = half // 2
+    upper_in = swap_chip(out_part[0:2, :cut], 1)
+    lower_in = swap_chip(out_part[0::2, cut:], 2)
+    upper_in2 = swap_chip((out_part[2, :cut].astype(f32) + upper_in[0].astype(f32)).astype(b16), 2)
+    lower_in2 = swap_chip((out_part[1, cut:].astype(f32) + lower_in[0].astype(f32)).astype(b16), 1)
+    mlp_out = out_part[3].astype(f32) + jnp.concatenate(
+        [
+            upper_in[1].astype(f32) + upper_in2.astype(f32),
+            lower_in[1].astype(f32) + lower_in2.astype(f32),
+        ],
+        0,
+    )
     output = both_halves((resid + mlp_out).astype(b16)).reshape(seq_count, rows_here, width)
 
     mlp_gain_term = jnp.sum(dnormed_mlp * resid * rms_mlp, 0)
-    dresid = my_half(cot2).astype(f32) + norm_back(resid, rms_mlp, gain_mlp, dnormed_mlp)
+    dresid = cot_half.astype(f32) + norm_back(resid, rms_mlp, gain_mlp, dnormed_mlp)
     dresid16 = both_halves(dresid.astype(b16))
     du_o = dot_t(dresid16, output_adapter_up)
     oup_term = t_dot(inner_output.astype(b16), dresid16)
@@ -749,21 +1327,20 @@
     step = output_weight.shape[1]
     for i in range(n):
         dattn = dattn + dot_t(dresid16[:, i * step : (i + 1) * step], out_g[i])
-    dattn16 = dattn.astype(b16).astype(f32).reshape(attn5.shape)
-    dqueries, dkey_ext, dvalue_ext, dfeatures, dstate, dtotals, dqmaps = attend_back(dattn16)
-    later_state, later_totals = line_totals(dstate, dtotals, False, 7)
-    dfeatures_more, dvalue_more = pieces_back((later_state, later_totals))
-    dkey_more, dkmaps = features_back(dfeatures + dfeatures_more)
-    dkey_ext = (dkey_ext + dkey_more).reshape(seq_count, extent, heads_kv * head_size)
-    dvalue_ext = (dvalue_ext + dvalue_more).reshape(seq_count, extent, heads_kv * head_size)
-    dkv_ext = jnp.concatenate([dkey_ext, dvalue_ext], -1)
+    dq16, dk_ext, dv_ext, dkfeats, dstates, dtotals, dqmaps = attend_back(
+        query_half, kv_ext, states, query_feature_matrix, key_feature_matrix, dattn.astype(b16)
+    )
+    dtotals = jnp.pad(dtotals[:, :, ::8].reshape(-1, 128), ((0, 8), (0, 0)))
+    later = line_sum(n, jnp.concatenate([dstates, dtotals], 0), False, 7)
+    dk_ext, dv_ext, dkmaps = key_back(kv_ext, later, key_feature_matrix, dk_ext, dv_ext, dkfeats)
+    dkv_ext = jnp.concatenate([dk_ext, dv_ext], -1)
     back = from_behind(dkv_ext[:, :SOFTMAX_SPAN].astype(b16), "seq", -1).astype(f32)
     dkv = dkv_ext[:, SOFTMAX_SPAN:]
     dkv = jnp.concatenate(
         [dkv[:, : rows_here - SOFTMAX_SPAN], dkv[:, rows_here - SOFTMAX_SPAN :] + back], 1
     )
     dqkv16 = jnp.concatenate(
-        [dqueries.reshape(total_rows, -1).astype(b16), dkv.reshape(total_rows, -1).astype(b16)], 1
+        [dq16, dkv.reshape(total_rows, -1).astype(b16)], 1
     )
     bounds = ((0, wide), (wide, wide + kv_wide), (wide + kv_wide, wide + 2 * kv_wide))
     seconds = (query_adapter_up, key_adapter_up, value_adapter_up)

time: 759 us -> 692 us (0.912)
  matrix products: 212 us -> 21.9 us
  Pallas kernels: 382 us -> 520 us
  waiting for transfers between devices: 0.09 us -> 45.6 us
  local copies, waits for them, and re-layouts: 79.2 us -> 33.9 us
  other arithmetic: 55.6 us -> 40.9 us
    pallas_call x4 -> x5, Pallas kernels: 165 us -> 330 us  [the longest x1 199 us: feed(): pl.pallas_call(functools.partial(feed_kernel, n, k, early), out_shape=[ja...]
    dot_general x22 -> x0, matrix products: 76.6 us -> none  [the longest x3 27.5 us: attend(): jnp.einsum('tkgd,ekd->kgte', query_rows, key_block, preferred_element_typ...]
    dot_general x14 -> x11, matrix products: 70 us -> 11.3 us  [dot_t(): lax.dot_general(left, right, (((1,), (1,)), ((), ())), preferred_element_...]
    dot_general x14 -> x11, matrix products: 53.7 us -> 9.06 us  [dot(): return jnp.dot(left, right, preferred_element_type=f32)]
    ppermute x0 -> x4, waiting for transfers between devices: none -> 37.4 us  [swap_chip(): return lax.ppermute(value, 'dp', [(i, i ^ bit) for i in range(4)])]
    pallas_call x2, Pallas kernels: 50.4 us -> 23.3 us  [line_sum(): pl.pallas_call(functools.partial(line_sum_kernel, n, up), out_shape=jax.S...]
    reshape x11 -> x0, local copies, waits for them, and re-layouts: 20.3 us -> none  [the longest x2 10.9 us: per_device(): dattn16 = dattn.astype(b16).astype(f32).reshape(attn5.shape)]
    div x6 -> x0, other arithmetic: 7.83 us -> none  [the longest x1 4.18 us: query_features(): jax.nn.softmax(-logits, -1)]
  transfers between devices with their start and end apart: 10 -> 12, of which waited for: 0 -> 7; matrix products, arithmetic and copies ran while one was open for 30% -> 7% of each run, Pallas kernels for 40% -> 47%
where the time goes in v2:
time: 692 us; the launch traced here: 685 us
  Pallas kernels  520 us (75%)
  waiting for transfers between devices  45.6 us (7%)
  other arithmetic  40.9 us (6%)
  local copies, waits for them, and re-layouts  33.9 us (5%)
  matrix products  21.9 us (3%)
  between operations  15.6 us (2%)
  starting transfers between devices  7.56 us (1%)
    pallas_call x1, Pallas kernels, feed(): pl.pallas_call(functools.partial(feed_kernel, n, k, early), out_shape=[ja...  199 us
    pallas_call x1, Pallas kernels, gather_weights(): pl.pallas_call(functools.partial(gather_weights_kernel, n, k), out_shape=...  137 us
    pallas_call x1, Pallas kernels, attend_back(): pl.pallas_call(attend_back_kernel, grid=(2, 2), out_shape=[jax.ShapeDtype...  90.6 us
    ppermute x4, waiting for transfers between devices, swap_chip(): return lax.ppermute(value, 'dp', [(i, i ^ bit) for i in range(4)])  37.4 us
    pallas_call x1, Pallas kernels, plane_total(): pl.pallas_call(functools.partial(plane_total_kernel, n, shared), out_shap...  29.1 us
    pallas_call x1, Pallas kernels, attend(): pl.pallas_call(attend_kernel, grid=(2, 2), out_shape=jax.ShapeDtypeStruct...  28.4 us
    pallas_call x2, Pallas kernels, line_sum(): pl.pallas_call(functools.partial(line_sum_kernel, n, up), out_shape=jax.S...  23.3 us
    unnamed x156, local copies, waits for them, and re-layouts  16.5 us
  transfers between devices with their start and end apart: 12, of which 7 were waited for; matrix products, arithmetic and copies ran while one was open for 7% of the time, Pallas kernels for 47%

profile of v2, /device:TPU:0, one launch (start us, length us, event | category | flops | bytes accessed | tf_op | source)
XLA Modules:
  0.0 685.1 jit_solution(3160051007487979201)
XLA Ops:
  10.2 1.8 pad_maximum_fusion.2
  12.0 1.6 copy-done.16
  15.9 137.0 %gather_weights.1 = (bf16[4,512,1536]{2,1,0:T(8,128)(2,1)}, bf16[4,1024,512]{2,1,0:T(8,128)(2,1)}) custom-call(bf16[512,1536]{1,0:T(8,128)(2,1)} %pad_maximum_fusion.4.refs_0_, bf16[1024,512]{1,0:T(8,128)(2,1)} %refs_1_.1), custom_call_target="tpu_custom_call" | custom-call | tf_op jit(solution)/shard_map/gather_weights/pallas_call | solution.py:166
  154.9 2.3 copy-done.70
  157.2 3.4 fusion.79
  163.2 4.8 collective-permute-done
  168.1 4.9 key_state.1.own
  173.0 7.9 %line_sum_3.1.st.tot = f32[528,128]{1,0:T(8,128)S(1)} custom-call(bf16[528,128]{1,0:T(8,128)(2,1)S(1)} %key_state.1.own), custom_call_target="tpu_custom_call" | custom-call | tf_op jit(solution)/shard_map/line_sum_3/pallas_call | solution.py:372
  181.0 28.4 %attend.1 = bf16[512,1024]{1,0:T(8,128)(2,1)S(1)} custom-call(bf16[512,1024]{1,0:T(8,128)(2,1)S(1)} %fusion.q, bf16[2,320,512]{2,1,0:T(8,128)(2,1)S(1)} %maximum_maximum_fusion.kv.k.v, bf16[2,320,512]{2,1,0:T(8,128)(2,1)S(1)} %maximum_maximum_fusion.kv.k.v, f32[528,128]{1,0:T(8,128)S(1)} %line_sum_3.1.st.tot, f32[528,128]{1,0:T(8,128)S(1)} %line_sum_3.1.st.tot, ...), custom_call_target="tpu_custom_call" | custom-call | tf_op jit(solution)/shard_map/attend/pallas_call | solution.py:657
  213.4 2.0 copy-done.26
  216.1 4.1 convert.46
  220.1 2.3 constant_dynamic-slice_fusion.11.ct_own
  222.4 3.0 multiply_reduce_fusion.5
  228.0 199.1 %feed.1 = (f32[256,2048]{1,0:T(8,128)}, bf16[4,256,2048]{2,1,0:T(8,128)(2,1)}) custom-call(bf16[256,2048]{1,0:T(8,128)(2,1)} %multiply_convert_fusion.2.xn_own, bf16[256,2048]{1,0:T(8,128)(2,1)} %constant_dynamic-slice_fusion.11.ct_own, bf16[4,3,1536,256]{3,2,1,0:T(8,128)(2,1)} %bitcast.109, bf16[512,4096]{1,0:T(8,128)(2,1)} %gate.1, bf16[512,4096]{1,0:T(8,128)(2,1)} %up.1, ...), custom_call_target="tpu_custom_call" | custom-call | tf_op jit(solution)/shard_map/feed/pallas_call | solution.py:1151
  427.0 1.8 fusion.74
  431.0 23.7 %collective-permute-done.2 = bf16[2,128,2048]{2,1,0:T(8,128)(2,1)S(1)} collective-permute-done((bf16[2,128,2048]{2,1,0:T(8,128)(2,1)S(1)}, bf16[2,128,2048]{2,1,0:T(8,128)(2,1)S(1)}, u32[]{:S(2)}, u32[]{:S(2)}) %collective-permute-start.2) | collective-permute-done | bytes 1048608 | tf_op jit(solution)/shard_map/ppermute | solution.py:1304
  460.8 10.7 %collective-permute-done.3 = bf16[128,2048]{1,0:T(8,128)(2,1)S(1)} collective-permute-done((bf16[128,2048]{1,0:T(8,128)(2,1)S(1)}, bf16[128,2048]{1,0:T(8,128)(2,1)S(1)}, u32[]{:S(2)}, u32[]{:S(2)}) %collective-permute-start.3) | collective-permute-done | bytes 524320 | tf_op jit(solution)/shard_map/ppermute | solution.py:1304
  471.6 1.9 collective-permute-done.5
  473.6 3.8 fusion.73
  478.5 1.7 collective-permute-done.7
  486.9 90.6 %attend_back.1 = (bf16[512,1024]{1,0:T(8,128)(2,1)S(1)}, f32[2,320,256]{2,1,0:T(8,128)S(1)}, f32[2,320,256]{2,1,0:T(8,128)S(1)}, f32[2,4,320,128]{3,2,1,0:T(8,12...) custom-call(bf16[512,1024]{1,0:T(8,128)(2,1)S(1)} %copy-done.3, ...), custom_call_target="tpu_custom_call" | custom-call | tf_op jit(solution)/shard_map/attend_back/pallas_call | solution.py:758
  581.1 15.3 %line_sum_7.1.later.tot = f32[528,128]{1,0:T(8,128)S(1)} custom-call(bf16[528,128]{1,0:T(8,128)(2,1)S(1)} %fusion.53.own), custom_call_target="tpu_custom_call" | custom-call | tf_op jit(solution)/shard_map/line_sum_7/pallas_call | solution.py:372
  599.9 7.4 %key_back.1 = (f32[2,320,256]{2,1,0:T(8,128)S(1)}, f32[2,320,256]{2,1,0:T(8,128)S(1)}, f32[4,64,64]{2,1,0:T(8,128)S(1)}) custom-call(bf16[2,320,512]{2,1,0:T(8,128)(2,1)S(1)} %maximum_maximum_fusion.kv.k.v, bf16[2,320,512]{2,1,0:T(8,128)(2,1)S(1)} %maximum_maximum_fusion.kv.k.v, f32[528,128]{1,0:T(8,128)S(1)} %line_sum_7.1.later.tot, ...), custom_call_target="tpu_custom_call" | custom-call | tf_op jit(solution)/shard_map/key_back/pallas_call | solution.py:826
  609.5 3.0 broadcast_select_fusion.5
  612.9 1.6 collective-permute-done.8
  614.7 5.6 fusion.3
  625.9 3.3 pad_maximum_fusion.3
  630.6 2.8 multiply_reduce_fusion.2
  633.8 4.0 subtract_add_fusion
  638.0 29.1 %plane_total_8.1 = bf16[4,352,128]{2,1,0:T(8,128)(2,1)S(1)} custom-call(f32[1408,128]{1,0:T(8,128)S(1)} %pad.9.part), custom_call_target="tpu_custom_call" | custom-call | tf_op jit(solution)/shard_map/plane_total_8/pallas_call | solution.py:494
  673.3 1.9 broadcast_select_fusion.1
  675.3 2.5 pad_maximum_fusion
  (258 shorter events, 56.4 us)
Async XLA Ops:
  7.2 205.4 %copy-start = (bf16[8,2048]{1,0:T(8,128)(2,1)S(1)}, bf16[8,2048]{1,0:T(8,128)(2,1)}, u32[]{:S(2)}) copy-start(bf16[8,2048]{1,0:T(8,128)(2,1)} %param.39) | copy-start | bytes 98308
  7.2 220.8 %all-gather.3.cloned.1.call-start = ((), (), s32[]{:S(2)}) async-start(), calls=%async_computation | async-start | bytes 11796480 | tf_op jit(solution)/shard_map/all_gather | solution.py:1244
  14.6 139.6 %copy-start.38 = (f32[2048]{0:T(1024)}, f32[2048]{0:T(1024)S(1)}, u32[]{:S(2)}) copy-start(f32[2048]{0:T(1024)S(1)} %convert_element_type.149) | copy-start | bytes 24580
  15.9 137.0 %copy-start.55 = (bf16[2048,8]{0,1:T(8,128)(2,1)S(1)}, bf16[2048,8]{0,1:T(8,128)(2,1)}, u32[]{:S(2)}) copy-start(bf16[2048,8]{0,1:T(8,128)(2,1)} %param.32) | copy-start | bytes 98308
  15.9 137.0 %copy-start.56 = (bf16[2048,8]{0,1:T(8,128)(2,1)S(1)}, bf16[2048,8]{0,1:T(8,128)(2,1)}, u32[]{:S(2)}) copy-start(bf16[2048,8]{0,1:T(8,128)(2,1)} %param.34) | copy-start | bytes 98308
  15.9 137.1 %copy-start.57 = (bf16[2048,8]{0,1:T(8,128)(2,1)S(1)}, bf16[2048,8]{0,1:T(8,128)(2,1)}, u32[]{:S(2)}) copy-start(bf16[2048,8]{0,1:T(8,128)(2,1)} %param.36) | copy-start | bytes 98308
  161.2 6.8 copy-start.6
  161.2 19.7 %copy-start.8 = (bf16[16,64,64]{2,1,0:T(8,128)(2,1)S(1)}, bf16[16,64,64]{2,1,0:T(8,128)(2,1)}, u32[]{:S(2)}) copy-start(bf16[16,64,64]{2,1,0:T(8,128)(2,1)} %qmaps.3) | copy-start | bytes 393220
  161.3 6.8 collective-permute-start
  163.2 46.2 %copy-start.2 = (bf16[512,1024]{1,0:T(8,128)(2,1)}, bf16[512,1024]{1,0:T(8,128)(2,1)S(1)}, u32[]{:S(2)}) copy-start(bf16[512,1024]{1,0:T(8,128)(2,1)S(1)} %fusion.q) | copy-start | bytes 3145732
  180.9 28.4 %copy-start.44 = (bf16[1024,8]{0,1:T(8,128)(2,1)S(1)}, bf16[1024,8]{0,1:T(8,128)(2,1)}, u32[]{:S(2)}) copy-start(bf16[1024,8]{0,1:T(8,128)(2,1)} %param.38) | copy-start | bytes 49156
  180.9 28.8 %copy-start.28 = (bf16[4,1024,512]{2,1,0:T(8,128)(2,1)S(1)}, bf16[4,1024,512]{2,1,0:T(8,128)(2,1)}, u32[]{:S(2)}) copy-start(bf16[4,1024,512]{2,1,0:T(8,128)(2,1)} %get-tuple-element.29) | copy-start | bytes 12582916
  215.5 6.9 %collective-permute-start.1 = (bf16[256,2048]{1,0:T(8,128)(2,1)S(1)}, bf16[256,2048]{1,0:T(8,128)(2,1)}, u32[]{:S(2)}, u32[]{:S(2)}) collective-permute-start(bf16[256,2048]{1,0:T(8,128)(2,1)S(1)} %dynamic-slice_convert_fusion), channel_id=1, source_target_pairs={{0,4},{4,0},{1,5},{5,1},{2,6},{6,2},{3,7},{7,3},{8,12},{12,8},{9,1... | collective-permute-start | bytes 3145736 | tf_op jit(solution)/shard_map/ppermute | solution.py:1208
  216.1 10.0 %copy-start.40 = (f32[2048]{0:T(1024)}, f32[2048]{0:T(1024)S(1)}, u32[]{:S(2)}) copy-start(f32[2048]{0:T(1024)S(1)} %convert_element_type.159) | copy-start | bytes 24580
  427.0 31.5 %copy-start.27 = (f32[256,2048]{1,0:T(8,128)S(1)}, f32[256,2048]{1,0:T(8,128)}, u32[]{:S(2)}) copy-start(f32[256,2048]{1,0:T(8,128)} %get-tuple-element.31) | copy-start | bytes 6291460
  428.9 29.7 %copy-start.18 = (f32[256,2048]{1,0:T(8,128)S(1)}, f32[256,2048]{1,0:T(8,128)}, u32[]{:S(2)}) copy-start(f32[256,2048]{1,0:T(8,128)} %copy-done.17) | copy-start | bytes 6291460
  428.9 29.7 %copy-start.41 = (f32[2048]{0:T(1024)S(1)}, f32[2048]{0:T(1024)}, u32[]{:S(2)}) copy-start(f32[2048]{0:T(1024)} %copy-done.40) | copy-start | bytes 24580
  428.9 29.7 %copy-start.59 = (f32[256]{0:T(256)S(1)}, f32[256]{0:T(256)}, u32[]{:S(2)}) copy-start(f32[256]{0:T(256)} %copy-done.58) | copy-start | bytes 3076
  428.9 25.8 %collective-permute-start.2 = (bf16[2,128,2048]{2,1,0:T(8,128)(2,1)S(1)}, bf16[2,128,2048]{2,1,0:T(8,128)(2,1)S(1)}, u32[]{:S(2)}, u32[]{:S(2)}) collective-permute-start(bf16[2,128,2048]{2,1,0:T(8,128)(2,1)S(1)} %get-tuple-element.56), channel_id=1, source_target_pairs={{0,1},{1,0},{2,3},{3,2},{4,5},{5,4},{6,7},{7,6},{8,9},{9,8},{10,11... | collective-permute-start | bytes 3145736 | tf_op jit(solution)/shard_map/ppermute | solution.py:1304
  430.0 25.9 %collective-permute-start.4 = (bf16[2,128,2048]{2,1,0:T(8,128)(2,1)S(1)}, bf16[2,128,2048]{2,1,0:T(8,128)(2,1)S(1)}, u32[]{:S(2)}, u32[]{:S(2)}) collective-permute-start(bf16[2,128,2048]{2,1,0:T(8,128)(2,1)S(1)} %get-tuple-element.57), channel_id=1, source_target_pairs={{0,2},{1,3},{2,0},{3,1},{4,6},{5,7},{6,4},{7,5},{8,10},{9,11},{10,... | collective-permute-start | bytes 3145736 | tf_op jit(solution)/shard_map/ppermute | solution.py:1304
  457.4 14.0 %collective-permute-start.3 = (bf16[128,2048]{1,0:T(8,128)(2,1)S(1)}, bf16[128,2048]{1,0:T(8,128)(2,1)S(1)}, u32[]{:S(2)}, u32[]{:S(2)}) collective-permute-start(bf16[128,2048]{1,0:T(8,128)(2,1)S(1)} %get-tuple-element.54), channel_id=1, source_target_pairs={{0,2},{1,3},{2,0},{3,1},{4,6},{5,7},{6,4},{7,5},{8,10},{9,11},{10,... | collective-permute-start | bytes 1572872 | tf_op jit(solution)/shard_map/ppermute | solution.py:1304
  459.8 13.7 %collective-permute-start.5 = (bf16[128,2048]{1,0:T(8,128)(2,1)S(1)}, bf16[128,2048]{1,0:T(8,128)(2,1)S(1)}, u32[]{:S(2)}, u32[]{:S(2)}) collective-permute-start(bf16[128,2048]{1,0:T(8,128)(2,1)S(1)} %get-tuple-element.55), channel_id=1, source_target_pairs={{0,1},{1,0},{2,3},{3,2},{4,5},{5,4},{6,7},{7,6},{8,9},{9,8},{10,11... | collective-permute-start | bytes 1572872 | tf_op jit(solution)/shard_map/ppermute | solution.py:1304
  460.8 12.8 %copy-start.30 = (bf16[2,256,2048]{2,1,0:T(8,128)(2,1)S(1)}, bf16[2,256,2048]{2,1,0:T(8,128)(2,1)}, u32[]{:S(2)}) copy-start(bf16[2,256,2048]{2,1,0:T(8,128)(2,1)} %param.22) | copy-start | bytes 6291460
  460.8 12.8 %copy-start.67 = (f32[256]{0:T(256)S(1)}, f32[256]{0:T(256)}, u32[]{:S(2)}) copy-start(f32[256]{0:T(256)} %get-tuple-element.89) | copy-start | bytes 3076
  477.4 2.8 collective-permute-start.7
  478.0 131.5 %collective-permute-start.6 = (bf16[256,2048]{1,0:T(8,128)(2,1)}, bf16[256,2048]{1,0:T(8,128)(2,1)}, u32[]{:S(2)}, u32[]{:S(2)}) collective-permute-start(bf16[256,2048]{1,0:T(8,128)(2,1)} %get-tuple-element.72), channel_id=1, source_target_pairs={{0,4},{4,0},{1,5},{5,1},{2,6},{6,2},{3,7},{7,3},{8,12},{12,8},{9,1... | collective-permute-start | bytes 3145736 | tf_op jit(solution)/shard_map/ppermute | solution.py:1208
  607.7 6.9 %collective-permute-start.8 = (bf16[2,64,512]{2,1,0:T(8,128)(2,1)S(1)}, bf16[2,64,512]{2,1,0:T(8,128)(2,1)S(1)}, u32[]{:S(2)}, u32[]{:S(2)}) collective-permute-start(bf16[2,64,512]{2,1,0:T(8,128)(2,1)S(1)} %slice.257), channel_id=1, source_target_pairs={{8,0},{16,8},{24,16},{9,1},{17,9},{25,17},{10,2},{18,10},{26,18},{... | collective-permute-start | bytes 393224 | tf_op jit(solution)/shard_map/ppermute | solution.py:1204
  614.6 5.7 copy-start.63
  614.6 5.8 copy-start.65
  614.6 6.0 copy-start.34
  622.5 8.1 %collective-permute-start.9 = (bf16[256,2048]{1,0:T(8,128)(2,1)}, bf16[256,2048]{1,0:T(8,128)(2,1)}, u32[]{:S(2)}, u32[]{:S(2)}) collective-permute-start(bf16[256,2048]{1,0:T(8,128)(2,1)} %constant_dynamic-slice_fusion.6), channel_id=1, source_target_pairs={{0,4},{4,0},{1,5},{5,1},{2,6},{6,2},{3,7},{7,3},{8,12},{12,8},{9,1... | collective-permute-start | bytes 3145736 | tf_op jit(solution)/shard_map/ppermute | solution.py:1208
  637.7 35.6 %collective-permute-start.10 = (f32[256,2048]{1,0:T(8,128)}, f32[256,2048]{1,0:T(8,128)S(1)}, u32[]{:S(2)}, u32[]{:S(2)}) collective-permute-start(f32[256,2048]{1,0:T(8,128)} %subtract_add_fusion), channel_id=1, source_target_pairs={{0,4},{4,0},{1,5},{5,1},{2,6},{6,2},{3,7},{7,3},{8,12},{12,8},{9,1... | collective-permute-start | bytes 6291464 | tf_op jit(solution)/shard_map/ppermute | solution.py:1208
  (51 other events, 114.6 us)
Sparse Core Ops, SparseCore 0:
  12.1 203.2 all-gather.2

commit v3 on v2

--- a/solution.py
+++ b/solution.py
@@ -61,14 +61,27 @@
 
 
 def gather_weights_kernel(n, k, *refs):
-    ins, outs = refs[:k], refs[k : 2 * k]
-    own_sem, z_send, z_recv, p_send, p_recv = refs[2 * k :]
+    ins, block, outs, blocks = refs[:k], refs[k], refs[k + 1 : 2 * k + 1], refs[2 * k + 1]
+    own_sem, z_send, z_recv, p_send, p_recv, b_send, b_recv = refs[2 * k + 2 :]
     spot = Spot()
     s, d = spot.s, spot.d
     own = [pltpu.make_async_copy(ins[a], outs[a].at[s], own_sem.at[a]) for a in range(k)]
+    own.append(pltpu.make_async_copy(block, blocks.at[3], own_sem.at[k]))
     for c in own:
         c.start()
     greet(spot, n, ("x", "y", "up", "dn"))
+
+    cut = block.shape[0] // 2
+    parts = (pl.ds(0, cut), pl.ds(cut, cut))
+
+    def block_copy(kind, sending):
+        if kind < 2:
+            dst = blocks.at[kind + 1]
+            src = block if sending else dst
+        else:
+            dst = blocks.at[0, parts[kind - 2]]
+            src = blocks.at[(2, 1)[kind - 2], parts[kind - 2]] if sending else dst
+        return remote(src, dst, b_send.at[kind], b_recv.at[kind], spot.to("xyxy"[kind]))
 
     def rows(a, who, part=None):
         size = ins[a].shape[0] // 4
@@ -113,7 +126,15 @@
             def _():
                 z_copy(a, up, 0, True).start()
 
+    block_copy(0, True).start()
+    block_copy(1, True).start()
+
     for t in range(n):
+        if t == n - 1:
+            block_copy(1, False).wait_recv()
+            block_copy(2, True).start()
+            block_copy(0, False).wait_recv()
+            block_copy(3, True).start()
         if t < n - 1:
             for a in range(k):
                 for up in (True, False):
@@ -156,174 +177,27 @@
                     for kind in range(4):
                         plane_copy(a, up, t, kind).wait_send()
 
+    for kind in (2, 3):
+        block_copy(kind, False).wait_recv()
+    for kind in range(4):
+        block_copy(kind, True).wait_send()
     for c in own:
         c.wait()
 
 
-def gather_weights(n, arrays, cid):
+def gather_weights(n, arrays, block, cid):
     k = len(arrays)
     DMA = pltpu.SemaphoreType.DMA
     return pl.pallas_call(
         functools.partial(gather_weights_kernel, n, k),
-        out_shape=[jax.ShapeDtypeStruct((n,) + a.shape, a.dtype) for a in arrays],
-        in_specs=[pl.BlockSpec(memory_space=ANY)] * k,
-        out_specs=[pl.BlockSpec(memory_space=ANY)] * k,
-        scratch_shapes=[DMA((k,)), DMA((k, 2, n - 1)), DMA((k, 2, n - 1)), DMA((k, 2, n - 1, 4)), DMA((k, 2, n - 1, 4))],
+        out_shape=[jax.ShapeDtypeStruct((n,) + a.shape, a.dtype) for a in arrays]
+        + [jax.ShapeDtypeStruct((4,) + block.shape, block.dtype)],
+        in_specs=[pl.BlockSpec(memory_space=ANY)] * (k + 1),
+        out_specs=[pl.BlockSpec(memory_space=ANY)] * (k + 1),
+        scratch_shapes=[DMA((k + 1,)), DMA((k, 2, n - 1)), DMA((k, 2, n - 1)), DMA((k, 2, n - 1, 4)), DMA((k, 2, n - 1, 4)), DMA((4,)), DMA((4,))],
         compiler_params=pltpu.CompilerParams(collective_id=cid, has_side_effects=True),
         name="gather_weights",
-    )(*arrays)
-
-
-def plane_gather_kernel(own, out, own_sem, c_send, c_recv, p_send, p_recv):
-    spot = Spot()
-    m, d = spot.m, spot.d
-    half = own.shape[0] // 2
-    mine = pltpu.make_async_copy(own, out.at[d, m], own_sem)
-    mine.start()
-    greet(spot, 0, ("x", "y", "c"))
-    parts = (pl.ds(0, half), pl.ds(half, half))
-
-    def copy(kind, sending):
-        who = (d, d, spot.y, spot.x)[kind] if sending else (spot.x, spot.y, spot.diag, spot.diag)[kind]
-        if kind < 2:
-            dst = out.at[who, m]
-            src = own if sending else dst
-        else:
-            dst = out.at[who, m, parts[kind - 2]]
-            src = dst
-        return remote(src, dst, p_send.at[kind], p_recv.at[kind], spot.to("xyxy"[kind]))
-
-    def core(index, sending):
-        who = (d, spot.x, spot.y, spot.diag, spot.diag)[index]
-        col = m if sending else 1 - m
-        if index < 3:
-            dst = out.at[who, col]
-            src = own if (sending and index == 0) else dst
-        else:
-            dst = out.at[who, col, parts[index - 3]]
-            src = dst
-        return remote(src, dst, c_send.at[index], c_recv.at[index], spot.to("c"))
-
-    copy(0, True).start()
-    copy(1, True).start()
-    core(0, True).start()
-    copy(0, False).wait_recv()
-    copy(3, True).start()
-    core(1, True).start()
-    copy(1, False).wait_recv()
-    copy(2, True).start()
-    core(2, True).start()
-    copy(2, False).wait_recv()
-    core(3, True).start()
-    copy(3, False).wait_recv()
-    core(4, True).start()
-    for index in range(5):
-        core(index, False).wait_recv()
-        core(index, True).wait_send()
-    for kind in range(4):
-        copy(kind, True).wait_send()
-    mine.wait()
-
-
-def plane_gather(own, cid):
-    DMA = pltpu.SemaphoreType.DMA
-    return pl.pallas_call(
-        plane_gather_kernel,
-        out_shape=jax.ShapeDtypeStruct((4, 2) + own.shape, own.dtype),
-        in_specs=[pl.BlockSpec(memory_space=ANY)],
-        out_specs=pl.BlockSpec(memory_space=ANY),
-        scratch_shapes=[DMA, DMA((5,)), DMA((5,)), DMA((4,)), DMA((4,))],
-        compiler_params=pltpu.CompilerParams(collective_id=cid, has_side_effects=True),
-        name=f"plane_gather_{cid}",
-    )(own)
-
-
-def plane_scatter_kernel(
-    part, out, mine, theirs, s1, xin, yin, t2, xin2, yin2, l_sem, c_send, c_recv, p_send, p_recv
-):
-    spot = Spot()
-    m, d = spot.m, spot.d
-    half = out.shape[0] // 2
-    A, B = pl.ds(0, half), pl.ds(half, half)
-    order = (spot.diag, spot.x, spot.y, d)
-    loads = [pltpu.make_async_copy(part.at[who, m], mine.at[i], l_sem.at[i]) for i, who in enumerate(order)]
-    for c in loads:
-        c.start()
-    greet(spot, 0, ("x", "y", "c"))
-
-    def core(i):
-        return remote(part.at[order[i], 1 - m], theirs.at[i], c_send.at[i], c_recv.at[i], spot.to("c"))
-
-    for i in range(4):
-        core(i).start()
-
-    first = {
-        "xdiag": remote(s1.at[0, A], xin.at[1], p_send.at[0], p_recv.at[0], spot.to("x")),
-        "ydiag": remote(s1.at[0, B], yin.at[1], p_send.at[1], p_recv.at[1], spot.to("y")),
-        "x": remote(s1.at[1, A], xin.at[0], p_send.at[2], p_recv.at[2], spot.to("x")),
-        "y": remote(s1.at[2, B], yin.at[0], p_send.at[3], p_recv.at[3], spot.to("y")),
-    }
-    for i in range(4):
-        loads[i].wait()
-        core(i).wait_recv()
-        s1[i] = (mine[i].astype(jnp.float32) + theirs[i].astype(jnp.float32)).astype(s1.dtype)
-        if i == 0:
-            first["xdiag"].start()
-            first["ydiag"].start()
-        elif i == 1:
-            first["x"].start()
-        elif i == 2:
-            first["y"].start()
-    second = (
-        remote(t2.at[0], yin2, p_send.at[4], p_recv.at[4], spot.to("y")),
-        remote(t2.at[1], xin2, p_send.at[5], p_recv.at[5], spot.to("x")),
-    )
-    first["xdiag"].wait_recv()
-    t2[0] = (s1[2, A].astype(jnp.float32) + xin[1].astype(jnp.float32)).astype(t2.dtype)
-    second[0].start()
-    first["ydiag"].wait_recv()
-    t2[1] = (s1[1, B].astype(jnp.float32) + yin[1].astype(jnp.float32)).astype(t2.dtype)
-    second[1].start()
-    first["x"].wait_recv()
-    first["y"].wait_recv()
-    second[0].wait_recv()
-    out[A] = s1[3, A].astype(jnp.float32) + xin[0].astype(jnp.float32) + yin2[...].astype(jnp.float32)
-    second[1].wait_recv()
-    out[B] = s1[3, B].astype(jnp.float32) + yin[0].astype(jnp.float32) + xin2[...].astype(jnp.float32)
-    for i in range(4):
-        core(i).wait_send()
-    for c in list(first.values()) + list(second):
-        c.wait_send()
-
-
-def plane_scatter(part, cid):
-    DMA = pltpu.SemaphoreType.DMA
-    r, w = part.shape[2:]
-    b = jnp.bfloat16
-    V = pltpu.VMEM
-    return pl.pallas_call(
-        plane_scatter_kernel,
-        out_shape=jax.ShapeDtypeStruct((r, w), jnp.float32),
-        in_specs=[pl.BlockSpec(memory_space=ANY)],
-        out_specs=pl.BlockSpec(memory_space=pltpu.VMEM),
-        scratch_shapes=[
-            V((4, r, w), b),
-            V((4, r, w), b),
-            V((4, r, w), b),
-            V((2, r // 2, w), b),
-            V((2, r // 2, w), b),
-            V((2, r // 2, w), b),
-            V((r // 2, w), b),
-            V((r // 2, w), b),
-            DMA((4,)),
-            DMA((4,)),
-            DMA((4,)),
-            DMA((6,)),
-            DMA((6,)),
-        ],
-        compiler_params=pltpu.CompilerParams(collective_id=cid, has_side_effects=True, vmem_limit_bytes=40 << 20),
-        name=f"plane_scatter_{cid}",
-    )(part)
+    )(*arrays, block)
 
 
 def line_sum_kernel(n, up, own, out, box, send, recv):
@@ -606,10 +480,27 @@
     )(kv_ext, kmaps)
 
 
+STACK = 4
+
+
 def masks():
-    r = lax.broadcasted_iota(jnp.int32, (TILE, REACH), 0)
-    c = lax.broadcasted_iota(jnp.int32, (TILE, REACH), 1)
+    r = lax.broadcasted_iota(jnp.int32, (STACK * TILE, REACH), 0) % TILE
+    c = lax.broadcasted_iota(jnp.int32, (STACK * TILE, REACH), 1)
     return (c > r) & (c <= r + SPAN), c <= r
+
+
+def stacked(ref, rows, head):
+    return jnp.concatenate([ref[rows, (head + i) * 64 : (head + i) * 64 + 64] for i in range(STACK)], 0)
+
+
+def beside(value):
+    return jnp.concatenate([value[i * TILE : (i + 1) * TILE] for i in range(STACK)], 1)
+
+
+def query_logits(queries, qmaps, head):
+    return jnp.concatenate(
+        [mm(queries[i * TILE : (i + 1) * TILE], signed_map(qmaps[head + i])) for i in range(STACK)], 0
+    )
 
 
 def state_of(states, totals, e, gp, j):
@@ -622,7 +513,7 @@
     return jnp.concatenate([states[:, j * 64 : j * 64 + 64], jnp.where(c == 0, one, 0.0)], 1)
 
 
-def attend_kernel(q, k, v, st, tot, qmaps, kmaps, out):
+def attend_kernel(q, k, v, st, tot, qmaps, kmaps, out, qf, inv):
     gp, e = pl.program_id(0), pl.program_id(1)
     first = start_row()
     b16 = jnp.bfloat16
@@ -638,26 +529,33 @@
                 state = state + mm(kfeats[:TILE], values[:TILE], ((0,), (0,)))
             state16 = state.astype(b16)
             reach = slice(i * TILE, i * TILE + REACH)
-            for h in range(0, 4, 2):
-                pair = []
-                for hh in (h, h + 1):
-                    col = (j * 4 + hh) * 64
-                    query = q[i * TILE : (i + 1) * TILE, col : col + 64]
-                    qfeats = maps_of(mm(query, signed_map(qmaps[j * 4 + hh]))).astype(b16)
-                    near = mm(query, keys8[reach], ((1,), (1,)))
-                    far = mm(qfeats, kfeats[reach], ((1,), (1,)))
-                    weights = jnp.where(window, jnp.exp(jnp.where(window, near, 0.0)), jnp.where(older, far, 0.0))
-                    both = mm(weights.astype(b16), values[reach]) + mm(qfeats, state16)
-                    pair.append(both[:, :64] / both[:, 64:65])
-                col = (j * 4 + h) * 64
-                out[i * TILE : (i + 1) * TILE, col : col + 128] = jnp.concatenate(pair, 1).astype(b16)
+            rows = slice(i * TILE, (i + 1) * TILE)
+            for h in range(0, 4, STACK):
+                head = j * 4 + h
+                query = stacked(q, rows, head)
+                qfeats = maps_of(query_logits(query, qmaps, head)).astype(b16)
+                near = mm(query, keys8[reach], ((1,), (1,)))
+                far = mm(qfeats, kfeats[reach], ((1,), (1,)))
+                weights = jnp.where(window, jnp.exp(near), jnp.where(older, far, 0.0))
+                both = mm(weights.astype(b16), values[reach]) + mm(qfeats, state16)
+                part = 1.0 / both[:, 64:65]
+                out[rows, head * 64 : (head + STACK) * 64] = beside((both[:, :64] * part).astype(b16))
+                inv[0, rows, head : head + STACK] = beside(part)
+                qf[0, 0, head // STACK, i] = qfeats
+
+
+STACKED = pl.BlockSpec((1, 1, 8 // STACK, 2, STACK * TILE, 128), lambda g, e: (e, g, 0, 0, 0, 0))
 
 
 def attend(q, kv_ext, st, qmaps, kmaps):
     return pl.pallas_call(
         attend_kernel,
         grid=(2, 2),
-        out_shape=jax.ShapeDtypeStruct(q.shape, jnp.bfloat16),
+        out_shape=[
+            jax.ShapeDtypeStruct(q.shape, jnp.bfloat16),
+            jax.ShapeDtypeStruct((2, 2, 8 // STACK, 2, STACK * TILE, 128), jnp.bfloat16),
+            jax.ShapeDtypeStruct((2, 512, 8), jnp.float32),
+        ],
         in_specs=[
             pl.BlockSpec((256, 512), lambda g, e: (e, g)),
             pl.BlockSpec((1, 320, 128), lambda g, e: (e, 0, g)),
@@ -667,13 +565,61 @@
             pl.BlockSpec((8, 64, 64), lambda g, e: (g, 0, 0)),
             pl.BlockSpec((2, 64, 64), lambda g, e: (g, 0, 0)),
         ],
-        out_specs=pl.BlockSpec((256, 512), lambda g, e: (e, g)),
+        out_specs=[
+            pl.BlockSpec((256, 512), lambda g, e: (e, g)),
+            STACKED,
+            pl.BlockSpec((1, 256, 8), lambda g, e: (g, e, 0)),
+        ],
         compiler_params=pltpu.CompilerParams(vmem_limit_bytes=40 << 20),
         name="attend",
     )(q, kv_ext, kv_ext, st, st, qmaps, kmaps)
 
 
-def attend_back_kernel(q, k, v, st, tot, qmaps, kmaps, dattn, dq, dk, dv, dkf, dst, dtot, dqm):
+def state_back_kernel(attn, dattn, inv, qf, grad1, dst, dtot):
+    b16, f32 = jnp.bfloat16, jnp.float32
+    lane = lax.broadcasted_iota(jnp.int32, (STACK * TILE, 64), 1)
+    states = []
+    for j in range(2):
+        total = None
+        for h in range(0, 4, STACK):
+            head = j * 4 + h
+            for i in range(2):
+                rows = slice(i * TILE, (i + 1) * TILE)
+                part = jnp.concatenate([inv[0, rows, head + z : head + z + 1] for z in range(STACK)], 0)
+                grad = stacked(dattn, rows, head).astype(f32) * part
+                c = jnp.sum(grad * stacked(attn, rows, head).astype(f32), -1, keepdims=True)
+                one = jnp.concatenate([grad, jnp.where(lane == 0, -c, 0.0)], 1).astype(b16)
+                grad1[0, 0, head // STACK, i] = one
+                g = mm(qf[0, 0, head // STACK, i], one, ((0,), (0,)))
+                total = g if total is None else total + g
+        states.append(total[:, :64])
+        dtot[0, 0, j * 8 : j * 8 + 8] = mm(pick(64), total.astype(b16), ((1,), (1,))).astype(b16)
+    dst[...] = jnp.concatenate(states, 1).astype(b16)
+
+
+def state_back(attn, dattn, inv, qf):
+    b16 = jnp.bfloat16
+    rows = pl.BlockSpec((256, 512), lambda g, e: (e, g))
+    return pl.pallas_call(
+        state_back_kernel,
+        grid=(2, 2),
+        out_shape=[
+            jax.ShapeDtypeStruct(qf.shape, b16),
+            jax.ShapeDtypeStruct((512, 128), b16),
+            jax.ShapeDtypeStruct((2, 2, 16, 128), b16),
+        ],
+        in_specs=[rows, rows, pl.BlockSpec((1, 256, 8), lambda g, e: (g, e, 0)), STACKED],
+        out_specs=[
+            STACKED,
+            pl.BlockSpec((128, 128), lambda g, e: (e * 2 + g, 0)),
+            pl.BlockSpec((1, 1, 16, 128), lambda g, e: (e, g, 0, 0)),
+        ],
+        compiler_params=pltpu.CompilerParams(vmem_limit_bytes=40 << 20),
+        name="state_back",
+    )(attn, dattn, inv, qf)
+
+
+def attend_back_kernel(q, k, v, st, tot, qmaps, kmaps, qf, gr, dq, dk, dv, dkf, dqm):
     gp, e = pl.program_id(0), pl.program_id(1)
     first = start_row()
     b16, f32 = jnp.bfloat16, jnp.float32
@@ -687,14 +633,12 @@
     def _():
         dqm[...] = jnp.zeros_like(dqm)
 
-    dstates = []
     for j in range(2):
         keys = k[0, :, j * 64 : j * 64 + 64]
         values = with_ones(v[0, :, j * 64 : j * 64 + 64], first)
         kfeats = maps_of(mm(keys, signed_map(kmaps[j]))).astype(b16)
         keys8 = keys * eighth
         state = state_of(st, tot, e, gp, j)
-        gsum = None
         for i in range(2):
             if i:
                 state = state + mm(kfeats[:TILE], values[:TILE], ((0,), (0,)))
@@ -702,43 +646,38 @@
             reach = slice(i * TILE, i * TILE + REACH)
             rows = slice(i * TILE, (i + 1) * TILE)
             dvalue = dkey = dkfeat = g = None
-            for h in range(0, 4, 2):
-                dqs = []
-                for hh in (h, h + 1):
-                    head = j * 4 + hh
-                    query = q[rows, head * 64 : head * 64 + 64]
-                    grad = dattn[rows, head * 64 : head * 64 + 64].astype(f32)
-                    signed = signed_map(qmaps[head])
-                    qmap = maps_of(mm(query, signed))
-                    qfeats = qmap.astype(b16)
-                    near = mm(query, keys8[reach], ((1,), (1,)))
-                    far = mm(qfeats, kfeats[reach], ((1,), (1,)))
-                    close = jnp.where(window, jnp.exp(jnp.where(window, near, 0.0)), 0.0)
-                    weights = (close + jnp.where(older, far, 0.0)).astype(b16)
-                    both = mm(weights, values[reach]) + mm(qfeats, state16)
-                    inv = 1.0 / both[:, 64:65]
-                    grad = grad * inv
-                    c = jnp.sum(grad * both[:, :64], -1, keepdims=True) * inv
-                    lane = lax.broadcasted_iota(jnp.int32, (TILE, 64), 1)
-                    grad1 = jnp.concatenate([grad, jnp.where(lane == 0, -c, 0.0)], 1).astype(b16)
-                    dweights = mm(grad1, values[reach], ((1,), (1,)))
-                    ds = (close * dweights).astype(b16)
-                    dl = jnp.where(older, dweights, 0.0).astype(b16)
-                    dqmap = mm(dl, kfeats[reach]) + mm(grad1, state16, ((1,), (1,)))
-                    da = maps_back(qmap, dqmap).astype(b16)
-                    dqs.append(mm(ds, keys8[reach]) + mm(da, signed, ((1,), (1,))))
-                    x = mm(query, da, ((0,), (0,)))
-                    dqm[head] += x[:, :64] - x[:, 64:]
-                    a1 = mm(weights, grad1, ((0,), (0,)))
-                    a2 = mm(ds, query * eighth, ((0,), (0,)))
-                    a3 = mm(dl, qfeats, ((0,), (0,)))
-                    a4 = mm(qfeats, grad1, ((0,), (0,)))
-                    if dvalue is None:
-                        dvalue, dkey, dkfeat, g = a1, a2, a3, a4
-                    else:
-                        dvalue, dkey, dkfeat, g = dvalue + a1, dkey + a2, dkfeat + a3, g + a4
-                col = (j * 4 + h) * 64
-                dq[rows, col : col + 128] = jnp.concatenate(dqs, 1).astype(b16)
+            for h in range(0, 4, STACK):
+                head = j * 4 + h
+                query = stacked(q, rows, head)
+                grad1 = gr[0, 0, head // STACK, i]
+                qfeats = qf[0, 0, head // STACK, i]
+                qmap = qfeats.astype(f32)
+                near = mm(query, keys8[reach], ((1,), (1,)))
+                far = mm(qfeats, kfeats[reach], ((1,), (1,)))
+                close = jnp.where(window, jnp.exp(near), 0.0)
+                weights = (close + jnp.where(older, far, 0.0)).astype(b16)
+                dweights = mm(grad1, values[reach], ((1,), (1,)))
+                ds = (close * dweights).astype(b16)
+                dl = jnp.where(older, dweights, 0.0).astype(b16)
+                dqmap = mm(dl, kfeats[reach]) + mm(grad1, state16, ((1,), (1,)))
+                da = maps_back(qmap, dqmap).astype(b16)
+                dmaps = []
+                for z in range(STACK):
+                    part = slice(z * TILE, (z + 1) * TILE)
+                    dmaps.append(mm(da[part], signed_map(qmaps[head + z]), ((1,), (1,))))
+                    x = mm(query[part], da[part], ((0,), (0,)))
+                    dqm[head + z] += x[:, :64] - x[:, 64:]
+                dquery = mm(ds, keys8[reach]) + jnp.concatenate(dmaps, 0)
+                dq[rows, head * 64 : (head + STACK) * 64] = beside(dquery.astype(b16))
+                a1 = mm(weights, grad1, ((0,), (0,)))
+                a2 = mm(ds, query * eighth, ((0,), (0,)))
+                a3 = mm(dl, qfeats, ((0,), (0,)))
+                a4 = mm(qfeats, grad1, ((0,), (0,))) if i else None
+                if dvalue is None:
+                    dvalue, dkey, dkfeat, g = a1, a2, a3, a4
+                else:
+                    dvalue, dkey, dkfeat = dvalue + a1, dkey + a2, dkfeat + a3
+                    g = g + a4 if i else None
             dv[0, reach, j * 64 : j * 64 + 64] += dvalue[:, :64]
             dk[0, reach, j * 64 : j * 64 + 64] += dkey
             dkf[0, j, reach] += dkfeat
@@ -746,13 +685,9 @@
                 g16 = g.astype(b16)
                 dkf[0, j, :TILE] += mm(values[:TILE], g16, ((1,), (1,)))
                 dv[0, :TILE, j * 64 : j * 64 + 64] += mm(kfeats[:TILE], g16)[:, :64]
-            gsum = g if gsum is None else gsum + g
-        dstates.append(gsum[:, :64])
-        dtot[0, 0, j * 8 : j * 8 + 8] = mm(pick(64), gsum.astype(b16), ((1,), (1,))).astype(b16)
-    dst[...] = jnp.concatenate(dstates, 1).astype(b16)
-
-
-def attend_back(q, kv_ext, st, qmaps, kmaps, dattn):
+
+
+def attend_back(q, kv_ext, st, qmaps, kmaps, qf, grad1):
     f32, b16 = jnp.float32, jnp.bfloat16
     e2, ext = kv_ext.shape[:2]
     return pl.pallas_call(
@@ -763,8 +698,6 @@
             jax.ShapeDtypeStruct((e2, ext, 256), f32),
             jax.ShapeDtypeStruct((e2, ext, 256), f32),
             jax.ShapeDtypeStruct((e2, 4, ext, 128), f32),
-            jax.ShapeDtypeStruct((512, 128), b16),
-            jax.ShapeDtypeStruct((2, 2, 16, 128), b16),
             jax.ShapeDtypeStruct((16, 64, 64), f32),
         ],
         in_specs=[
@@ -775,20 +708,20 @@
             pl.BlockSpec((16, 128), lambda g, e: (32, 0)),
             pl.BlockSpec((8, 64, 64), lambda g, e: (g, 0, 0)),
             pl.BlockSpec((2, 64, 64), lambda g, e: (g, 0, 0)),
-            pl.BlockSpec((256, 512), lambda g, e: (e, g)),
+            STACKED,
+            STACKED,
         ],
         out_specs=[
             pl.BlockSpec((256, 512), lambda g, e: (e, g)),
             pl.BlockSpec((1, 320, 128), lambda g, e: (e, 0, g)),
             pl.BlockSpec((1, 320, 128), lambda g, e: (e, 0, g)),
             pl.BlockSpec((1, 2, 320, 128), lambda g, e: (e, g, 0, 0)),
-            pl.BlockSpec((128, 128), lambda g, e: (e * 2 + g, 0)),
-            pl.BlockSpec((1, 1, 16, 128), lambda g, e: (e, g, 0, 0)),
             pl.BlockSpec((8, 64, 64), lambda g, e: (g, 0, 0)),
         ],
         compiler_params=pltpu.CompilerParams(vmem_limit_bytes=40 << 20),
+        cost_estimate=pl.CostEstimate(flops=40 * 10**9, bytes_accessed=10**7, transcendentals=4 * 10**6),
         name="attend_back",
-    )(q, kv_ext, kv_ext, st, st, qmaps, kmaps, dattn)
+    )(q, kv_ext, kv_ext, st, st, qmaps, kmaps, qf, grad1)
 
 
 def key_back_kernel(k, v, later, tot, kmaps, dk_in, dv_in, dkf, dk, dv, dkm):
@@ -850,7 +783,7 @@
 CHUNKS = 4
 
 
-def feed_kernel(n, k, early, xn_own, ct_own, packed, gate, up, down, dxn, out_part, *scratch):
+def feed_kernel(n, k, early, xn_own, ct_all, packed, gate, up, down, dxn, out_part, *scratch):
     (xn, ct, gw, uw, dw, da, oa, xin, yin, t2, xin2, yin2) = scratch[:12]
     (o_sem, a_send, a_recv, w_sem, w_send, w_recv, z_sem, z_send, z_recv, c_send, c_recv, p_send, p_recv, st_sem) = scratch[12:]
     spot = Spot()
@@ -862,7 +795,7 @@
     half = xn.shape[1] // 2
     A, B = pl.ds(0, half), pl.ds(half, half)
 
-    own = [pltpu.make_async_copy(xn_own, xn.at[3], o_sem.at[0]), pltpu.make_async_copy(ct_own, ct.at[3], o_sem.at[1])]
+    own = [pltpu.make_async_copy(xn_own, xn.at[3], o_sem.at[0]), pltpu.make_async_copy(ct_all, ct, o_sem.at[1])]
     for c in own:
         c.start()
 
@@ -911,20 +844,18 @@
 
     greet(spot, n, ("x", "y", "c", "up", "dn"))
 
-    def block_copy(a, kind, sending):
-        ref, src_own = ((xn, xn_own), (ct, ct_own))[a]
+    def block_copy(kind, sending):
         if kind < 2:
-            dst = ref.at[kind + 1]
-            src = src_own if sending else dst
+            dst = xn.at[kind + 1]
+            src = xn_own if sending else dst
         else:
             rows = (A, B)[kind - 2]
-            dst = ref.at[0, rows]
-            src = ref.at[(2, 1)[kind - 2], rows] if sending else dst
-        return remote(src, dst, a_send.at[a, kind], a_recv.at[a, kind], spot.to("xyxy"[kind]))
-
-    for a in range(2):
-        block_copy(a, 0, True).start()
-        block_copy(a, 1, True).start()
+            dst = xn.at[0, rows]
+            src = xn.at[(2, 1)[kind - 2], rows] if sending else dst
+        return remote(src, dst, a_send.at[kind], a_recv.at[kind], spot.to("xyxy"[kind]))
+
+    block_copy(0, True).start()
+    block_copy(1, True).start()
 
     def sends(upward, t):
         return ((s - t >= 0) & (s + 1 < n)) if upward else ((s + t < n) & (s > 0))
@@ -966,20 +897,19 @@
         for c in early_core(q):
             c.start()
 
-    def relay(i, t):
-        for w in range(3):
-            for upward in (True, False):
-
-                @pl.when(receives(upward, t))
-                def _():
-                    z_copy(i, w, upward, t, False).wait_recv()
-                    if t + 1 < n - 1:
-
-                        @pl.when(sends(upward, t + 1))
-                        def _():
-                            z_copy(i, w, upward, t + 1, True).start()
-
-                    core_copy(i, w, s - 1 - t if upward else s + 1 + t, True).start()
+    def relay(i, t, w):
+        for upward in (True, False):
+
+            @pl.when(receives(upward, t))
+            def _():
+                z_copy(i, w, upward, t, False).wait_recv()
+                if t + 1 < n - 1:
+
+                    @pl.when(sends(upward, t + 1))
+                    def _():
+                        z_copy(i, w, upward, t + 1, True).start()
+
+                core_copy(i, w, s - 1 - t if upward else s + 1 + t, True).start()
 
     for i in range(len(late)):
         for w in range(3):
@@ -999,21 +929,21 @@
 
     steps = 4 * CHUNKS
     turns = {}
-    total = len(late) * (n - 1)
+    total = len(late) * (n - 1) * 3
     for j in range(total):
-        i, t = j // (n - 1), j % (n - 1)
-        at = min(4 * late[i], 2 + (4 * late[i] - 2) * (j + 1) // (i * (n - 1) + n - 1))
-        turns.setdefault(at, []).append((i, t))
+        i, t, w = j // (3 * n - 3), j // 3 % (n - 1), j % 3
+        at = min(4 * late[i], 1 + (4 * late[i] - 1) * j // ((i + 1) * (n - 1) * 3))
+        turns.setdefault(at, []).append((i, t, w))
 
     @pl.loop(0, steps)
     def _(step):
-        c = step // 4
         last = step >= steps - 4
-        t = jnp.where(last, step % 4, 3 - step % 4)
+        c = jnp.where(step < 4 * early, step % early, step // 4)
+        t = jnp.where(step < 4 * early, 3 - step // early, step % 4)
 
         for q in range(early):
 
-            @pl.when(step == 4 * q)
+            @pl.when(step == q)
             def _():
                 for copy in early_own[q]:
                     copy.wait()
@@ -1024,8 +954,8 @@
 
             @pl.when(step == at)
             def _():
-                for i, t in jobs:
-                    relay(i, t)
+                for i, t, w in jobs:
+                    relay(i, t, w)
 
         for i, q in enumerate(late):
 
@@ -1035,21 +965,19 @@
                     for who in range(n):
                         core_copy(i, w, who, False).wait_recv()
 
-        @pl.when(step == 1)
+        @pl.when(step == early)
         def _():
-            for a in range(2):
-                block_copy(a, 1, False).wait_recv()
-                block_copy(a, 2, True).start()
-                block_copy(a, 0, False).wait_recv()
-                block_copy(a, 3, True).start()
-
-        @pl.when(step == 3)
+            block_copy(1, False).wait_recv()
+            block_copy(2, True).start()
+            block_copy(0, False).wait_recv()
+            block_copy(3, True).start()
+
+        @pl.when(step == 3 * early)
         def _():
-            for a in range(2):
-                for kind in (2, 3):
-                    block_copy(a, kind, False).wait_recv()
-                for kind in range(4):
-                    block_copy(a, kind, True).wait_send()
+            for kind in (2, 3):
+                block_copy(kind, False).wait_recv()
+            for kind in range(4):
+                block_copy(kind, True).wait_send()
 
         x, cot = xn[t], ct[t]
         g_all = gw[c].reshape(n * k, 2 * unit)
@@ -1069,12 +997,12 @@
             o = mm(hid, dw[c, i])
             e = mm(dg, gw[c, i], ((1,), (1,))) + mm(du, uw[c, i], ((1,), (1,)))
 
-            @pl.when(step < 4)
+            @pl.when(c == 0)
             def _():
                 oa[t, :, cols] = o
                 da[t, :, cols] = e
 
-            @pl.when(step >= 4)
+            @pl.when(c > 0)
             def _():
                 oa[t, :, cols] += o
                 da[t, :, cols] += e
@@ -1131,7 +1059,7 @@
                         z_copy(i, w, upward, t, True).wait_send()
 
 
-def feed(n, early, xn_own, ct_own, packed, gate, up, down, cid):
+def feed(n, early, xn_own, ct_all, packed, gate, up, down, cid):
     DMA, V = pltpu.SemaphoreType.DMA, pltpu.VMEM
     b, f32 = jnp.bfloat16, jnp.float32
     r, w = xn_own.shape
@@ -1144,7 +1072,7 @@
     scratch += [V((CHUNKS, n, k, 2 * unit), b), V((CHUNKS, n, k, 2 * unit), b), V((CHUNKS, n, 2 * unit, k), b)]
     scratch += [V((4, r, w), f32), V((4, r, w), f32)]
     scratch += [V((2, r // 2, w), b), V((2, r // 2, w), b), V((2, r // 2, w), b), V((r // 2, w), b), V((r // 2, w), b)]
-    scratch += [DMA((2,)), DMA((2, 4)), DMA((2, 4))]
+    scratch += [DMA((2,)), DMA((4,)), DMA((4,))]
     scratch += [DMA((max(early, 1), pieces))] * 3
     scratch += [DMA((late, 3)), DMA((late, 3, 2, n - 1)), DMA((late, 3, 2, n - 1)), DMA((late, 3, n)), DMA((late, 3, n))]
     scratch += [DMA((6,)), DMA((6,)), DMA((4,))]
@@ -1156,7 +1084,7 @@
         scratch_shapes=scratch,
         compiler_params=pltpu.CompilerParams(collective_id=cid, has_side_effects=True, vmem_limit_bytes=62 << 20),
         name="feed",
-    )(xn_own, ct_own, packed, gate, up, down)
+    )(xn_own, ct_all, packed, gate, up, down)
 
 
 def pack_early(k, early, gate, up, down, d):
@@ -1244,14 +1172,15 @@
     packed = lax.all_gather(
         pack_early(gate_weight.shape[0], EARLY, gate_weight, up_weight, down_weight, d), "seq"
     )
+    def my_half(a):
+        return lax.dynamic_slice_in_dim(a, m * half, half, 0)
+
+    cot_half = my_half(cotangent.reshape(total_rows, width))
     qkv_own = jnp.concatenate([query_weight, key_weight, value_weight], 1)
-    qkv_g, out_g = gather_weights(n, [qkv_own, output_weight], 1)
+    qkv_g, out_g, cot_blocks = gather_weights(n, [qkv_own, output_weight], cot_half, 1)
     qkv_w = qkv_g.reshape(width, -1)
     wide = query_weight.shape[1]
     kv_wide = key_weight.shape[1]
-
-    def my_half(a):
-        return lax.dynamic_slice_in_dim(a, m * half, half, 0)
 
     def both_halves(own):
         other = swap_core(own)
@@ -1262,9 +1191,6 @@
     gain_attn = attention_norm_gain.astype(f32)
     rms_attn = lax.rsqrt(jnp.mean(inputs * inputs, -1, keepdims=True) + epsilon)
     normed = (inputs * rms_attn * gain_attn).astype(b16)
-
-    cot2 = cotangent.reshape(total_rows, width)
-    cot_half = my_half(cot2)
 
     downs = jnp.concatenate([query_adapter_down, key_adapter_down, value_adapter_down], 1)
     inner = dot(normed, downs)
@@ -1285,7 +1211,7 @@
     kv_prev = from_behind(kv3[:, rows_here - SOFTMAX_SPAN :], "seq", 1)
     kv_ext = jnp.concatenate([kv_prev, kv3], 1)
     states = line_sum(n, key_state(kv_ext, key_feature_matrix), True, 3)
-    attn16 = attend(query_half, kv_ext, states, query_feature_matrix, key_feature_matrix)
+    attn16, qfeats, inv_weights = attend(query_half, kv_ext, states, query_feature_matrix, key_feature_matrix)
     inner_output = dot(attn16, output_adapter_down)
     branch = jnp.concatenate([dot(attn16, out_g[i]) for i in range(n)], 1) + dot(
         inner_output.astype(b16), output_adapter_up
@@ -1297,7 +1223,7 @@
     rms_mlp = lax.rsqrt(jnp.mean(resid * resid, -1, keepdims=True) + epsilon)
     normed_mlp = (resid * rms_mlp * gain_mlp).astype(b16)
     dnormed_mlp, out_part = feed(
-        n, EARLY, normed_mlp, cot_half, packed, gate_weight, up_weight, down_weight, 4
+        n, EARLY, normed_mlp, cot_blocks, packed, gate_weight, up_weight, down_weight, 4
     )
 
     def swap_chip(value, bit):
@@ -1306,16 +1232,7 @@
     cut = half // 2
     upper_in = swap_chip(out_part[0:2, :cut], 1)
     lower_in = swap_chip(out_part[0::2, cut:], 2)
-    upper_in2 = swap_chip((out_part[2, :cut].astype(f32) + upper_in[0].astype(f32)).astype(b16), 2)
-    lower_in2 = swap_chip((out_part[1, cut:].astype(f32) + lower_in[0].astype(f32)).astype(b16), 1)
-    mlp_out = out_part[3].astype(f32) + jnp.concatenate(
-        [
-            upper_in[1].astype(f32) + upper_in2.astype(f32),
-            lower_in[1].astype(f32) + lower_in2.astype(f32),
-        ],
-        0,
-    )
-    output = both_halves((resid + mlp_out).astype(b16)).reshape(seq_count, rows_here, width)
+
 
     mlp_gain_term = jnp.sum(dnormed_mlp * resid * rms_mlp, 0)
     dresid = cot_half.astype(f32) + norm_back(resid, rms_mlp, gain_mlp, dnormed_mlp)
@@ -1327,12 +1244,30 @@
     step = output_weight.shape[1]
     for i in range(n):
         dattn = dattn + dot_t(dresid16[:, i * step : (i + 1) * step], out_g[i])
-    dq16, dk_ext, dv_ext, dkfeats, dstates, dtotals, dqmaps = attend_back(
-        query_half, kv_ext, states, query_feature_matrix, key_feature_matrix, dattn.astype(b16)
-    )
+    grad1, dstates, dtotals = state_back(attn16, dattn.astype(b16), inv_weights, qfeats)
     dtotals = jnp.pad(dtotals[:, :, ::8].reshape(-1, 128), ((0, 8), (0, 0)))
-    later = line_sum(n, jnp.concatenate([dstates, dtotals], 0), False, 7)
+    dstates = jnp.concatenate([dstates, dtotals], 0)
+    later = [from_behind(dstates, "seq", -i) for i in range(1, n)]
+    dresid_other = swap_core(dresid)
+    dq16, dk_ext, dv_ext, dkfeats, dqmaps = attend_back(
+        query_half, kv_ext, states, query_feature_matrix, key_feature_matrix, qfeats, grad1
+    )
+    dq16, later, upper_in, lower_in, dresid_other = lax.optimization_barrier(
+        (dq16, later, upper_in, lower_in, dresid_other)
+    )
+    upper_in2 = swap_chip((out_part[2, :cut].astype(f32) + upper_in[0].astype(f32)).astype(b16), 2)
+    lower_in2 = swap_chip((out_part[1, cut:].astype(f32) + lower_in[0].astype(f32)).astype(b16), 1)
+    later = functools.reduce(jnp.add, [a.astype(f32) for a in later])
     dk_ext, dv_ext, dkmaps = key_back(kv_ext, later, key_feature_matrix, dk_ext, dv_ext, dkfeats)
+    dk_ext, upper_in2, lower_in2 = lax.optimization_barrier((dk_ext, upper_in2, lower_in2))
+    mlp_out = out_part[3].astype(f32) + jnp.concatenate(
+        [
+            upper_in[1].astype(f32) + upper_in2.astype(f32),
+            lower_in[1].astype(f32) + lower_in2.astype(f32),
+        ],
+        0,
+    )
+    output = both_halves((resid + mlp_out).astype(b16)).reshape(seq_count, rows_here, width)
     dkv_ext = jnp.concatenate([dk_ext, dv_ext], -1)
     back = from_behind(dkv_ext[:, :SOFTMAX_SPAN].astype(b16), "seq", -1).astype(f32)
     dkv = dkv_ext[:, SOFTMAX_SPAN:]
@@ -1353,11 +1288,12 @@
     up_terms = [
         t_dot(inner16[:, i * rank : (i + 1) * rank], dqkv16[:, a:b]) for i, (a, b) in enumerate(bounds)
     ]
-    from_other = swap_core(lax.dynamic_slice_in_dim(dnormed, (1 - m) * half, half, 0))
-    dnormed = my_half(dnormed).astype(f32) + from_other.astype(f32)
-    x_half, r_half = my_half(inputs), my_half(rms_attn)
-    attn_gain_term = jnp.sum(dnormed * x_half * r_half, 0)
-    tokens_grad = both_halves(dresid + norm_back(x_half, r_half, gain_attn, dnormed)).reshape(
+    dnormed = dnormed.astype(f32) + swap_core(dnormed).astype(f32)
+    attn_gain_term = jnp.sum(my_half(dnormed * inputs * rms_attn), 0)
+    dresid_both = jnp.concatenate(
+        [jnp.where(m == 0, dresid, dresid_other), jnp.where(m == 0, dresid_other, dresid)], 0
+    )
+    tokens_grad = (dresid_both + norm_back(inputs, rms_attn, gain_attn, dnormed)).reshape(
         seq_count, rows_here, width
     )
 

time: 692 us -> 530 us (0.77)
  Pallas kernels: 520 us -> 371 us
  waiting for transfers between devices: 45.6 us -> 18.4 us
    pallas_call x1, Pallas kernels: 90.6 us -> 20 us  [attend_back(): pl.pallas_call(attend_back_kernel, grid=(2, 2), out_shape=[jax.ShapeDtype...]
    pallas_call x1, Pallas kernels: 199 us -> 134 us  [feed(): pl.pallas_call(functools.partial(feed_kernel, n, k, early), out_shape=[ja...]
    ppermute x4, waiting for transfers between devices: 37.4 us -> 0.01 us  [swap_chip(): return lax.ppermute(value, 'dp', [(i, i ^ bit) for i in range(4)])]
    pallas_call x2 -> x1, Pallas kernels: 23.3 us -> 5.11 us  [line_sum(): pl.pallas_call(functools.partial(line_sum_kernel, n, up), out_shape=jax.S...]
    pallas_call x1, Pallas kernels: 137 us -> 151 us  [gather_weights(): pl.pallas_call(functools.partial(gather_weights_kernel, n, k), out_shape=...]
    ppermute x2 -> x5, waiting for transfers between devices: 6.44 us -> 17.8 us  [from_behind(): lax.ppermute(value, axis, [(source, source + steps) for source in range(f...]
    pallas_call x1 -> x2, Pallas kernels: 28.4 us -> 21.3 us  [the longest x1 13.4 us: attend(): pl.pallas_call(attend_kernel, grid=(2, 2), out_shape=[jax.ShapeDtypeStruc...]
    unnamed x156 -> x179, local copies, waits for them, and re-layouts: 16.5 us -> 12.4 us
  transfers between devices with their start and end apart: 12 -> 15, of which waited for: 7 -> 3; matrix products, arithmetic and copies ran while one was open for 7% -> 12% of each run, Pallas kernels for 47% -> 40%
where the time goes in v3:
time: 530 us; the launch traced here: 523 us
  Pallas kernels  371 us (70%)
  other arithmetic  47.7 us (9%)
  local copies, waits for them, and re-layouts  31.9 us (6%)
  matrix products  25.5 us (5%)
  waiting for transfers between devices  18.4 us (3%)
  between operations  15.7 us (3%)
  starting transfers between devices  12.4 us (2%)
    pallas_call x1, Pallas kernels, gather_weights(): pl.pallas_call(functools.partial(gather_weights_kernel, n, k), out_shape=...  151 us
    pallas_call x1, Pallas kernels, feed(): pl.pallas_call(functools.partial(feed_kernel, n, k, early), out_shape=[ja...  134 us
    pallas_call x1, Pallas kernels, plane_total(): pl.pallas_call(functools.partial(plane_total_kernel, n, shared), out_shap...  27.6 us
    pallas_call x1, Pallas kernels, attend_back(): pl.pallas_call(attend_back_kernel, grid=(2, 2), out_shape=[jax.ShapeDtype...  20 us
    ppermute x5, waiting for transfers between devices, from_behind(): lax.ppermute(value, axis, [(source, source + steps) for source in range(f...  17.8 us
    pallas_call x1, Pallas kernels, attend(): pl.pallas_call(attend_kernel, grid=(2, 2), out_shape=[jax.ShapeDtypeStruc...  13.4 us
    unnamed x179, local copies, waits for them, and re-layouts  12.4 us
    dot_general x11, matrix products, dot(): return jnp.dot(left, right, preferred_element_type=f32)  11.2 us
  transfers between devices with their start and end apart: 15, of which 3 were waited for; matrix products, arithmetic and copies ran while one was open for 12% of the time, Pallas kernels for 40%

profile of v3, /device:TPU:0, one launch (start us, length us, event | category | flops | bytes accessed | tf_op | source)
XLA Modules:
  0.0 522.5 jit_solution(4195680970073943540)
XLA Ops:
  10.2 1.7 pad_maximum_fusion.1
  12.6 2.2 multiply_reduce_fusion.1
  14.8 2.3 constant_dynamic-slice_fusion.8.refs_2_
  18.4 150.7 %gather_weights.1 = (bf16[4,512,1536]{2,1,0:T(8,128)(2,1)}, bf16[4,1024,512]{2,1,0:T(8,128)(2,1)}, bf16[4,256,2048]{2,1,0:T(8,128)(2,1)}) custom-call(bf16[512,1536]{1,0:T(8,128)(2,1)} %pad_maximum_fusion.3.refs_0_, bf16[1024,512]{1,0:T(8,128)(2,1)} %refs_1_.1, bf16[256,2048]{1,0:T(8,128)(2,1)} %constant_dynamic-slice_fusion.8.refs_2_), custom_call_target="tpu_custom_call" | custom-call | tf_op jit(solution)/shard_map/gather_weights/pallas_call | solution.py:191
  169.2 2.2 multiply_convert_fusion
  172.1 1.7 copy-done.24
  174.3 5.6 %fusion.80 = f32[512,1536]{1,0:T(8,128)S(1)} fusion(bf16[512,2048]{1,0:T(8,128)(2,1)S(1)} %bitcast.114, bf16[2048,1536]{1,0:T(8,128)(2,1)} %bitcast.122), kind=kOutput, calls=%fused_computation.168 | convolution fusion | flops 3221225472 | bytes 11534336 | tf_op jit(solution)/shard_map/dot_general | solution.py:1112
  182.5 6.1 %collective-permute-done = bf16[2,64,512]{2,1,0:T(8,128)(2,1)S(1)} collective-permute-done((bf16[2,64,512]{2,1,0:T(8,128)(2,1)S(1)}, bf16[2,64,512]{2,1,0:T(8,128)(2,1)S(1)}, u32[]{:S(2)}, u32[]{:S(2)}) %collective-permute-start) | collective-permute-done | bytes 131104 | tf_op jit(solution)/shard_map/ppermute | solution.py:1132
  188.7 4.9 key_state.1.own
  193.6 5.1 line_sum_3.1.st.tot
  198.7 13.4 %attend.1 = (bf16[512,1024]{1,0:T(8,128)(2,1)S(1)}, bf16[2,2,2,2,512,128]{5,4,3,2,1,0:T(8,128)(2,1)S(1)}, f32[2,512,8]{2,1,0:T(8,128)S(1)}) custom-call(bf16[512,1024]{1,0:T(8,128)(2,1)S(1)} %fusion.2.q, bf16[2,320,512]{2,1,0:T(8,128)(2,1)S(1)} %maximum_maximum_fusion.kv.k.v, bf16[2,320,512]{2,1,0:T(8,128)(2,1)S(1)} %maximum_maximum_fusion.kv.k.v, ...), custom_call_target="tpu_custom_call" | custom-call | tf_op jit(solution)/shard_map/attend/pallas_call | solution.py:551
  219.4 2.1 multiply_reduce_fusion.4
  222.7 2.9 multiply_convert_fusion.2.xn_own
  225.5 134.3 %feed.1 = (f32[256,2048]{1,0:T(8,128)}, bf16[4,256,2048]{2,1,0:T(8,128)(2,1)}) custom-call(bf16[256,2048]{1,0:T(8,128)(2,1)} %multiply_convert_fusion.2.xn_own, bf16[4,256,2048]{2,1,0:T(8,128)(2,1)} %get-tuple-element.46.ct_all, bf16[4,3,1536,256]{3,2,1,0:T(8,128)(2,1)} %bitcast.100, bf16[512,4096]{1,0:T(8,128)(2,1)} %gate.1, bf16[512,4096]{1,0:T(8,128)(2,1)} %up.1, ...), custom_call_target="tpu_custom_call" | custom-call | tf_op jit(solution)/shard_map/feed/pallas_call | solution.py:1079
  359.9 3.5 multiply_reduce_fusion.2
  363.5 3.6 fusion.74
  368.8 3.1 fusion.75
  380.4 7.9 %state_back.1 = (bf16[2,2,2,2,512,128]{5,4,3,2,1,0:T(8,128)(2,1)S(1)}, bf16[512,128]{1,0:T(8,128)(2,1)S(1)}, bf16[2,2,16,128]{3,2,1,0:T(8,128)(2,1)S(1)}) custom-call(bf16[512,1024]{1,0:T(8,128)(2,1)S(1)} %get-tuple-element.44.attn, bf16[512,1024]{1,0:T(8,128)(2,1)S(1)} %add_convert_fusion.1.dattn, f32[2,512,8]{2,1,0:T(8,128)S(1)} %copy-done.18, ...), custom_call_target="tpu_custom_call" | custom-call | tf_op jit(solution)/shard_map/state_back/pallas_call | solution.py:603
  391.0 1.8 collective-permute-start.4
  396.0 20.0 %attend_back.1 = (bf16[512,1024]{1,0:T(8,128)(2,1)S(1)}, f32[2,320,256]{2,1,0:T(8,128)S(1)}, f32[2,320,256]{2,1,0:T(8,128)S(1)}, f32[2,4,320,128]{3,2,1,0:T(8,128)S(1)}, f32[16,64,64]{2,1,0:T(8,128)S(1)}) custom-call(bf16[512,1024]{1,0:T(8,128)(2,1)S(1)} %copy-done.3, bf16[2,320,512]{2,1,0:T(8,128)(2,1)S(1)} %maximum_maximum_fusion.kv.k.v, ...), custom_call_target="tpu_custom_call" | custom-call | flops 40000000000 | bytes 10000000 | tf_op jit(solution)/shard_map/attend_back/pallas_call | solution.py:693
  417.9 11.7 %collective-permute-done.5 = bf16[528,128]{1,0:T(8,128)(2,1)S(1)} collective-permute-done((bf16[528,128]{1,0:T(8,128)(2,1)S(1)}, bf16[528,128]{1,0:T(8,128)(2,1)S(1)}, u32[]{:S(2)}, u32[]{:S(2)}) %collective-permute-start.5) | collective-permute-done | bytes 135200 | tf_op jit(solution)/shard_map/ppermute | solution.py:1132
  429.6 3.0 fusion.38
  437.9 1.9 reshape.206
  440.9 7.2 %key_back.1 = (f32[2,320,256]{2,1,0:T(8,128)S(1)}, f32[2,320,256]{2,1,0:T(8,128)S(1)}, f32[4,64,64]{2,1,0:T(8,128)S(1)}) custom-call(bf16[2,320,512]{2,1,0:T(8,128)(2,1)S(1)} %maximum_maximum_fusion.kv.k.v, bf16[2,320,512]{2,1,0:T(8,128)(2,1)S(1)} %maximum_maximum_fusion.kv.k.v, f32[528,128]{1,0:T(8,128)S(1)} %convert_add_fusion.4.later.tot, ...), custom_call_target="tpu_custom_call" | custom-call | tf_op jit(solution)/shard_map/key_back/pallas_call | solution.py:759
  453.2 2.5 fusion.4
  456.8 3.4 fusion.5
  460.3 2.1 add_convert_fusion
  462.4 4.1 broadcast_select_fusion.1
  466.8 2.0 fusion.56
  471.7 3.6 multiply_reduce_fusion
  475.4 5.1 convert_add_fusion
  481.6 27.6 %plane_total_8.1 = bf16[4,352,128]{2,1,0:T(8,128)(2,1)S(1)} custom-call(f32[1408,128]{1,0:T(8,128)S(1)} %pad.9.part), custom_call_target="tpu_custom_call" | custom-call | tf_op jit(solution)/shard_map/plane_total_8/pallas_call | solution.py:368
  (290 shorter events, 57.8 us)
Async XLA Ops:
  7.2 208.6 %copy-start = (bf16[8,2048]{1,0:T(8,128)(2,1)S(1)}, bf16[8,2048]{1,0:T(8,128)(2,1)}, u32[]{:S(2)}) copy-start(bf16[8,2048]{1,0:T(8,128)(2,1)} %param.39) | copy-start | bytes 98308
  7.2 218.3 %all-gather.3.cloned.1.call-start = ((), (), s32[]{:S(2)}) async-start(), calls=%async_computation | async-start | bytes 11796480 | tf_op jit(solution)/shard_map/all_gather | solution.py:1172
  12.5 159.5 %copy-start.48 = (f32[2048]{0:T(1024)}, f32[2048]{0:T(1024)S(1)}, u32[]{:S(2)}) copy-start(f32[2048]{0:T(1024)S(1)} %convert_element_type.158) | copy-start | bytes 24580
  14.8 154.4 %copy-start.59 = (f32[1,2,2,128]{3,1,2,0:T(2,128)}, f32[1,2,2,128]{3,1,2,0:T(2,128)S(1)}, u32[]{:S(2)}) copy-start(f32[1,2,2,128]{3,1,2,0:T(2,128)S(1)} %copy.47) | copy-start | bytes 6148
  18.4 150.7 %copy-start.67 = (bf16[2048,8]{0,1:T(8,128)(2,1)S(1)}, bf16[2048,8]{0,1:T(8,128)(2,1)}, u32[]{:S(2)}) copy-start(bf16[2048,8]{0,1:T(8,128)(2,1)} %param.32) | copy-start | bytes 98308
  18.4 150.7 %copy-start.68 = (bf16[2048,8]{0,1:T(8,128)(2,1)S(1)}, bf16[2048,8]{0,1:T(8,128)(2,1)}, u32[]{:S(2)}) copy-start(bf16[2048,8]{0,1:T(8,128)(2,1)} %param.34) | copy-start | bytes 98308
  18.4 150.7 %copy-start.69 = (bf16[2048,8]{0,1:T(8,128)(2,1)S(1)}, bf16[2048,8]{0,1:T(8,128)(2,1)}, u32[]{:S(2)}) copy-start(bf16[2048,8]{0,1:T(8,128)(2,1)} %param.36) | copy-start | bytes 98308
  180.5 18.2 %copy-start.20 = (bf16[16,64,64]{2,1,0:T(8,128)(2,1)S(1)}, bf16[16,64,64]{2,1,0:T(8,128)(2,1)}, u32[]{:S(2)}) copy-start(bf16[16,64,64]{2,1,0:T(8,128)(2,1)} %qmaps.3) | copy-start | bytes 393220
  180.5 8.1 %collective-permute-start = (bf16[2,64,512]{2,1,0:T(8,128)(2,1)S(1)}, bf16[2,64,512]{2,1,0:T(8,128)(2,1)S(1)}, u32[]{:S(2)}, u32[]{:S(2)}) collective-permute-start(bf16[2,64,512]{2,1,0:T(8,128)(2,1)S(1)} %pad_maximum_fusion.9), channel_id=1, source_target_pairs={{0,8},{8,16},{16,24},{1,9},{9,17},{17,25},{2,10},{10,18},{18,26},{... | collective-permute-start | bytes 393224 | tf_op jit(solution)/shard_map/ppermute | solution.py:1132
  182.5 29.7 %copy-start.2 = (bf16[512,1024]{1,0:T(8,128)(2,1)}, bf16[512,1024]{1,0:T(8,128)(2,1)S(1)}, u32[]{:S(2)}) copy-start(bf16[512,1024]{1,0:T(8,128)(2,1)S(1)} %fusion.2.q) | copy-start | bytes 3145732
  188.7 23.5 %copy-start.55 = (bf16[1024,8]{0,1:T(8,128)(2,1)S(1)}, bf16[1024,8]{0,1:T(8,128)(2,1)}, u32[]{:S(2)}) copy-start(bf16[1024,8]{0,1:T(8,128)(2,1)} %param.38) | copy-start | bytes 49156
  216.7 2.7 collective-permute-start.1
  367.0 6.8 %collective-permute-start.2 = (bf16[256,2048]{1,0:T(8,128)(2,1)S(1)}, bf16[256,2048]{1,0:T(8,128)(2,1)}, u32[]{:S(2)}, u32[]{:S(2)}) collective-permute-start(bf16[256,2048]{1,0:T(8,128)(2,1)S(1)} %get-tuple-element.74), channel_id=1, source_target_pairs={{0,4},{4,0},{1,5},{5,1},{2,6},{6,2},{3,7},{7,3},{8,12},{12,8},{9,1... | collective-permute-start | bytes 3145736 | tf_op jit(solution)/shard_map/ppermute | solution.py:1136
  368.3 61.3 %collective-permute-start.8 = (f32[256,2048]{1,0:T(8,128)}, f32[256,2048]{1,0:T(8,128)}, u32[]{:S(2)}, u32[]{:S(2)}) collective-permute-start(f32[256,2048]{1,0:T(8,128)} %get-tuple-element.75), channel_id=1, source_target_pairs={{0,4},{4,0},{1,5},{5,1},{2,6},{6,2},{3,7},{7,3},{8,12},{12,8},{9,1... | collective-permute-start | bytes 6291464 | tf_op jit(solution)/shard_map/ppermute | solution.py:1136
  371.9 44.2 %collective-permute-start.6 = (bf16[2,128,2048]{2,1,0:T(8,128)(2,1)}, bf16[2,128,2048]{2,1,0:T(8,128)(2,1)}, u32[]{:S(2)}, u32[]{:S(2)}) collective-permute-start(bf16[2,128,2048]{2,1,0:T(8,128)(2,1)} %get-tuple-element.85), channel_id=1, source_target_pairs={{0,1},{1,0},{2,3},{3,2},{4,5},{5,4},{6,7},{7,6},{8,9},{9,8},{10,11... | collective-permute-start | bytes 3145736 | tf_op jit(solution)/shard_map/ppermute | solution.py:1230
  372.3 45.6 %collective-permute-start.7 = (bf16[2,128,2048]{2,1,0:T(8,128)(2,1)}, bf16[2,128,2048]{2,1,0:T(8,128)(2,1)}, u32[]{:S(2)}, u32[]{:S(2)}) collective-permute-start(bf16[2,128,2048]{2,1,0:T(8,128)(2,1)} %get-tuple-element.84), channel_id=1, source_target_pairs={{0,2},{1,3},{2,0},{3,1},{4,6},{5,7},{6,4},{7,5},{8,10},{9,11},{10,... | collective-permute-start | bytes 3145736 | tf_op jit(solution)/shard_map/ppermute | solution.py:1230
  389.7 28.2 %collective-permute-start.3 = (bf16[528,128]{1,0:T(8,128)(2,1)S(1)}, bf16[528,128]{1,0:T(8,128)(2,1)S(1)}, u32[]{:S(2)}, u32[]{:S(2)}) collective-permute-start(bf16[528,128]{1,0:T(8,128)(2,1)S(1)} %fusion.55), channel_id=1, source_target_pairs={{8,0},{16,8},{24,16},{9,1},{17,9},{25,17},{10,2},{18,10},{26,18},{... | collective-permute-start | bytes 405512 | tf_op jit(solution)/shard_map/ppermute | solution.py:1132
  391.0 26.9 %collective-permute-start.4 = (bf16[528,128]{1,0:T(8,128)(2,1)S(1)}, bf16[528,128]{1,0:T(8,128)(2,1)S(1)}, u32[]{:S(2)}, u32[]{:S(2)}) collective-permute-start(bf16[528,128]{1,0:T(8,128)(2,1)S(1)} %fusion.55), channel_id=1, source_target_pairs={{16,0},{24,8},{17,1},{25,9},{18,2},{26,10},{19,3},{27,11},{20,4},{... | collective-permute-start | bytes 405512 | tf_op jit(solution)/shard_map/ppermute | solution.py:1132
  396.0 21.6 %copy-start.65 = (bf16[512,8]{0,1:T(8,128)(2,1)S(1)}, bf16[512,8]{0,1:T(8,128)(2,1)}, u32[]{:S(2)}) copy-start(bf16[512,8]{0,1:T(8,128)(2,1)} %copy-done.64) | copy-start | bytes 24580
  416.0 16.6 %copy-start.4 = (bf16[512,1024]{1,0:T(8,128)(2,1)}, bf16[512,1024]{1,0:T(8,128)(2,1)S(1)}, u32[]{:S(2)}) copy-start(bf16[512,1024]{1,0:T(8,128)(2,1)S(1)} %get-tuple-element.67) | copy-start | bytes 3145732
  416.0 16.6 %copy-start.9 = (f32[2,4,320,128]{3,2,1,0:T(8,128)}, f32[2,4,320,128]{3,2,1,0:T(8,128)S(1)}, u32[]{:S(2)}) copy-start(f32[2,4,320,128]{3,2,1,0:T(8,128)S(1)} %get-tuple-element.61.dkf) | copy-start | bytes 3932164
  416.0 17.4 %copy-start.19 = (f32[16,64,64]{2,1,0:T(8,128)}, f32[16,64,64]{2,1,0:T(8,128)S(1)}, u32[]{:S(2)}) copy-start(f32[16,64,64]{2,1,0:T(8,128)S(1)} %get-tuple-element.70) | copy-start | bytes 786436
  416.0 18.8 %copy-start.28 = (bf16[256,2048]{1,0:T(8,128)(2,1)S(1)}, bf16[256,2048]{1,0:T(8,128)(2,1)}, u32[]{:S(2)}) copy-start(bf16[256,2048]{1,0:T(8,128)(2,1)} %copy-done.27) | copy-start | bytes 3145732
  416.0 18.8 %copy-start.30 = (bf16[256,2048]{1,0:T(8,128)(2,1)S(1)}, bf16[256,2048]{1,0:T(8,128)(2,1)}, u32[]{:S(2)}) copy-start(bf16[256,2048]{1,0:T(8,128)(2,1)} %copy-done.29) | copy-start | bytes 3145732
  416.0 18.7 %copy-start.63 = (bf16[512,8]{0,1:T(8,128)(2,1)S(1)}, bf16[512,8]{0,1:T(8,128)(2,1)}, u32[]{:S(2)}) copy-start(bf16[512,8]{0,1:T(8,128)(2,1)} %copy-done.62) | copy-start | bytes 24580
  416.1 13.5 %collective-permute-start.5 = (bf16[528,128]{1,0:T(8,128)(2,1)S(1)}, bf16[528,128]{1,0:T(8,128)(2,1)S(1)}, u32[]{:S(2)}, u32[]{:S(2)}) collective-permute-start(bf16[528,128]{1,0:T(8,128)(2,1)S(1)} %fusion.55), channel_id=1, source_target_pairs={{24,0},{25,1},{26,2},{27,3},{28,4},{29,5},{30,6},{31,7}} | collective-permute-start | bytes 405512 | tf_op jit(solution)/shard_map/ppermute | solution.py:1132
  432.6 15.9 %collective-permute-start.10 = (bf16[128,2048]{1,0:T(8,128)(2,1)}, bf16[128,2048]{1,0:T(8,128)(2,1)}, u32[]{:S(2)}, u32[]{:S(2)}) collective-permute-start(bf16[128,2048]{1,0:T(8,128)(2,1)} %get-tuple-element.82), channel_id=1, source_target_pairs={{0,1},{1,0},{2,3},{3,2},{4,5},{5,4},{6,7},{7,6},{8,9},{9,8},{10,11... | collective-permute-start | bytes 1572872 | tf_op jit(solution)/shard_map/ppermute | solution.py:1230
  433.4 15.1 %collective-permute-start.9 = (bf16[128,2048]{1,0:T(8,128)(2,1)}, bf16[128,2048]{1,0:T(8,128)(2,1)}, u32[]{:S(2)}, u32[]{:S(2)}) collective-permute-start(bf16[128,2048]{1,0:T(8,128)(2,1)} %get-tuple-element.83), channel_id=1, source_target_pairs={{0,2},{1,3},{2,0},{3,1},{4,6},{5,7},{6,4},{7,5},{8,10},{9,11},{10,... | collective-permute-start | bytes 1572872 | tf_op jit(solution)/shard_map/ppermute | solution.py:1230
  448.8 7.0 %collective-permute-start.12 = (bf16[2,64,512]{2,1,0:T(8,128)(2,1)S(1)}, bf16[2,64,512]{2,1,0:T(8,128)(2,1)S(1)}, u32[]{:S(2)}, u32[]{:S(2)}) collective-permute-start(bf16[2,64,512]{2,1,0:T(8,128)(2,1)S(1)} %slice.253), channel_id=1, source_target_pairs={{8,0},{16,8},{24,16},{9,1},{17,9},{25,17},{10,2},{18,10},{26,18},{... | collective-permute-start | bytes 393224 | tf_op jit(solution)/shard_map/ppermute | solution.py:1132
  455.8 13.4 %collective-permute-start.11 = (bf16[256,2048]{1,0:T(8,128)(2,1)S(1)}, bf16[256,2048]{1,0:T(8,128)(2,1)S(1)}, u32[]{:S(2)}, u32[]{:S(2)}) collective-permute-start(bf16[256,2048]{1,0:T(8,128)(2,1)S(1)} %fusion.4), channel_id=1, source_target_pairs={{0,4},{4,0},{1,5},{5,1},{2,6},{6,2},{3,7},{7,3},{8,12},{12,8},{9,1... | collective-permute-start | bytes 3145736 | tf_op jit(solution)/shard_map/ppermute | solution.py:1136
  462.3 8.6 %collective-permute-start.13 = (bf16[512,2048]{1,0:T(8,128)(2,1)}, bf16[512,2048]{1,0:T(8,128)(2,1)}, u32[]{:S(2)}, u32[]{:S(2)}) collective-permute-start(bf16[512,2048]{1,0:T(8,128)(2,1)} %add_convert_fusion), channel_id=1, source_target_pairs={{0,4},{4,0},{1,5},{5,1},{2,6},{6,2},{3,7},{7,3},{8,12},{12,8},{9,1... | collective-permute-start | bytes 6291464 | tf_op jit(solution)/shard_map/ppermute | solution.py:1136
  481.6 33.9 %copy-start.1 = (bf16[8,2048]{1,0:T(8,128)(2,1)S(1)}, bf16[8,2048]{1,0:T(8,128)(2,1)}, u32[]{:S(2)}) copy-start(bf16[8,2048]{1,0:T(8,128)(2,1)} %param.39) | copy-start | bytes 98308
  (66 other events, 298.9 us)
Sparse Core Ops, SparseCore 0:
  12.0 205.7 all-gather.2

commit v4 on v3

--- a/solution.py
+++ b/solution.py
@@ -119,24 +119,18 @@
         ref = outs[a].at[piece_of(up, t), rows(a, who, part)]
         return remote(ref, ref, p_send.at[a, way, t, kind], p_recv.at[a, way, t, kind], spot.to("xyxy"[kind]))
 
-    for a in range(k):
+    def begin(a):
         for up in (True, False):
 
             @pl.when(sends(up, 0))
             def _():
                 z_copy(a, up, 0, True).start()
 
-    block_copy(0, True).start()
-    block_copy(1, True).start()
-
-    for t in range(n):
-        if t == n - 1:
-            block_copy(1, False).wait_recv()
-            block_copy(2, True).start()
-            block_copy(0, False).wait_recv()
-            block_copy(3, True).start()
-        if t < n - 1:
-            for a in range(k):
+    begin(0)
+    for step in range(n + k - 1):
+        for a in range(k):
+            t = step - a
+            if 0 <= t < n - 1:
                 for up in (True, False):
 
                     @pl.when(receives(up, t))
@@ -151,8 +145,12 @@
                         plane_copy(a, up, t, 0).start()
                         plane_copy(a, up, t, 1).start()
 
-        if t > 0:
-            for a in range(k):
+            if t == 0 and a + 1 < k:
+                begin(a + 1)
+                block_copy(0, True).start()
+                block_copy(1, True).start()
+
+            if 0 < t < n:
                 for up in (True, False):
 
                     @pl.when(receives(up, t - 1))
@@ -161,6 +159,11 @@
                         plane_copy(a, up, t - 1, 3).start()
                         landed(a, up, t - 1, 1).wait_recv()
                         plane_copy(a, up, t - 1, 2).start()
+
+    block_copy(1, False).wait_recv()
+    block_copy(2, True).start()
+    block_copy(0, False).wait_recv()
+    block_copy(3, True).start()
 
     for t in range(n - 1):
         for a in range(k):
@@ -200,163 +203,140 @@
     )(*arrays, block)
 
 
-def line_sum_kernel(n, up, own, out, box, send, recv):
+def look_back_kernel(n, near, whole, edge, states, before, box, send, recv, e_send, e_recv):
     spot = Spot()
     s = spot.s
-    greet(spot, n, ("up", "dn"))
-    go = "up" if up else "dn"
-
-    def sends(t):
-        return ((s - t >= 0) & (s + 1 < n)) if up else ((s + t < n) & (s > 0))
-
-    def receives(t):
-        return s - 1 - t >= 0 if up else s + 1 + t < n
-
-    def copy(t):
-        src = own if t == 0 else box.at[t - 1]
-        return remote(src, box.at[t], send.at[t], recv.at[t], spot.to(go))
-
-    @pl.when(sends(0))
+    bar = pltpu.get_barrier_semaphore()
+    for i in range(1, n):
+        pl.semaphore_signal(
+            bar, inc=1, device_id={"seq": (s + i) % n, "mp": spot.m, "dp": spot.d}, device_id_type=MESH
+        )
+    pl.semaphore_wait(bar, n - 1)
+    edge_copy = remote(edge, before, e_send, e_recv, spot.to("up"))
+
+    def copy(i):
+        return remote(
+            near if i == 1 else whole,
+            box.at[i - 1],
+            send.at[i - 1],
+            recv.at[i - 1],
+            {"seq": s + i, "mp": spot.m, "dp": spot.d},
+        )
+
+    @pl.when(s + 1 < n)
     def _():
-        copy(0).start()
-
-    out[...] = jnp.zeros_like(out)
-    for t in range(n - 1):
-
-        @pl.when(receives(t))
+        edge_copy.start()
+
+    for i in range(1, n):
+
+        @pl.when(s + i < n)
         def _():
-            copy(t).wait_recv()
-            if t + 1 < n - 1:
-
-                @pl.when(sends(t + 1))
-                def _():
-                    copy(t + 1).start()
-
-            out[...] += box[t].astype(jnp.float32)
-
-    for t in range(n - 1):
-
-        @pl.when(sends(t))
+            copy(i).start()
+
+    states[...] = jnp.zeros_like(states)
+
+    @pl.when(s > 0)
+    def _():
+        edge_copy.wait_recv()
+
+    @pl.when(s == 0)
+    def _():
+        before[...] = jnp.zeros_like(before)
+
+    for i in range(1, n):
+
+        @pl.when(s - i >= 0)
         def _():
-            copy(t).wait_send()
-
-
-def line_sum(n, own, up, cid):
+            copy(i).wait_recv()
+            states[...] += box[i - 1].astype(jnp.float32)
+
+    @pl.when(s + 1 < n)
+    def _():
+        edge_copy.wait_send()
+
+    for i in range(1, n):
+
+        @pl.when(s + i < n)
+        def _():
+            copy(i).wait_send()
+
+
+def look_back(n, near, whole, edge, cid):
     DMA = pltpu.SemaphoreType.DMA
+    vmem = pl.BlockSpec(memory_space=pltpu.VMEM)
     return pl.pallas_call(
-        functools.partial(line_sum_kernel, n, up),
-        out_shape=jax.ShapeDtypeStruct(own.shape, jnp.float32),
-        in_specs=[pl.BlockSpec(memory_space=pltpu.VMEM)],
-        out_specs=pl.BlockSpec(memory_space=pltpu.VMEM),
-        scratch_shapes=[pltpu.VMEM((n - 1,) + own.shape, own.dtype), DMA((n - 1,)), DMA((n - 1,))],
+        functools.partial(look_back_kernel, n),
+        out_shape=[
+            jax.ShapeDtypeStruct(whole.shape, jnp.float32),
+            jax.ShapeDtypeStruct(edge.shape, edge.dtype),
+        ],
+        in_specs=[vmem] * 3,
+        out_specs=[vmem] * 2,
+        scratch_shapes=[pltpu.VMEM((n - 1,) + whole.shape, whole.dtype), DMA((n - 1,)), DMA((n - 1,)), DMA, DMA],
         compiler_params=pltpu.CompilerParams(collective_id=cid, has_side_effects=True, vmem_limit_bytes=40 << 20),
-        name=f"line_sum_{cid}",
-    )(own)
+        name="look_back",
+    )(near, whole, edge)
+
+
 def plane_total_kernel(
-    n, shared, part, out, mine, core_in, xin, yin, t2, xin2, yin2, line, c_send, c_recv, p_send, p_recv, z_send, z_recv, g_send, g_recv
+    n, shared, part, out, mine, core_in, near, line, c_send, c_recv, p_send, p_recv, z_send, z_recv, g_send, g_recv
 ):
     spot = Spot()
-    s, d = spot.s, spot.d
-    h = out.shape[1] // 2
-    A, B = pl.ds(0, h), pl.ds(h, h)
+    s, m, d = spot.s, spot.m, spot.d
+    h = out.shape[1]
     f32, b16 = jnp.float32, jnp.bfloat16
     mine[...] = part[...].astype(b16)
-    greet(spot, n, ("x", "y", "c", "up", "dn"))
+    bar = pltpu.get_barrier_semaphore()
+    plane = [{"seq": s, "mp": m, "dp": (d + i) % 4} for i in range(1, 4)]
+    lines = [{"seq": (s + i) % n, "mp": m, "dp": d} for i in range(1, n)]
+    for where in plane + lines + [spot.to("c")]:
+        pl.semaphore_signal(bar, inc=1, device_id=where, device_id_type=MESH)
+    pl.semaphore_wait(bar, n + 3)
     core = remote(mine.at[pl.ds(0, shared)], core_in, c_send, c_recv, spot.to("c"))
     core.start()
     core.wait()
     mine[:shared] = (mine[:shared].astype(f32) + core_in[...].astype(f32)).astype(b16)
 
-    def block(who, part):
-        return mine.at[pl.ds(who * 2 * h + part * h, h)]
-
-    def read(who, part):
-        return mine[pl.ds(who * 2 * h + part * h, h)].astype(f32)
-
-    first = (
-        remote(block(spot.diag, 0), xin.at[1], p_send.at[0], p_recv.at[0], spot.to("x")),
-        remote(block(spot.diag, 1), yin.at[1], p_send.at[1], p_recv.at[1], spot.to("y")),
-        remote(block(spot.x, 0), xin.at[0], p_send.at[2], p_recv.at[2], spot.to("x")),
-        remote(block(spot.y, 1), yin.at[0], p_send.at[3], p_recv.at[3], spot.to("y")),
-    )
-    for c in first:
-        c.start()
-    second = (
-        remote(t2.at[0], yin2, p_send.at[4], p_recv.at[4], spot.to("y")),
-        remote(t2.at[1], xin2, p_send.at[5], p_recv.at[5], spot.to("x")),
-    )
-    first[0].wait_recv()
-    t2[0] = (read(spot.y, 0) + xin[1].astype(f32)).astype(b16)
-    second[0].start()
-    first[1].wait_recv()
-    t2[1] = (read(spot.x, 1) + yin[1].astype(f32)).astype(b16)
-    second[1].start()
-    first[2].wait_recv()
-    first[3].wait_recv()
-    second[0].wait_recv()
-    line[s, A] = (read(d, 0) + xin[0].astype(f32) + yin2[...].astype(f32)).astype(b16)
-    second[1].wait_recv()
-    line[s, B] = (read(d, 1) + yin[0].astype(f32) + xin2[...].astype(f32)).astype(b16)
-
-    def sends(up, t):
-        return ((s - t >= 0) & (s + 1 < n)) if up else ((s + t < n) & (s > 0))
-
-    def receives(up, t):
-        return s - 1 - t >= 0 if up else s + 1 + t < n
-
-    def z_copy(up, t, sending):
-        way = 0 if up else 1
-        piece = (s - t if up else s + t) if sending else (s - 1 - t if up else s + 1 + t)
-        return remote(line.at[piece], line.at[piece], z_send.at[way, t], z_recv.at[way, t], spot.to("up" if up else "dn"))
-
-    for up in (True, False):
-
-        @pl.when(sends(up, 0))
-        def _():
-            z_copy(up, 0, True).start()
-
-    for t in range(n - 1):
-        for up in (True, False):
-
-            @pl.when(receives(up, t))
-            def _():
-                z_copy(up, t, False).wait_recv()
-                if t + 1 < n - 1:
-
-                    @pl.when(sends(up, t + 1))
-                    def _():
-                        z_copy(up, t + 1, True).start()
-
+    def rows(who):
+        return pl.ds(pl.multiple_of(who * h, h), h)
+
+    def scatter(i):
+        return remote(mine.at[rows((d + i) % 4)], near.at[i - 1], p_send.at[i - 1], p_recv.at[i - 1], plane[i - 1])
+
+    for i in (2, 1, 3):
+        scatter(i).start()
+    total = mine[rows(d)].astype(f32)
+    for i in range(1, 4):
+        scatter(i).wait_recv()
+        total = total + near[i - 1].astype(f32)
+    line[s] = total.astype(b16)
+
+    def along(i, sending):
+        who = s if sending else (s - i) % n
+        return remote(line.at[who], line.at[who], z_send.at[i - 1], z_recv.at[i - 1], lines[i - 1])
+
+    for i in range(1, n):
+        along(i, True).start()
+    for i in range(1, n):
+        along(i, False).wait_recv()
     total = line[0].astype(f32)
     for i in range(1, n):
         total = total + line[i].astype(f32)
     out[d] = total.astype(b16)
 
-    parts = (A, B)
-
-    def back(kind, sending):
-        who = (d, d, spot.y, spot.x)[kind] if sending else (spot.x, spot.y, spot.diag, spot.diag)[kind]
-        ref = out.at[who] if kind < 2 else out.at[who, parts[kind - 2]]
-        return remote(ref, ref, g_send.at[kind], g_recv.at[kind], spot.to("xyxy"[kind]))
-
-    back(0, True).start()
-    back(1, True).start()
-    back(0, False).wait_recv()
-    back(3, True).start()
-    back(1, False).wait_recv()
-    back(2, True).start()
-    back(2, False).wait_recv()
-    back(3, False).wait_recv()
-    for kind in range(4):
-        back(kind, True).wait_send()
-    for c in first + second:
-        c.wait_send()
-    for t in range(n - 1):
-        for up in (True, False):
-
-            @pl.when(sends(up, t))
-            def _():
-                z_copy(up, t, True).wait_send()
+    def back(i, sending):
+        who = d if sending else (d - i) % 4
+        return remote(out.at[who], out.at[who], g_send.at[i - 1], g_recv.at[i - 1], plane[i - 1])
+
+    for i in (2, 1, 3):
+        back(i, True).start()
+    for i in range(1, 4):
+        back(i, False).wait_recv()
+    for i in range(1, 4):
+        scatter(i).wait_send()
+        back(i, True).wait_send()
+    for i in range(1, n):
+        along(i, True).wait_send()
 
 
 def plane_total(n, part, shared, cid):
@@ -364,32 +344,28 @@
     V = pltpu.VMEM
     b = jnp.bfloat16
     rows, w = part.shape
-    h = rows // 8
+    h = rows // 4
     return pl.pallas_call(
         functools.partial(plane_total_kernel, n, shared),
-        out_shape=jax.ShapeDtypeStruct((4, 2 * h, w), b),
+        out_shape=jax.ShapeDtypeStruct((4, h, w), b),
         in_specs=[pl.BlockSpec(memory_space=pltpu.VMEM)],
         out_specs=pl.BlockSpec(memory_space=pltpu.VMEM),
         scratch_shapes=[
             V((rows, w), b),
             V((shared, w), b),
-            V((2, h, w), b),
-            V((2, h, w), b),
-            V((2, h, w), b),
-            V((h, w), b),
-            V((h, w), b),
-            V((n, 2 * h, w), b),
+            V((3, h, w), b),
+            V((n, h, w), b),
             DMA,
             DMA,
-            DMA((6,)),
-            DMA((6,)),
-            DMA((2, n - 1)),
-            DMA((2, n - 1)),
-            DMA((4,)),
-            DMA((4,)),
+            DMA((3,)),
+            DMA((3,)),
+            DMA((n - 1,)),
+            DMA((n - 1,)),
+            DMA((3,)),
+            DMA((3,)),
         ],
         compiler_params=pltpu.CompilerParams(collective_id=cid, has_side_effects=True, vmem_limit_bytes=40 << 20),
-        name=f"plane_total_{cid}",
+        name="plane_total",
     )(part)
 
 
@@ -449,35 +425,42 @@
     return jnp.where(lax.axis_index("seq") == 0, SPAN, 0)
 
 
-def key_state_kernel(kv, kmaps, out):
-    first = start_row()
+def key_state_kernel(kv, kmaps, near, whole):
     b16 = jnp.bfloat16
-    out[512:] = jnp.zeros((16, 128), b16)
+    rows = kv.shape[1]
+    near[512:] = jnp.zeros((16, 128), b16)
+    whole[512:] = jnp.zeros((16, 128), b16)
     for e in range(2):
         for gp in range(2):
-            parts = []
+            parts = ([], [])
             for j in range(2):
                 g = 2 * gp + j
-                keys = kv[e, :256, g * 64 : g * 64 + 64]
-                values = with_ones(kv[e, :256, 256 + g * 64 : 320 + g * 64], first)
+                keys = kv[e, :, g * 64 : g * 64 + 64]
+                values = with_ones(kv[e, :, 256 + g * 64 : 320 + g * 64], 0)
                 feats = maps_of(mm(keys, signed_map(kmaps[g]))).astype(b16)
-                state = mm(feats, values, ((0,), (0,)))
-                parts.append(state[:, :64])
-                total = mm(pick(64), state.astype(b16), ((1,), (1,)))
-                out[512 + e * 4 + g : 513 + e * 4 + g] = total[:1].astype(b16)
-            block = jnp.concatenate(parts, 1).astype(b16)
-            out[(e * 2 + gp) * 128 : (e * 2 + gp) * 128 + 128] = block
-
-
-def key_state(kv_ext, kmaps):
+                cut = rows - SPAN
+                state = mm(feats[:cut], values[:cut], ((0,), (0,)))
+                for out, part in ((near, 0), (whole, 1)):
+                    if part:
+                        state = state + mm(feats[cut:], values[cut:], ((0,), (0,)))
+                    parts[part].append(state[:, :64])
+                    total = mm(pick(64), state.astype(b16), ((1,), (1,)))
+                    out[512 + e * 4 + g : 513 + e * 4 + g] = total[:1].astype(b16)
+            for out, part in ((near, 0), (whole, 1)):
+                block = jnp.concatenate(parts[part], 1).astype(b16)
+                out[(e * 2 + gp) * 128 : (e * 2 + gp) * 128 + 128] = block
+
+
+def key_state(kv, kmaps):
+    vmem = pl.BlockSpec(memory_space=pltpu.VMEM)
     return pl.pallas_call(
         key_state_kernel,
-        out_shape=jax.ShapeDtypeStruct((528, 128), jnp.bfloat16),
-        in_specs=[pl.BlockSpec(memory_space=pltpu.VMEM)] * 2,
-        out_specs=pl.BlockSpec(memory_space=pltpu.VMEM),
+        out_shape=[jax.ShapeDtypeStruct((528, 128), jnp.bfloat16)] * 2,
+        in_specs=[vmem] * 2,
+        out_specs=[vmem] * 2,
         compiler_params=pltpu.CompilerParams(vmem_limit_bytes=40 << 20),
         name="key_state",
-    )(kv_ext, kmaps)
+    )(kv, kmaps)
 
 
 STACK = 4
@@ -615,6 +598,7 @@
             pl.BlockSpec((1, 1, 16, 128), lambda g, e: (e, g, 0, 0)),
         ],
         compiler_params=pltpu.CompilerParams(vmem_limit_bytes=40 << 20),
+        cost_estimate=pl.CostEstimate(flops=8 * 10**9, bytes_accessed=10**6, transcendentals=0),
         name="state_back",
     )(attn, dattn, inv, qf)
 
@@ -719,7 +703,7 @@
             pl.BlockSpec((8, 64, 64), lambda g, e: (g, 0, 0)),
         ],
         compiler_params=pltpu.CompilerParams(vmem_limit_bytes=40 << 20),
-        cost_estimate=pl.CostEstimate(flops=40 * 10**9, bytes_accessed=10**7, transcendentals=4 * 10**6),
+        cost_estimate=pl.CostEstimate(flops=8 * 10**9, bytes_accessed=10**7, transcendentals=4 * 10**6),
         name="attend_back",
     )(q, kv_ext, kv_ext, st, st, qmaps, kmaps, qf, grad1)
 
@@ -783,9 +767,9 @@
 CHUNKS = 4
 
 
-def feed_kernel(n, k, early, xn_own, ct_all, packed, gate, up, down, dxn, out_part, *scratch):
+def feed_kernel(n, k, early, xn_own, ct_all, packed, gate, up, down, res, gain, gsum, dres16, out_part, *scratch):
     (xn, ct, gw, uw, dw, da, oa, xin, yin, t2, xin2, yin2) = scratch[:12]
-    (o_sem, a_send, a_recv, w_sem, w_send, w_recv, z_sem, z_send, z_recv, c_send, c_recv, p_send, p_recv, st_sem) = scratch[12:]
+    (o_sem, a_send, a_recv, w_sem, w_send, w_recv, z_sem, z_send, z_recv, c_send, c_recv, p_send, p_recv, st_sem, e_sem) = scratch[12:]
     spot = Spot()
     s, m, d = spot.s, spot.m, spot.d
     f32, b16 = jnp.float32, jnp.bfloat16
@@ -926,6 +910,11 @@
         remote(xn.at[2, B], yin.at[0], p_send.at[3], p_recv.at[3], spot.to("y")),
     )
     stores = [pltpu.make_async_copy(ct.at[i], out_part.at[i], st_sem.at[i]) for i in range(4)]
+
+    again = (
+        pltpu.make_async_copy(res, da.at[0], e_sem.at[0]),
+        pltpu.make_async_copy(ct_all.at[3], ct.at[0], e_sem.at[1]),
+    )
 
     steps = 4 * CHUNKS
     turns = {}
@@ -1017,6 +1006,8 @@
             @pl.when(step == steps - 4 + i)
             def _():
                 stores[i].start()
+                if i == 1:
+                    again[0].start()
                 if i == 0:
                     first[0].start()
                     first[1].start()
@@ -1027,22 +1018,50 @@
         remote(t2.at[0], yin2, p_send.at[4], p_recv.at[4], spot.to("y")),
         remote(t2.at[1], xin2, p_send.at[5], p_recv.at[5], spot.to("x")),
     )
+    stores[0].wait()
+    again[1].start()
     first[0].wait_recv()
     t2[0] = (xn[2, A].astype(f32) + xin[1].astype(f32)).astype(b16)
     second[0].start()
     first[1].wait_recv()
     t2[1] = (xn[1, B].astype(f32) + yin[1].astype(f32)).astype(b16)
     second[1].start()
+    for c in first:
+        c.wait_send()
+    for c in again:
+        c.wait()
     first[2].wait_recv()
     first[3].wait_recv()
     second[0].wait_recv()
-    dxn[A] = da[3, A] + xin[0].astype(f32) + yin2[...].astype(f32)
     second[1].wait_recv()
-    dxn[B] = da[3, B] + yin[0].astype(f32) + xin2[...].astype(f32)
-
-    for c in stores:
+    scale = gain[...].astype(f32)
+    chunk = half // 4
+    gsum[...] = jnp.zeros_like(gsum)
+    for part, inner, outer in ((0, xin, yin2), (1, yin, xin2)):
+
+        @pl.loop(0, 4)
+        def _(i):
+            at = pl.ds(pl.multiple_of(i * chunk, chunk), chunk)
+            rows = pl.ds(pl.multiple_of(part * half + i * chunk, chunk), chunk)
+            dxn = da[3, rows] + inner[0, at].astype(f32) + outer[at].astype(f32)
+            r = da[0, rows]
+            inv = lax.rsqrt(jnp.mean(r * r, -1, keepdims=True) + epsilon)
+            ri = r * inv
+            gsum[...] += jnp.sum((dxn * ri).reshape(chunk // 8, 8, -1), 0)
+            gx = scale * dxn
+            grad = ct[0, rows].astype(f32) + inv * (gx - ri * jnp.mean(gx * ri, -1, keepdims=True))
+            xn[0, rows] = grad.astype(b16)
+
+    swap = remote(xn.at[0], dres16.at[m], e_sem.at[2], e_sem.at[3], spot.to("c"))
+    keep = pltpu.make_async_copy(xn.at[0], dres16.at[m], e_sem.at[4])
+    swap.start()
+    keep.start()
+    keep.wait()
+    swap.wait_send()
+    remote(xn.at[0], dres16.at[1 - m], e_sem.at[2], e_sem.at[3], spot.to("c")).wait_recv()
+    for c in stores[1:]:
         c.wait()
-    for c in first + second:
+    for c in second:
         c.wait_send()
     for q in range(early):
         for c in early_core(q):
@@ -1059,7 +1078,7 @@
                         z_copy(i, w, upward, t, True).wait_send()
 
 
-def feed(n, early, xn_own, ct_all, packed, gate, up, down, cid):
+def feed(n, early, xn_own, ct_all, packed, gate, up, down, res, gain, cid):
     DMA, V = pltpu.SemaphoreType.DMA, pltpu.VMEM
     b, f32 = jnp.bfloat16, jnp.float32
     r, w = xn_own.shape
@@ -1075,16 +1094,20 @@
     scratch += [DMA((2,)), DMA((4,)), DMA((4,))]
     scratch += [DMA((max(early, 1), pieces))] * 3
     scratch += [DMA((late, 3)), DMA((late, 3, 2, n - 1)), DMA((late, 3, 2, n - 1)), DMA((late, 3, n)), DMA((late, 3, n))]
-    scratch += [DMA((6,)), DMA((6,)), DMA((4,))]
+    scratch += [DMA((6,)), DMA((6,)), DMA((4,)), DMA((5,))]
     return pl.pallas_call(
         functools.partial(feed_kernel, n, k, early),
-        out_shape=[jax.ShapeDtypeStruct((r, w), f32), jax.ShapeDtypeStruct((4, r, w), b)],
-        in_specs=[pl.BlockSpec(memory_space=ANY)] * 6,
-        out_specs=[pl.BlockSpec(memory_space=pltpu.VMEM), pl.BlockSpec(memory_space=ANY)],
+        out_shape=[
+            jax.ShapeDtypeStruct((8, w), f32),
+            jax.ShapeDtypeStruct((2, r, w), b),
+            jax.ShapeDtypeStruct((4, r, w), b),
+        ],
+        in_specs=[pl.BlockSpec(memory_space=ANY)] * 7 + [pl.BlockSpec(memory_space=pltpu.VMEM)],
+        out_specs=[pl.BlockSpec(memory_space=pltpu.VMEM)] + [pl.BlockSpec(memory_space=ANY)] * 2,
         scratch_shapes=scratch,
         compiler_params=pltpu.CompilerParams(collective_id=cid, has_side_effects=True, vmem_limit_bytes=62 << 20),
         name="feed",
-    )(xn_own, ct_all, packed, gate, up, down)
+    )(xn_own, ct_all, packed, gate, up, down, res, gain)
 
 
 def pack_early(k, early, gate, up, down, d):
@@ -1100,6 +1123,65 @@
         rows += [dn[q * unit : (q + 1) * unit, i : i + wd] for i in range(0, k, wd)]
         chunks.append(jnp.concatenate(rows, 0))
     return jnp.stack(chunks)
+
+
+def branch_kernel(n, attn, weight, first, second, tok, gain, res, xn, inner, part, other, send, recv):
+    spot = Spot()
+    m = spot.m
+    f32, b16 = jnp.float32, jnp.bfloat16
+    half = attn.shape[0] // 2
+    k = weight.shape[2]
+    greet(spot, n, ("c",))
+    low = mm(attn[...], first[...])
+    inner[...] = low
+
+    def terms(who, i):
+        rows = pl.ds(pl.multiple_of(who * half, half), half)
+        return mm(attn[rows], weight[i]) + mm(
+            inner[rows].astype(b16), second[:, i * k : (i + 1) * k]
+        )
+
+    for i in range(n):
+        part[:, i * k : (i + 1) * k] = terms(1 - m, i).astype(b16)
+    swap = remote(part, other, send, recv, spot.to("c"))
+    swap.start()
+    mine = pl.ds(pl.multiple_of(m * half, half), half)
+    for i in range(n):
+        cols = slice(i * k, (i + 1) * k)
+        res[:, cols] = tok[mine, cols].astype(f32) + terms(m, i)
+    swap.wait_recv()
+    scale = gain[...].astype(f32)
+    step = 64
+
+    @pl.loop(0, half // step)
+    def _(i):
+        at = pl.ds(pl.multiple_of(i * step, step), step)
+        r = res[at] + other[at].astype(f32)
+        res[at] = r
+        xn[at] = (r * lax.rsqrt(jnp.mean(r * r, -1, keepdims=True) + epsilon) * scale).astype(b16)
+
+    swap.wait_send()
+
+
+def branch(n, attn, weight, first, second, tok, gain, cid):
+    DMA, V = pltpu.SemaphoreType.DMA, pltpu.VMEM
+    b, f32 = jnp.bfloat16, jnp.float32
+    total, width = tok.shape
+    half = total // 2
+    vmem = pl.BlockSpec(memory_space=pltpu.VMEM)
+    return pl.pallas_call(
+        functools.partial(branch_kernel, n),
+        out_shape=[
+            jax.ShapeDtypeStruct((half, width), f32),
+            jax.ShapeDtypeStruct((half, width), b),
+            jax.ShapeDtypeStruct((total, first.shape[1]), f32),
+        ],
+        in_specs=[vmem] * 6,
+        out_specs=[vmem] * 3,
+        scratch_shapes=[V((half, width), b), V((half, width), b), DMA, DMA],
+        compiler_params=pltpu.CompilerParams(collective_id=cid, has_side_effects=True, vmem_limit_bytes=48 << 20),
+        name="branch",
+    )(attn, weight, first, second, tok, gain)
 
 
 EARLY = 3
@@ -1208,23 +1290,34 @@
     key3 = key_half.reshape(seq_count, rows_here, heads_kv * head_size)
     value3 = value_half.reshape(seq_count, rows_here, heads_kv * head_size)
     kv3 = jnp.concatenate([key3, value3], -1)
-    kv_prev = from_behind(kv3[:, rows_here - SOFTMAX_SPAN :], "seq", 1)
+    near, whole = key_state(kv3, key_feature_matrix)
+    states, kv_prev = look_back(n, near, whole, kv3[:, rows_here - SOFTMAX_SPAN :], 3)
     kv_ext = jnp.concatenate([kv_prev, kv3], 1)
-    states = line_sum(n, key_state(kv_ext, key_feature_matrix), True, 3)
     attn16, qfeats, inv_weights = attend(query_half, kv_ext, states, query_feature_matrix, key_feature_matrix)
-    inner_output = dot(attn16, output_adapter_down)
-    branch = jnp.concatenate([dot(attn16, out_g[i]) for i in range(n)], 1) + dot(
-        inner_output.astype(b16), output_adapter_up
-    )
-    branch16 = branch.astype(b16)
-    from_other = swap_core(lax.dynamic_slice_in_dim(branch16, (1 - m) * half, half, 0))
-    resid = my_half(inputs) + my_half(branch) + from_other.astype(f32)
-    gain_mlp = feedforward_norm_gain.astype(f32)
-    rms_mlp = lax.rsqrt(jnp.mean(resid * resid, -1, keepdims=True) + epsilon)
-    normed_mlp = (resid * rms_mlp * gain_mlp).astype(b16)
-    dnormed_mlp, out_part = feed(
-        n, EARLY, normed_mlp, cot_blocks, packed, gate_weight, up_weight, down_weight, 4
-    )
+    resid, normed_mlp, inner_output = branch(
+        n,
+        attn16,
+        out_g,
+        output_adapter_down,
+        output_adapter_up,
+        tok2,
+        feedforward_norm_gain.reshape(1, width),
+        5,
+    )
+    mlp_gain_rows, dresid16, out_part = feed(
+        n,
+        EARLY,
+        normed_mlp,
+        cot_blocks,
+        packed,
+        gate_weight,
+        up_weight,
+        down_weight,
+        resid,
+        feedforward_norm_gain.reshape(1, width),
+        4,
+    )
+    dresid16 = dresid16.reshape(total_rows, width)
 
     def swap_chip(value, bit):
         return lax.ppermute(value, "dp", [(i, i ^ bit) for i in range(4)])
@@ -1234,9 +1327,7 @@
     lower_in = swap_chip(out_part[0::2, cut:], 2)
 
 
-    mlp_gain_term = jnp.sum(dnormed_mlp * resid * rms_mlp, 0)
-    dresid = cot_half.astype(f32) + norm_back(resid, rms_mlp, gain_mlp, dnormed_mlp)
-    dresid16 = both_halves(dresid.astype(b16))
+    mlp_gain_term = jnp.sum(mlp_gain_rows, 0)
     du_o = dot_t(dresid16, output_adapter_up)
     oup_term = t_dot(inner_output.astype(b16), dresid16)
     odown_term = t_dot(du_o.astype(b16), attn16)
@@ -1248,13 +1339,10 @@
     dtotals = jnp.pad(dtotals[:, :, ::8].reshape(-1, 128), ((0, 8), (0, 0)))
     dstates = jnp.concatenate([dstates, dtotals], 0)
     later = [from_behind(dstates, "seq", -i) for i in range(1, n)]
-    dresid_other = swap_core(dresid)
     dq16, dk_ext, dv_ext, dkfeats, dqmaps = attend_back(
         query_half, kv_ext, states, query_feature_matrix, key_feature_matrix, qfeats, grad1
     )
-    dq16, later, upper_in, lower_in, dresid_other = lax.optimization_barrier(
-        (dq16, later, upper_in, lower_in, dresid_other)
-    )
+    dq16, later, upper_in, lower_in = lax.optimization_barrier((dq16, later, upper_in, lower_in))
     upper_in2 = swap_chip((out_part[2, :cut].astype(f32) + upper_in[0].astype(f32)).astype(b16), 2)
     lower_in2 = swap_chip((out_part[1, cut:].astype(f32) + lower_in[0].astype(f32)).astype(b16), 1)
     later = functools.reduce(jnp.add, [a.astype(f32) for a in later])
@@ -1290,10 +1378,7 @@
     ]
     dnormed = dnormed.astype(f32) + swap_core(dnormed).astype(f32)
     attn_gain_term = jnp.sum(my_half(dnormed * inputs * rms_attn), 0)
-    dresid_both = jnp.concatenate(
-        [jnp.where(m == 0, dresid, dresid_other), jnp.where(m == 0, dresid_other, dresid)], 0
-    )
-    tokens_grad = (dresid_both + norm_back(inputs, rms_attn, gain_attn, dnormed)).reshape(
+    tokens_grad = (dresid16.astype(f32) + norm_back(inputs, rms_attn, gain_attn, dnormed)).reshape(
         seq_count, rows_here, width
     )
 

time: 530 us -> 508 us (0.958)
  other arithmetic: 47.7 us -> 24.5 us
  Pallas kernels: 371 us -> 386 us
  waiting for transfers between devices: 18.4 us -> 9.95 us
    pallas_call x2 -> x3, Pallas kernels: 10 us -> 31 us  [the longest x1 16.9 us: look_back(): pl.pallas_call(functools.partial(look_back_kernel, n), out_shape=[jax.Sha...]
    ppermute x5 -> x4, waiting for transfers between devices: 17.8 us -> 5.67 us  [from_behind(): lax.ppermute(value, axis, [(source, source + steps) for source in range(f...]
    convert_element_type x3 -> x0, other arithmetic: 6.44 us -> none  [the longest x1 3.58 us: per_device(): dresid16 = both_halves(dresid.astype(b16))]
    dot_general x11 -> x5, matrix products: 11.2 us -> 5.17 us  [dot(): return jnp.dot(left, right, preferred_element_type=f32)]
    select_n x2 -> x0, other arithmetic: 5.49 us -> none  [the longest x1 4.12 us: per_device(): jnp.where(m == 0, dresid, dresid_other)]
    unnamed x179 -> x146, local copies, waits for them, and re-layouts: 12.4 us -> 16.2 us
  transfers between devices with their start and end apart: 15 -> 11, of which waited for: 3 -> 3; matrix products, arithmetic and copies ran while one was open for 12% -> 6% of each run, Pallas kernels for 40% -> 46%
where the time goes in v4:
time: 508 us; the launch traced here: 501 us
  Pallas kernels  386 us (76%)
  local copies, waits for them, and re-layouts  31.4 us (6%)
  other arithmetic  24.5 us (5%)
  matrix products  22.8 us (4%)
  between operations  15.5 us (3%)
  starting transfers between devices  10.5 us (2%)
  waiting for transfers between devices  9.95 us (2%)
    pallas_call x1, Pallas kernels, gather_weights(): pl.pallas_call(functools.partial(gather_weights_kernel, n, k), out_shape=...  152 us
    pallas_call x1, Pallas kernels, feed(): pl.pallas_call(functools.partial(feed_kernel, n, k, early), out_shape=[ja...  130 us
    pallas_call x1, Pallas kernels, plane_total(): pl.pallas_call(functools.partial(plane_total_kernel, n, shared), out_shap...  25.8 us
    pallas_call x1, Pallas kernels, attend_back(): pl.pallas_call(attend_back_kernel, grid=(2, 2), out_shape=[jax.ShapeDtype...  19.8 us
    pallas_call x1, Pallas kernels, look_back(): pl.pallas_call(functools.partial(look_back_kernel, n), out_shape=[jax.Sha...  16.9 us
    unnamed x146, local copies, waits for them, and re-layouts  16.2 us
    dot_general x11, matrix products, dot_t(): lax.dot_general(left, right, (((1,), (1,)), ((), ())), preferred_element_...  13.4 us
    pallas_call x1, Pallas kernels, attend(): pl.pallas_call(attend_kernel, grid=(2, 2), out_shape=[jax.ShapeDtypeStruc...  13.4 us
  transfers between devices with their start and end apart: 11, of which 3 were waited for; matrix products, arithmetic and copies ran while one was open for 6% of the time, Pallas kernels for 46%

profile of v4, /device:TPU:0, one launch (start us, length us, event | category | flops | bytes accessed | tf_op | source)
XLA Modules:
  0.0 501.0 jit_solution(15189085947780649463)
XLA Ops:
  10.2 1.7 pad_maximum_fusion
  14.9 2.3 constant_dynamic-slice_fusion.9.refs_2_
  18.5 151.5 %gather_weights.1 = (bf16[4,512,1536]{2,1,0:T(8,128)(2,1)}, bf16[4,1024,512]{2,1,0:T(8,128)(2,1)}, bf16[4,256,2048]{2,1,0:T(8,128)(2,1)}) custom-call(bf16[512,1536]{1,0:T(8,128)(2,1)} %pad_maximum_fusion.2.refs_0_, bf16[1024,512]{1,0:T(8,128)(2,1)} %refs_1_.1, bf16[256,2048]{1,0:T(8,128)(2,1)} %constant_dynamic-slice_fusion.9.refs_2_), custom_call_target="tpu_custom_call" | custom-call | tf_op jit(solution)/shard_map/gather_weights/pallas_call | solution.py:194
  171.4 1.5 copy-done.63
  172.9 3.4 fusion.60
  177.2 5.4 %key_state.1 = (bf16[528,128]{1,0:T(8,128)(2,1)S(1)}, bf16[528,128]{1,0:T(8,128)(2,1)S(1)}) custom-call(bf16[2,256,512]{2,1,0:T(8,128)(2,1)S(1)} %pad_maximum_fusion.3.kv, bf16[4,64,64]{2,1,0:T(8,128)(2,1)S(1)} %copy-done.7), custom_call_target="tpu_custom_call" | custom-call | tf_op jit(solution)/shard_map/key_state/pallas_call | solution.py:456
  182.6 16.9 %look_back.1 = (f32[528,128]{1,0:T(8,128)S(1)}, bf16[2,64,512]{2,1,0:T(8,128)(2,1)S(1)}) custom-call(bf16[528,128]{1,0:T(8,128)(2,1)S(1)} %get-tuple-element.51.near, bf16[528,128]{1,0:T(8,128)(2,1)S(1)} %get-tuple-element.52.whole, bf16[2,64,512]{2,1,0:T(8,128)(2,1)S(1)} %fusion.41.edge), custom_call_target="tpu_custom_call" | custom-call | tf_op jit(solution)/shard_map/look_back/pallas_call | solution.py:267
  200.4 13.4 %attend.1 = (bf16[512,1024]{1,0:T(8,128)(2,1)S(1)}, bf16[2,2,2,2,512,128]{5,4,3,2,1,0:T(8,128)(2,1)S(1)}, f32[2,512,8]{2,1,0:T(8,128)S(1)}) custom-call(bf16[512,1024]{1,0:T(8,128)(2,1)S(1)} %fusion.5.q, bf16[2,320,512]{2,1,0:T(8,128)(2,1)S(1)} %maximum_maximum_fusion.k.v, bf16[2,320,512]{2,1,0:T(8,128)(2,1)S(1)} %maximum_maximum_fusion.k.v, ...), custom_call_target="tpu_custom_call" | custom-call | tf_op jit(solution)/shard_map/attend/pallas_call | solution.py:534
  215.2 8.7 %branch.1 = (f32[256,2048]{1,0:T(8,128)S(1)}, bf16[256,2048]{1,0:T(8,128)(2,1)S(1)}, f32[512,8]{1,0:T(8,128)S(1)}) custom-call(bf16[512,1024]{1,0:T(8,128)(2,1)S(1)} %get-tuple-element.55.attn, bf16[4,1024,512]{2,1,0:T(8,128)(2,1)} %get-tuple-element.56.weight, bf16[1024,8]{1,0:T(8,128)(2,1)S(1)} %copy.36.first, bf16[8,2048]{1,0:T(8,128)(2,1)S(1)} %copy-done.15, ...), custom_call_target="tpu_custom_call" | custom-call | tf_op jit(solution)/shard_map/branch/pallas_call | solution.py:1172
  227.5 2.6 bitcast_convert_fusion.1
  230.1 129.9 %feed.1 = (f32[8,2048]{1,0:T(8,128)}, bf16[2,256,2048]{2,1,0:T(8,128)(2,1)}, bf16[4,256,2048]{2,1,0:T(8,128)(2,1)}) custom-call(bf16[256,2048]{1,0:T(8,128)(2,1)} %copy-done.6, bf16[4,256,2048]{2,1,0:T(8,128)(2,1)} %get-tuple-element.59.ct_all, bf16[4,3,1536,256]{3,2,1,0:T(8,128)(2,1)} %bitcast.92, bf16[512,4096]{1,0:T(8,128)(2,1)} %gate.1, ...), custom_call_target="tpu_custom_call" | custom-call | tf_op jit(solution)/shard_map/feed/pallas_call | solution.py:1098
  360.0 2.3 fusion.19
  362.3 2.1 fusion.17
  367.3 1.5 fusion.55
  368.8 1.7 collective-permute-start.3
  372.5 7.9 %state_back.1 = (bf16[2,2,2,2,512,128]{5,4,3,2,1,0:T(8,128)(2,1)S(1)}, bf16[512,128]{1,0:T(8,128)(2,1)S(1)}, bf16[2,2,16,128]{3,2,1,0:T(8,128)(2,1)S(1)}) custom-call(bf16[512,1024]{1,0:T(8,128)(2,1)S(1)} %copy-done.4, bf16[512,1024]{1,0:T(8,128)(2,1)S(1)} %add_convert_fusion.1.dattn, f32[2,512,8]{2,1,0:T(8,128)S(1)} %copy-done.21, ...), custom_call_target="tpu_custom_call" | custom-call | flops 8000000000 | bytes 1000000 | tf_op jit(solution)/shard_map/state_back/pallas_call | solution.py:586
  384.4 1.5 collective-permute-start.2
  386.0 1.6 copy-done.19
  387.5 1.6 copy-done.23
  389.1 19.8 %attend_back.1 = (bf16[512,1024]{1,0:T(8,128)(2,1)S(1)}, f32[2,320,256]{2,1,0:T(8,128)S(1)}, f32[2,320,256]{2,1,0:T(8,128)S(1)}, f32[2,4,320,128]{3,2,1,0:T(8,128)S(1)}, f32[16,64,64]{2,1,0:T(8,128)S(1)}) custom-call(bf16[512,1024]{1,0:T(8,128)(2,1)S(1)} %fusion.5.q, bf16[2,320,512]{2,1,0:T(8,128)(2,1)S(1)} %maximum_maximum_fusion.k.v, ...), custom_call_target="tpu_custom_call" | custom-call | flops 8000000000 | bytes 10000000 | tf_op jit(solution)/shard_map/attend_back/pallas_call | solution.py:677
  409.0 1.8 fusion.27
  413.4 7.2 %key_back.1 = (f32[2,320,256]{2,1,0:T(8,128)S(1)}, f32[2,320,256]{2,1,0:T(8,128)S(1)}, f32[4,64,64]{2,1,0:T(8,128)S(1)}) custom-call(bf16[2,320,512]{2,1,0:T(8,128)(2,1)S(1)} %maximum_maximum_fusion.k.v, bf16[2,320,512]{2,1,0:T(8,128)(2,1)S(1)} %maximum_maximum_fusion.k.v, f32[528,128]{1,0:T(8,128)S(1)} %convert_add_fusion.3.later.tot, ...), custom_call_target="tpu_custom_call" | custom-call | tf_op jit(solution)/shard_map/key_back/pallas_call | solution.py:743
  421.0 3.8 collective-permute-done.5
  425.6 1.7 collective-permute-start.8
  429.7 5.7 %collective-permute-done.8 = bf16[2,64,512]{2,1,0:T(8,128)(2,1)S(1)} collective-permute-done((bf16[2,64,512]{2,1,0:T(8,128)(2,1)S(1)}, bf16[2,64,512]{2,1,0:T(8,128)(2,1)S(1)}, u32[]{:S(2)}, u32[]{:S(2)}) %collective-permute-start.8) | collective-permute-done | bytes 131104 | tf_op jit(solution)/shard_map/ppermute | solution.py:1214
  435.8 3.4 fusion.8
  439.3 2.1 add_convert_fusion
  446.2 2.3 fusion.25
  450.3 1.5 pad_maximum_fusion.1
  452.6 3.4 multiply_reduce_fusion
  456.1 4.8 convert_add_fusion
  461.8 25.8 %plane_total.1 = bf16[4,352,128]{2,1,0:T(8,128)(2,1)S(1)} custom-call(f32[1408,128]{1,0:T(8,128)S(1)} %pad.9.part), custom_call_target="tpu_custom_call" | custom-call | tf_op jit(solution)/shard_map/plane_total/pallas_call | solution.py:348
  (236 shorter events, 45.0 us)
Async XLA Ops:
  7.2 192.4 %copy-start = (bf16[8,1024]{1,0:T(8,128)(2,1)S(1)}, bf16[8,1024]{1,0:T(8,128)(2,1)}, u32[]{:S(2)}) copy-start(bf16[8,1024]{1,0:T(8,128)(2,1)} %param.33) | copy-start | bytes 49156
  7.2 223.0 %all-gather.3.cloned.1.call-start = ((), (), s32[]{:S(2)}) async-start(), calls=%async_computation | async-start | bytes 11796480 | tf_op jit(solution)/shard_map/all_gather | solution.py:1254
  13.5 157.4 %copy-start.40 = (f32[2048]{0:T(1024)}, f32[2048]{0:T(1024)S(1)}, u32[]{:S(2)}) copy-start(f32[2048]{0:T(1024)S(1)} %convert_element_type.137) | copy-start | bytes 24580
  14.0 210.0 %copy-start.51 = (f32[1,2,2,128]{3,1,2,0:T(2,128)}, f32[1,2,2,128]{3,1,2,0:T(2,128)S(1)}, u32[]{:S(2)}) copy-start(f32[1,2,2,128]{3,1,2,0:T(2,128)S(1)} %copy.37) | copy-start | bytes 6148
  14.0 201.2 %copy-start.16 = (bf16[1,2048]{1,0:T(2,128)(2,1)}, bf16[1,2048]{1,0:T(2,128)(2,1)S(1)}, u32[]{:S(2)}) copy-start(bf16[1,2048]{1,0:T(2,128)(2,1)S(1)} %reshape.184.gain) | copy-start | bytes 12292
  18.5 151.5 %copy-start.48 = (bf16[2048,8]{0,1:T(8,128)(2,1)S(1)}, bf16[2048,8]{0,1:T(8,128)(2,1)}, u32[]{:S(2)}) copy-start(bf16[2048,8]{0,1:T(8,128)(2,1)} %param.32) | copy-start | bytes 98308
  18.5 151.6 %copy-start.49 = (bf16[2048,8]{0,1:T(8,128)(2,1)S(1)}, bf16[2048,8]{0,1:T(8,128)(2,1)}, u32[]{:S(2)}) copy-start(bf16[2048,8]{0,1:T(8,128)(2,1)} %param.34) | copy-start | bytes 98308
  18.5 151.6 %copy-start.50 = (bf16[2048,8]{0,1:T(8,128)(2,1)S(1)}, bf16[2048,8]{0,1:T(8,128)(2,1)}, u32[]{:S(2)}) copy-start(bf16[2048,8]{0,1:T(8,128)(2,1)} %param.36) | copy-start | bytes 98308
  170.8 28.7 %copy-start.43 = (bf16[512,24]{0,1:T(8,128)(2,1)}, bf16[512,24]{0,1:T(8,128)(2,1)S(1)}, u32[]{:S(2)}) copy-start(bf16[512,24]{0,1:T(8,128)(2,1)S(1)} %convolution_convert_fusion) | copy-start | bytes 73732
  200.0 15.2 %copy-start.15 = (bf16[8,2048]{1,0:T(8,128)(2,1)S(1)}, bf16[8,2048]{1,0:T(8,128)(2,1)}, u32[]{:S(2)}) copy-start(bf16[8,2048]{1,0:T(8,128)(2,1)} %second.1) | copy-start | bytes 98308
  215.2 8.8 %copy-start.3 = (bf16[512,1024]{1,0:T(8,128)(2,1)}, bf16[512,1024]{1,0:T(8,128)(2,1)S(1)}, u32[]{:S(2)}) copy-start(bf16[512,1024]{1,0:T(8,128)(2,1)S(1)} %get-tuple-element.55.attn) | copy-start | bytes 3145732
  215.2 8.8 %copy-start.20 = (f32[2,512,8]{2,1,0:T(8,128)}, f32[2,512,8]{2,1,0:T(8,128)S(1)}, u32[]{:S(2)}) copy-start(f32[2,512,8]{2,1,0:T(8,128)S(1)} %get-tuple-element.63.inv) | copy-start | bytes 98308
  215.2 12.3 %copy-start.25 = (bf16[2,256,2048]{2,1,0:T(8,128)(2,1)S(1)}, bf16[2,256,2048]{2,1,0:T(8,128)(2,1)}, u32[]{:S(2)}) copy-start(bf16[2,256,2048]{2,1,0:T(8,128)(2,1)} %param.21) | copy-start | bytes 6291460
  368.8 40.2 %collective-permute-start.3 = (bf16[2,128,2048]{2,1,0:T(8,128)(2,1)}, bf16[2,128,2048]{2,1,0:T(8,128)(2,1)}, u32[]{:S(2)}, u32[]{:S(2)}) collective-permute-start(bf16[2,128,2048]{2,1,0:T(8,128)(2,1)} %get-tuple-element.91), channel_id=1, source_target_pairs={{0,1},{1,0},{2,3},{3,2},{4,5},{5,4},{6,7},{7,6},{8,9},{9,8},{10,11... | collective-permute-start | bytes 3145736 | tf_op jit(solution)/shard_map/ppermute | solution.py:1323
  370.5 38.5 %collective-permute-start.4 = (bf16[2,128,2048]{2,1,0:T(8,128)(2,1)}, bf16[2,128,2048]{2,1,0:T(8,128)(2,1)}, u32[]{:S(2)}, u32[]{:S(2)}) collective-permute-start(bf16[2,128,2048]{2,1,0:T(8,128)(2,1)} %get-tuple-element.90), channel_id=1, source_target_pairs={{0,2},{1,3},{2,0},{3,1},{4,6},{5,7},{6,4},{7,5},{8,10},{9,11},{10,... | collective-permute-start | bytes 3145736 | tf_op jit(solution)/shard_map/ppermute | solution.py:1323
  372.5 13.4 %copy-start.8 = (bf16[4,64,64]{2,1,0:T(8,128)(2,1)S(1)}, bf16[4,64,64]{2,1,0:T(8,128)(2,1)}, u32[]{:S(2)}) copy-start(bf16[4,64,64]{2,1,0:T(8,128)(2,1)} %kmaps.7) | copy-start | bytes 98308
  372.5 13.4 %copy-start.12 = (bf16[16,64,64]{2,1,0:T(8,128)(2,1)S(1)}, bf16[16,64,64]{2,1,0:T(8,128)(2,1)}, u32[]{:S(2)}) copy-start(bf16[16,64,64]{2,1,0:T(8,128)(2,1)} %qmaps.3) | copy-start | bytes 393220
  381.8 27.2 %collective-permute-start = (bf16[528,128]{1,0:T(8,128)(2,1)S(1)}, bf16[528,128]{1,0:T(8,128)(2,1)S(1)}, u32[]{:S(2)}, u32[]{:S(2)}) collective-permute-start(bf16[528,128]{1,0:T(8,128)(2,1)S(1)} %fusion.40), channel_id=1, source_target_pairs={{8,0},{16,8},{24,16},{9,1},{17,9},{25,17},{10,2},{18,10},{26,18},{... | collective-permute-start | bytes 405512 | tf_op jit(solution)/shard_map/ppermute | solution.py:1214
  383.1 25.9 %collective-permute-start.1 = (bf16[528,128]{1,0:T(8,128)(2,1)S(1)}, bf16[528,128]{1,0:T(8,128)(2,1)S(1)}, u32[]{:S(2)}, u32[]{:S(2)}) collective-permute-start(bf16[528,128]{1,0:T(8,128)(2,1)S(1)} %fusion.40), channel_id=1, source_target_pairs={{16,0},{24,8},{17,1},{25,9},{18,2},{26,10},{19,3},{27,11},{20,4},{... | collective-permute-start | bytes 405512 | tf_op jit(solution)/shard_map/ppermute | solution.py:1214
  384.4 24.6 %collective-permute-start.2 = (bf16[528,128]{1,0:T(8,128)(2,1)S(1)}, bf16[528,128]{1,0:T(8,128)(2,1)S(1)}, u32[]{:S(2)}, u32[]{:S(2)}) collective-permute-start(bf16[528,128]{1,0:T(8,128)(2,1)S(1)} %fusion.40), channel_id=1, source_target_pairs={{24,0},{25,1},{26,2},{27,3},{28,4},{29,5},{30,6},{31,7}} | collective-permute-start | bytes 405512 | tf_op jit(solution)/shard_map/ppermute | solution.py:1214
  389.1 19.9 %copy-start.33 = (bf16[4,256,2048]{2,1,0:T(8,128)(2,1)S(1)}, bf16[4,256,2048]{2,1,0:T(8,128)(2,1)}, u32[]{:S(2)}) copy-start(bf16[4,256,2048]{2,1,0:T(8,128)(2,1)} %get-tuple-element.60) | copy-start | bytes 12582916
  410.9 14.0 %collective-permute-start.5 = (bf16[128,2048]{1,0:T(8,128)(2,1)S(1)}, bf16[128,2048]{1,0:T(8,128)(2,1)S(1)}, u32[]{:S(2)}, u32[]{:S(2)}) collective-permute-start(bf16[128,2048]{1,0:T(8,128)(2,1)S(1)} %get-tuple-element.89), channel_id=1, source_target_pairs={{0,2},{1,3},{2,0},{3,1},{4,6},{5,7},{6,4},{7,5},{8,10},{9,11},{10,... | collective-permute-start | bytes 1572872 | tf_op jit(solution)/shard_map/ppermute | solution.py:1323
  411.9 13.3 %collective-permute-start.6 = (bf16[128,2048]{1,0:T(8,128)(2,1)S(1)}, bf16[128,2048]{1,0:T(8,128)(2,1)S(1)}, u32[]{:S(2)}, u32[]{:S(2)}) collective-permute-start(bf16[128,2048]{1,0:T(8,128)(2,1)S(1)} %get-tuple-element.88), channel_id=1, source_target_pairs={{0,1},{1,0},{2,3},{3,2},{4,5},{5,4},{6,7},{7,6},{8,9},{9,8},{10,11... | collective-permute-start | bytes 1572872 | tf_op jit(solution)/shard_map/ppermute | solution.py:1323
  413.4 22.4 %slice-start = ((s8[6291456]{0:T(1024)(128)(4,1)}), s8[4194304]{0:T(1024)(128)(4,1)S(1)}, s32[]{:S(2)}) async-start(s8[6291456]{0:T(1024)(128)(4,1)} %bitcast.117), calls=%async_computation.1 | async-start | bytes 8388608
  421.0 18.3 %copy-start.47 = (bf16[512,8]{0,1:T(8,128)(2,1)}, bf16[512,8]{0,1:T(8,128)(2,1)S(1)}, u32[]{:S(2)}) copy-start(bf16[512,8]{0,1:T(8,128)(2,1)S(1)} %convolution_convert_fusion.3) | copy-start | bytes 24580
  425.5 10.3 %slice-start.1 = ((s8[6291456]{0:T(1024)(128)(4,1)}), s8[2097152]{0:T(1024)(128)(4,1)S(1)}, s32[]{:S(2)}) async-start(s8[6291456]{0:T(1024)(128)(4,1)} %bitcast.117), calls=%async_computation.2 | async-start | bytes 4194304
  425.6 9.8 %collective-permute-start.8 = (bf16[2,64,512]{2,1,0:T(8,128)(2,1)S(1)}, bf16[2,64,512]{2,1,0:T(8,128)(2,1)S(1)}, u32[]{:S(2)}, u32[]{:S(2)}) collective-permute-start(bf16[2,64,512]{2,1,0:T(8,128)(2,1)S(1)} %slice.247), channel_id=1, source_target_pairs={{8,0},{16,8},{24,16},{9,1},{17,9},{25,17},{10,2},{18,10},{26,18},{... | collective-permute-start | bytes 393224 | tf_op jit(solution)/shard_map/ppermute | solution.py:1214
  428.4 7.0 %copy-start.57 = (bf16[8,256]{1,0:T(8,128)(2,1)S(1)}, bf16[8,256]{1,0:T(8,128)(2,1)}, u32[]{:S(2)}) copy-start(bf16[8,256]{1,0:T(8,128)(2,1)} %param.37) | copy-start | bytes 12292
  428.5 7.2 %copy-start.59 = (bf16[8,256]{1,0:T(8,128)(2,1)S(1)}, bf16[8,256]{1,0:T(8,128)(2,1)}, u32[]{:S(2)}) copy-start(bf16[8,256]{1,0:T(8,128)(2,1)} %param.35) | copy-start | bytes 12292
  441.4 10.4 %collective-permute-start.9 = (bf16[512,2048]{1,0:T(8,128)(2,1)}, bf16[512,2048]{1,0:T(8,128)(2,1)}, u32[]{:S(2)}, u32[]{:S(2)}) collective-permute-start(bf16[512,2048]{1,0:T(8,128)(2,1)} %add_convert_fusion), channel_id=1, source_target_pairs={{0,4},{4,0},{1,5},{5,1},{2,6},{6,2},{3,7},{7,3},{8,12},{12,8},{9,1... | collective-permute-start | bytes 6291464 | tf_op jit(solution)/shard_map/ppermute | solution.py:1218
  442.0 6.9 %collective-permute-start.7 = (bf16[256,2048]{1,0:T(8,128)(2,1)S(1)}, bf16[256,2048]{1,0:T(8,128)(2,1)}, u32[]{:S(2)}, u32[]{:S(2)}) collective-permute-start(bf16[256,2048]{1,0:T(8,128)(2,1)S(1)} %fusion.7), channel_id=1, source_target_pairs={{0,4},{4,0},{1,5},{5,1},{2,6},{6,2},{3,7},{7,3},{8,12},{12,8},{9,1... | collective-permute-start | bytes 3145736 | tf_op jit(solution)/shard_map/ppermute | solution.py:1218
  456.0 4.8 copy-start.31
  (45 other events, 106.9 us)
Sparse Core Ops, SparseCore 0:
  12.0 205.8 all-gather.2

commit v5 on v4

--- a/solution.py
+++ b/solution.py
@@ -60,16 +60,24 @@
     pl.semaphore_wait(bar, count)
 
 
-def gather_weights_kernel(n, k, *refs):
-    ins, block, outs, blocks = refs[:k], refs[k], refs[k + 1 : 2 * k + 1], refs[2 * k + 1]
-    own_sem, z_send, z_recv, p_send, p_recv, b_send, b_recv = refs[2 * k + 2 :]
+def opening_kernel(n, k, *refs):
+    ins, block, tok, gain, downs, seconds, kmaps = refs[:k], *refs[k : k + 6]
+    refs = refs[k + 6 :]
+    outs, blocks, normed, inner, query, kv, states, before = refs[:k], *refs[k : k + 7]
+    weight, near, whole, box = refs[k + 7 : k + 11]
+    own_sem, z_send, z_recv, p_send, p_recv, b_send, b_recv, w_sem, l_send, l_recv, e_send, e_recv = refs[k + 11 :]
     spot = Spot()
     s, d = spot.s, spot.d
+    block = block.at[spot.m]
     own = [pltpu.make_async_copy(ins[a], outs[a].at[s], own_sem.at[a]) for a in range(k)]
     own.append(pltpu.make_async_copy(block, blocks.at[3], own_sem.at[k]))
     for c in own:
         c.start()
-    greet(spot, n, ("x", "y", "up", "dn"))
+    bar = pltpu.get_barrier_semaphore()
+    others = [{"seq": (s + i) % n, "mp": spot.m, "dp": d} for i in range(1, n)]
+    for where in [spot.to("x"), spot.to("y")] + others:
+        pl.semaphore_signal(bar, inc=1, device_id=where, device_id_type=MESH)
+    pl.semaphore_wait(bar, n + 1)
 
     cut = block.shape[0] // 2
     parts = (pl.ds(0, cut), pl.ds(cut, cut))
@@ -127,6 +135,18 @@
                 z_copy(a, up, 0, True).start()
 
     begin(0)
+    f32, b16 = jnp.float32, jnp.bfloat16
+    scale = gain[...].astype(f32)
+    total = tok.shape[0]
+
+    @pl.loop(0, total // 64)
+    def _(i):
+        at = pl.ds(pl.multiple_of(i * 64, 64), 64)
+        x = tok[at].astype(f32)
+        normed[at] = (x * lax.rsqrt(jnp.mean(x * x, -1, keepdims=True) + epsilon) * scale).astype(b16)
+
+    low = mm(normed[...], downs[...])
+    inner[...] = low
     for step in range(n + k - 1):
         for a in range(k):
             t = step - a
@@ -165,6 +185,53 @@
     block_copy(0, False).wait_recv()
     block_copy(3, True).start()
 
+    own[0].wait()
+    for t in range(n - 1):
+        for up in (True, False):
+
+            @pl.when(receives(up, t))
+            def _():
+                landed(0, up, t, 2).wait_recv()
+                landed(0, up, t, 3).wait_recv()
+
+    loads = [pltpu.make_async_copy(outs[0].at[i], weight.at[i], w_sem.at[i]) for i in range(n)]
+    for c in loads:
+        c.start()
+    for c in loads:
+        c.wait()
+    wide = query.shape[1]
+    length = kv.shape[1]
+    cols = weight.shape[2]
+    low16 = low.astype(b16)
+    for at in range(0, cols, 512):
+        full = mm(normed[...], weight[:, :, at : at + 512].reshape(-1, 512)) + mm(low16, seconds[:, at : at + 512])
+        if at < wide:
+            query[:, at : at + 512] = full.astype(b16)
+        else:
+            kv[...] = full.astype(b16).reshape(kv.shape)
+    key_states(kv, kmaps, near, whole)
+
+    edge_copy = remote(kv.at[:, pl.ds(length - before.shape[1], before.shape[1])], before, e_send, e_recv, spot.to("up"))
+
+    def state_copy(i):
+        return remote(
+            near if i == 1 else whole,
+            box.at[i - 1],
+            l_send.at[i - 1],
+            l_recv.at[i - 1],
+            {"seq": s + i, "mp": spot.m, "dp": d},
+        )
+
+    @pl.when(s + 1 < n)
+    def _():
+        edge_copy.start()
+
+    for i in range(1, n):
+
+        @pl.when(s + i < n)
+        def _():
+            state_copy(i).start()
+
     for t in range(n - 1):
         for a in range(k):
             for up in (True, False):
@@ -175,8 +242,9 @@
 
                 @pl.when(receives(up, t))
                 def _():
-                    landed(a, up, t, 2).wait_recv()
-                    landed(a, up, t, 3).wait_recv()
+                    if a:
+                        landed(a, up, t, 2).wait_recv()
+                        landed(a, up, t, 3).wait_recv()
                     for kind in range(4):
                         plane_copy(a, up, t, kind).wait_send()
 
@@ -184,54 +252,8 @@
         block_copy(kind, False).wait_recv()
     for kind in range(4):
         block_copy(kind, True).wait_send()
-    for c in own:
+    for c in own[1:]:
         c.wait()
-
-
-def gather_weights(n, arrays, block, cid):
-    k = len(arrays)
-    DMA = pltpu.SemaphoreType.DMA
-    return pl.pallas_call(
-        functools.partial(gather_weights_kernel, n, k),
-        out_shape=[jax.ShapeDtypeStruct((n,) + a.shape, a.dtype) for a in arrays]
-        + [jax.ShapeDtypeStruct((4,) + block.shape, block.dtype)],
-        in_specs=[pl.BlockSpec(memory_space=ANY)] * (k + 1),
-        out_specs=[pl.BlockSpec(memory_space=ANY)] * (k + 1),
-        scratch_shapes=[DMA((k + 1,)), DMA((k, 2, n - 1)), DMA((k, 2, n - 1)), DMA((k, 2, n - 1, 4)), DMA((k, 2, n - 1, 4)), DMA((4,)), DMA((4,))],
-        compiler_params=pltpu.CompilerParams(collective_id=cid, has_side_effects=True),
-        name="gather_weights",
-    )(*arrays, block)
-
-
-def look_back_kernel(n, near, whole, edge, states, before, box, send, recv, e_send, e_recv):
-    spot = Spot()
-    s = spot.s
-    bar = pltpu.get_barrier_semaphore()
-    for i in range(1, n):
-        pl.semaphore_signal(
-            bar, inc=1, device_id={"seq": (s + i) % n, "mp": spot.m, "dp": spot.d}, device_id_type=MESH
-        )
-    pl.semaphore_wait(bar, n - 1)
-    edge_copy = remote(edge, before, e_send, e_recv, spot.to("up"))
-
-    def copy(i):
-        return remote(
-            near if i == 1 else whole,
-            box.at[i - 1],
-            send.at[i - 1],
-            recv.at[i - 1],
-            {"seq": s + i, "mp": spot.m, "dp": spot.d},
-        )
-
-    @pl.when(s + 1 < n)
-    def _():
-        edge_copy.start()
-
-    for i in range(1, n):
-
-        @pl.when(s + i < n)
-        def _():
-            copy(i).start()
 
     states[...] = jnp.zeros_like(states)
 
@@ -247,8 +269,8 @@
 
         @pl.when(s - i >= 0)
         def _():
-            copy(i).wait_recv()
-            states[...] += box[i - 1].astype(jnp.float32)
+            state_copy(i).wait_recv()
+            states[...] += box[i - 1].astype(f32)
 
     @pl.when(s + 1 < n)
     def _():
@@ -258,24 +280,54 @@
 
         @pl.when(s + i < n)
         def _():
-            copy(i).wait_send()
-
-
-def look_back(n, near, whole, edge, cid):
-    DMA = pltpu.SemaphoreType.DMA
+            state_copy(i).wait_send()
+
+
+def opening(n, arrays, block, tok, gain, downs, seconds, kmaps, wide, cid):
+    k = len(arrays)
+    DMA, V = pltpu.SemaphoreType.DMA, pltpu.VMEM
+    b, f32 = jnp.bfloat16, jnp.float32
+    total, width = tok.shape
+    cols = arrays[0].shape[1]
+    depth = arrays[0].shape[0]
+    seqs, rows = block.shape[:2]
     vmem = pl.BlockSpec(memory_space=pltpu.VMEM)
+    far = pl.BlockSpec(memory_space=ANY)
     return pl.pallas_call(
-        functools.partial(look_back_kernel, n),
-        out_shape=[
-            jax.ShapeDtypeStruct(whole.shape, jnp.float32),
-            jax.ShapeDtypeStruct(edge.shape, edge.dtype),
-        ],
-        in_specs=[vmem] * 3,
-        out_specs=[vmem] * 2,
-        scratch_shapes=[pltpu.VMEM((n - 1,) + whole.shape, whole.dtype), DMA((n - 1,)), DMA((n - 1,)), DMA, DMA],
-        compiler_params=pltpu.CompilerParams(collective_id=cid, has_side_effects=True, vmem_limit_bytes=40 << 20),
-        name="look_back",
-    )(near, whole, edge)
+        functools.partial(opening_kernel, n, k),
+        out_shape=[jax.ShapeDtypeStruct((n,) + a.shape, a.dtype) for a in arrays]
+        + [
+            jax.ShapeDtypeStruct((4,) + block.shape[1:], b),
+            jax.ShapeDtypeStruct((total, width), b),
+            jax.ShapeDtypeStruct((total, downs.shape[1]), f32),
+            jax.ShapeDtypeStruct((total, wide), b),
+            jax.ShapeDtypeStruct((seqs, rows, cols - wide), b),
+            jax.ShapeDtypeStruct((528, 128), f32),
+            jax.ShapeDtypeStruct((seqs, SPAN, cols - wide), b),
+        ],
+        in_specs=[far] * (k + 1) + [vmem] * 5,
+        out_specs=[far] * (k + 1) + [vmem] * 6,
+        scratch_shapes=[
+            V((n, depth, cols), b),
+            V((528, 128), b),
+            V((528, 128), b),
+            V((n - 1, 528, 128), b),
+            DMA((k + 1,)),
+            DMA((k, 2, n - 1)),
+            DMA((k, 2, n - 1)),
+            DMA((k, 2, n - 1, 4)),
+            DMA((k, 2, n - 1, 4)),
+            DMA((4,)),
+            DMA((4,)),
+            DMA((n,)),
+            DMA((n - 1,)),
+            DMA((n - 1,)),
+            DMA,
+            DMA,
+        ],
+        compiler_params=pltpu.CompilerParams(collective_id=cid, has_side_effects=True, vmem_limit_bytes=48 << 20),
+        name="opening",
+    )(*arrays, block, tok, gain, downs, seconds, kmaps)
 
 
 def plane_total_kernel(
@@ -425,7 +477,7 @@
     return jnp.where(lax.axis_index("seq") == 0, SPAN, 0)
 
 
-def key_state_kernel(kv, kmaps, near, whole):
+def key_states(kv, kmaps, near, whole):
     b16 = jnp.bfloat16
     rows = kv.shape[1]
     near[512:] = jnp.zeros((16, 128), b16)
@@ -449,18 +501,6 @@
             for out, part in ((near, 0), (whole, 1)):
                 block = jnp.concatenate(parts[part], 1).astype(b16)
                 out[(e * 2 + gp) * 128 : (e * 2 + gp) * 128 + 128] = block
-
-
-def key_state(kv, kmaps):
-    vmem = pl.BlockSpec(memory_space=pltpu.VMEM)
-    return pl.pallas_call(
-        key_state_kernel,
-        out_shape=[jax.ShapeDtypeStruct((528, 128), jnp.bfloat16)] * 2,
-        in_specs=[vmem] * 2,
-        out_specs=[vmem] * 2,
-        compiler_params=pltpu.CompilerParams(vmem_limit_bytes=40 << 20),
-        name="key_state",
-    )(kv, kmaps)
 
 
 STACK = 4
@@ -558,8 +598,13 @@
     )(q, kv_ext, kv_ext, st, st, qmaps, kmaps)
 
 
-def state_back_kernel(attn, dattn, inv, qf, grad1, dst, dtot):
+def state_back_kernel(attn, dres, weight, du, down, inv, qf, grad1, dst, dtot, dattn):
     b16, f32 = jnp.bfloat16, jnp.float32
+    k = weight.shape[2]
+    grads = mm(du[...], down[...], ((1,), (1,)))
+    for i in range(weight.shape[0]):
+        grads = grads + mm(dres[:, i * k : (i + 1) * k], weight[i], ((1,), (1,)))
+    dattn[...] = grads.astype(b16)
     lane = lax.broadcasted_iota(jnp.int32, (STACK * TILE, 64), 1)
     states = []
     for j in range(2):
@@ -580,8 +625,9 @@
     dst[...] = jnp.concatenate(states, 1).astype(b16)
 
 
-def state_back(attn, dattn, inv, qf):
+def state_back(attn, dres, weight, du, down, inv, qf):
     b16 = jnp.bfloat16
+    n, _, k = weight.shape
     rows = pl.BlockSpec((256, 512), lambda g, e: (e, g))
     return pl.pallas_call(
         state_back_kernel,
@@ -591,16 +637,25 @@
             jax.ShapeDtypeStruct((512, 128), b16),
             jax.ShapeDtypeStruct((2, 2, 16, 128), b16),
         ],
-        in_specs=[rows, rows, pl.BlockSpec((1, 256, 8), lambda g, e: (g, e, 0)), STACKED],
+        in_specs=[
+            rows,
+            pl.BlockSpec((256, dres.shape[1]), lambda g, e: (e, 0)),
+            pl.BlockSpec((n, 512, k), lambda g, e: (0, g, 0)),
+            pl.BlockSpec((256, du.shape[1]), lambda g, e: (e, 0)),
+            pl.BlockSpec((512, du.shape[1]), lambda g, e: (g, 0)),
+            pl.BlockSpec((1, 256, 8), lambda g, e: (g, e, 0)),
+            STACKED,
+        ],
+        scratch_shapes=[pltpu.VMEM((256, 512), b16)],
         out_specs=[
             STACKED,
             pl.BlockSpec((128, 128), lambda g, e: (e * 2 + g, 0)),
             pl.BlockSpec((1, 1, 16, 128), lambda g, e: (e, g, 0, 0)),
         ],
-        compiler_params=pltpu.CompilerParams(vmem_limit_bytes=40 << 20),
+        compiler_params=pltpu.CompilerParams(vmem_limit_bytes=61 << 20),
         cost_estimate=pl.CostEstimate(flops=8 * 10**9, bytes_accessed=10**6, transcendentals=0),
         name="state_back",
-    )(attn, dattn, inv, qf)
+    )(attn, dres, weight, du, down, inv, qf)
 
 
 def attend_back_kernel(q, k, v, st, tot, qmaps, kmaps, qf, gr, dq, dk, dv, dkf, dqm):
@@ -1257,41 +1312,37 @@
     def my_half(a):
         return lax.dynamic_slice_in_dim(a, m * half, half, 0)
 
-    cot_half = my_half(cotangent.reshape(total_rows, width))
     qkv_own = jnp.concatenate([query_weight, key_weight, value_weight], 1)
-    qkv_g, out_g, cot_blocks = gather_weights(n, [qkv_own, output_weight], cot_half, 1)
-    qkv_w = qkv_g.reshape(width, -1)
-    wide = query_weight.shape[1]
-    kv_wide = key_weight.shape[1]
-
     def both_halves(own):
         other = swap_core(own)
         return jnp.concatenate([jnp.where(m == 0, own, other), jnp.where(m == 0, other, own)], 0)
 
+    wide = query_weight.shape[1]
+    kv_wide = key_weight.shape[1]
+    rank = query_adapter_down.shape[1]
     tok2 = tokens.reshape(total_rows, width)
-    inputs = tok2.astype(f32)
-    gain_attn = attention_norm_gain.astype(f32)
-    rms_attn = lax.rsqrt(jnp.mean(inputs * inputs, -1, keepdims=True) + epsilon)
-    normed = (inputs * rms_attn * gain_attn).astype(b16)
-
     downs = jnp.concatenate([query_adapter_down, key_adapter_down, value_adapter_down], 1)
-    inner = dot(normed, downs)
-    rank = query_adapter_down.shape[1]
-    full = dot(normed, qkv_w)
-
-    def project(index, first, last, second):
-        return (
-            full[:, first:last] + dot(inner[:, index * rank : (index + 1) * rank].astype(b16), second)
-        ).astype(b16)
-
-    query_half = project(0, 0, wide, query_adapter_up)
-    key_half = project(1, wide, wide + kv_wide, key_adapter_up)
-    value_half = project(2, wide + kv_wide, wide + 2 * kv_wide, value_adapter_up)
-    key3 = key_half.reshape(seq_count, rows_here, heads_kv * head_size)
-    value3 = value_half.reshape(seq_count, rows_here, heads_kv * head_size)
-    kv3 = jnp.concatenate([key3, value3], -1)
-    near, whole = key_state(kv3, key_feature_matrix)
-    states, kv_prev = look_back(n, near, whole, kv3[:, rows_here - SOFTMAX_SPAN :], 3)
+    block_seconds = jnp.concatenate(
+        [
+            jnp.pad(query_adapter_up, ((0, 0), (0, 2 * kv_wide))),
+            jnp.pad(key_adapter_up, ((0, 0), (wide, kv_wide))),
+            jnp.pad(value_adapter_up, ((0, 0), (wide + kv_wide, 0))),
+        ],
+        0,
+    )
+    qkv_g, out_g, cot_blocks, normed, inner, query_half, kv3, states, kv_prev = opening(
+        n,
+        [qkv_own, output_weight],
+        cotangent,
+        tok2,
+        attention_norm_gain.reshape(1, width),
+        downs,
+        block_seconds,
+        key_feature_matrix,
+        wide,
+        1,
+    )
+    qkv_w = qkv_g.reshape(width, -1)
     kv_ext = jnp.concatenate([kv_prev, kv3], 1)
     attn16, qfeats, inv_weights = attend(query_half, kv_ext, states, query_feature_matrix, key_feature_matrix)
     resid, normed_mlp, inner_output = branch(
@@ -1330,12 +1381,11 @@
     mlp_gain_term = jnp.sum(mlp_gain_rows, 0)
     du_o = dot_t(dresid16, output_adapter_up)
     oup_term = t_dot(inner_output.astype(b16), dresid16)
-    odown_term = t_dot(du_o.astype(b16), attn16)
-    dattn = dot_t(du_o.astype(b16), output_adapter_down)
-    step = output_weight.shape[1]
-    for i in range(n):
-        dattn = dattn + dot_t(dresid16[:, i * step : (i + 1) * step], out_g[i])
-    grad1, dstates, dtotals = state_back(attn16, dattn.astype(b16), inv_weights, qfeats)
+    du_o16 = du_o.astype(b16)
+    odown_term = t_dot(du_o16, attn16)
+    grad1, dstates, dtotals = state_back(
+        attn16, dresid16, out_g, du_o16, output_adapter_down, inv_weights, qfeats
+    )
     dtotals = jnp.pad(dtotals[:, :, ::8].reshape(-1, 128), ((0, 8), (0, 0)))
     dstates = jnp.concatenate([dstates, dtotals], 0)
     later = [from_behind(dstates, "seq", -i) for i in range(1, n)]
@@ -1347,15 +1397,6 @@
     lower_in2 = swap_chip((out_part[1, cut:].astype(f32) + lower_in[0].astype(f32)).astype(b16), 1)
     later = functools.reduce(jnp.add, [a.astype(f32) for a in later])
     dk_ext, dv_ext, dkmaps = key_back(kv_ext, later, key_feature_matrix, dk_ext, dv_ext, dkfeats)
-    dk_ext, upper_in2, lower_in2 = lax.optimization_barrier((dk_ext, upper_in2, lower_in2))
-    mlp_out = out_part[3].astype(f32) + jnp.concatenate(
-        [
-            upper_in[1].astype(f32) + upper_in2.astype(f32),
-            lower_in[1].astype(f32) + lower_in2.astype(f32),
-        ],
-        0,
-    )
-    output = both_halves((resid + mlp_out).astype(b16)).reshape(seq_count, rows_here, width)
     dkv_ext = jnp.concatenate([dk_ext, dv_ext], -1)
     back = from_behind(dkv_ext[:, :SOFTMAX_SPAN].astype(b16), "seq", -1).astype(f32)
     dkv = dkv_ext[:, SOFTMAX_SPAN:]
@@ -1376,6 +1417,18 @@
     up_terms = [
         t_dot(inner16[:, i * rank : (i + 1) * rank], dqkv16[:, a:b]) for i, (a, b) in enumerate(bounds)
     ]
+    inputs = tok2.astype(f32)
+    gain_attn = attention_norm_gain.astype(f32)
+    rms_attn = lax.rsqrt(jnp.mean(inputs * inputs, -1, keepdims=True) + epsilon)
+    dnormed, upper_in2, lower_in2 = lax.optimization_barrier((dnormed, upper_in2, lower_in2))
+    mlp_out = out_part[3].astype(f32) + jnp.concatenate(
+        [
+            upper_in[1].astype(f32) + upper_in2.astype(f32),
+            lower_in[1].astype(f32) + lower_in2.astype(f32),
+        ],
+        0,
+    )
+    output = both_halves((resid + mlp_out).astype(b16)).reshape(seq_count, rows_here, width)
     dnormed = dnormed.astype(f32) + swap_core(dnormed).astype(f32)
     attn_gain_term = jnp.sum(my_half(dnormed * inputs * rms_attn), 0)
     tokens_grad = (dresid16.astype(f32) + norm_back(inputs, rms_attn, gain_attn, dnormed)).reshape(

time: 508 us -> 476 us (0.937)
  Pallas kernels: 386 us -> 376 us
  matrix products: 22.8 us -> 14.8 us
    pallas_call x1, Pallas kernels: 130 us -> 114 us  [feed(): pl.pallas_call(functools.partial(feed_kernel, n, k, early), out_shape=[ja...]
    dot_general x5 -> x0, matrix products: 5.17 us -> none  [dot(): return jnp.dot(left, right, preferred_element_type=f32)]
    dot_general x11 -> x6, matrix products: 13.4 us -> 11.3 us  [dot_t(): lax.dot_general(left, right, (((1,), (1,)), ((), ())), preferred_element_...]
    unnamed x146 -> x115, local copies, waits for them, and re-layouts: 16.2 us -> 14.4 us
    pallas_call x3 -> x1, Pallas kernels: 174 us -> 174 us  [opening(): pl.pallas_call(functools.partial(opening_kernel, n, k), out_shape=[jax.Sh...]
  transfers between devices with their start and end apart: 11 -> 11, of which waited for: 3 -> 1; matrix products, arithmetic and copies ran while one was open for 6% -> 5% of each run, Pallas kernels for 46% -> 46%
where the time goes in v5:
time: 476 us; the launch traced here: 469 us
  Pallas kernels  376 us (79%)
  local copies, waits for them, and re-layouts  26.8 us (6%)
  other arithmetic  21 us (4%)
  between operations  15.2 us (3%)
  matrix products  14.8 us (3%)
  starting transfers between devices  10.2 us (2%)
  waiting for transfers between devices  4.87 us (1%)
    pallas_call x1, Pallas kernels, opening(): pl.pallas_call(functools.partial(opening_kernel, n, k), out_shape=[jax.Sh...  174 us
    pallas_call x1, Pallas kernels, feed(): pl.pallas_call(functools.partial(feed_kernel, n, k, early), out_shape=[ja...  114 us
    pallas_call x1, Pallas kernels, plane_total(): pl.pallas_call(functools.partial(plane_total_kernel, n, shared), out_shap...  26.3 us
    pallas_call x1, Pallas kernels, attend_back(): pl.pallas_call(attend_back_kernel, grid=(2, 2), out_shape=[jax.ShapeDtype...  19.8 us
    unnamed x115, local copies, waits for them, and re-layouts  14.4 us
    pallas_call x1, Pallas kernels, attend(): pl.pallas_call(attend_kernel, grid=(2, 2), out_shape=[jax.ShapeDtypeStruc...  13.3 us
    pallas_call x1, Pallas kernels, state_back(): pl.pallas_call(state_back_kernel, grid=(2, 2), out_shape=[jax.ShapeDtypeS...  12.5 us
    dot_general x6, matrix products, dot_t(): lax.dot_general(left, right, (((1,), (1,)), ((), ())), preferred_element_...  11.3 us
  transfers between devices with their start and end apart: 11, of which 1 were waited for; matrix products, arithmetic and copies ran while one was open for 5% of the time, Pallas kernels for 46%

profile of v5, /device:TPU:0, one launch (start us, length us, event | category | flops | bytes accessed | tf_op | source)
XLA Modules:
  0.0 469.0 jit_solution(17451402465165730789)
XLA Ops:
  7.2 1.5 constant_dynamic-slice_fusion.4
  10.2 1.7 pad_maximum_fusion
  14.4 1.4 pad_maximum_fusion.2.refs_0_
  15.8 174.4 %opening.1 = (bf16[4,512,1536]{2,1,0:T(8,128)(2,1)}, bf16[4,1024,512]{2,1,0:T(8,128)(2,1)}, bf16[4,256,2048]{2,1,0:T(8,128)(2,1)}, bf16[512,2048]{1,0:T(8,128)(2...) custom-call(bf16[512,1536]{1,0:T(8,128)(2,1)S(1)} %pad_maximum_fusio, ...), custom_call_target="tpu_custom_call" | custom-call | tf_op jit(solution)/shard_map/opening/pallas_call | solution.py:296
  194.3 13.3 %attend.1 = (bf16[512,1024]{1,0:T(8,128)(2,1)S(1)}, bf16[2,2,2,2,512,128]{5,4,3,2,1,0:T(8,128)(2,1)S(1)}, f32[2,512,8]{2,1,0:T(8,128)S(1)}) custom-call(bf16[512,1024]{1,0:T(8,128)(2,1)S(1)} %copy-done.6, bf16[2,320,512]{2,1,0:T(8,128)(2,1)S(1)} %constant_dynamic-update-slice_fusion.3.k.v, bf16[2,320,512]{2,1,0:T(8,128)(2,1)S(1)} %constant_dynamic-update-slice_fusion.3.k.v, ...), custom_call_target="tpu_custom_call" | custom-call | tf_op jit(solution)/shard_map/attend/pallas_call | solution.py:574
  207.6 1.3 copy-done.19
  209.7 8.5 %branch.1 = (f32[256,2048]{1,0:T(8,128)S(1)}, bf16[256,2048]{1,0:T(8,128)(2,1)S(1)}, f32[512,8]{1,0:T(8,128)S(1)}) custom-call(bf16[512,1024]{1,0:T(8,128)(2,1)S(1)} %get-tuple-element.56.attn, bf16[4,1024,512]{2,1,0:T(8,128)(2,1)} %get-tuple-element.57.weight, bf16[1024,8]{1,0:T(8,128)(2,1)S(1)} %copy-done.9, bf16[8,2048]{1,0:T(8,128)(2,1)S(1)} %copy-done.18, ...), custom_call_target="tpu_custom_call" | custom-call | tf_op jit(solution)/shard_map/branch/pallas_call | solution.py:1227
  218.3 1.3 copy-done
  221.3 2.6 bitcast_convert_fusion.1
  223.9 114.1 %feed.1 = (f32[8,2048]{1,0:T(8,128)}, bf16[2,256,2048]{2,1,0:T(8,128)(2,1)}, bf16[4,256,2048]{2,1,0:T(8,128)(2,1)}) custom-call(bf16[256,2048]{1,0:T(8,128)(2,1)} %copy-done.8, bf16[4,256,2048]{2,1,0:T(8,128)(2,1)} %get-tuple-element.60.ct_all, bf16[4,3,1536,256]{3,2,1,0:T(8,128)(2,1)} %bitcast.62, bf16[512,4096]{1,0:T(8,128)(2,1)} %gate.1, ...), custom_call_target="tpu_custom_call" | custom-call | tf_op jit(solution)/shard_map/feed/pallas_call | solution.py:1153
  338.0 2.9 convolution_convert_fusion.du
  340.9 12.5 %state_back.1 = (bf16[2,2,2,2,512,128]{5,4,3,2,1,0:T(8,128)(2,1)}, bf16[512,128]{1,0:T(8,128)(2,1)}, bf16[2,2,16,128]{3,2,1,0:T(8,128)(2,1)}) custom-call(bf16[512,1024]{1,0:T(8,128)(2,1)} %copy-done.2, bf16[512,2048]{1,0:T(8,128)(2,1)} %bitcast.64, bf16[4,1024,512]{2,1,0:T(8,128)(2,1)} %get-tuple-element.57.weight, ...), custom_call_target="tpu_custom_call" | custom-call | flops 8000000000 | bytes 1000000 | tf_op jit(solution)/shard_map/state_back/pallas_call | solution.py:632
  354.2 1.8 fusion.35
  356.1 1.5 collective-permute-start.3
  358.2 1.3 collective-permute-start
  359.5 1.3 collective-permute-start.1
  360.8 1.5 collective-permute-start.2
  362.4 1.6 copy-done.22
  364.0 19.8 %attend_back.1 = (bf16[512,1024]{1,0:T(8,128)(2,1)S(1)}, f32[2,320,256]{2,1,0:T(8,128)S(1)}, f32[2,320,256]{2,1,0:T(8,128)S(1)}, f32[2,4,320,128]{3,2,1,0:T(8,128)S(1)}, f32[16,64,64]{2,1,0:T(8,128)S(1)}) custom-call(bf16[512,1024]{1,0:T(8,128)(2,1)S(1)} %copy-done.7, bf16[2,320,512]{2,1,0:T(8,128)(2,1)S(1)} %constant_dynamic-update-slice_fusion.3.k.v, ...), custom_call_target="tpu_custom_call" | custom-call | flops 8000000000 | bytes 10000000 | tf_op jit(solution)/shard_map/attend_back/pallas_call | solution.py:732
  384.3 7.2 %key_back.1 = (f32[2,320,256]{2,1,0:T(8,128)S(1)}, f32[2,320,256]{2,1,0:T(8,128)S(1)}, f32[4,64,64]{2,1,0:T(8,128)S(1)}) custom-call(bf16[2,320,512]{2,1,0:T(8,128)(2,1)S(1)} %constant_dynamic-update-slice_fusion.3.k.v, bf16[2,320,512]{2,1,0:T(8,128)(2,1)S(1)} %constant_dynamic-update-slice_fusion.3.k.v, f32[528,128]{1,0:T(8,128)S(1)} %convert_add_fusion.3.later.tot, ...), custom_call_target="tpu_custom_call" | custom-call | tf_op jit(solution)/shard_map/key_back/pallas_call | solution.py:798
  391.9 1.8 collective-permute-start.5
  394.2 1.4 collective-permute-start.6
  396.7 4.8 %collective-permute-done.5 = bf16[2,64,512]{2,1,0:T(8,128)(2,1)S(1)} collective-permute-done((bf16[2,64,512]{2,1,0:T(8,128)(2,1)S(1)}, bf16[2,64,512]{2,1,0:T(8,128)(2,1)S(1)}, u32[]{:S(2)}, u32[]{:S(2)}) %collective-permute-start.5) | collective-permute-done | bytes 131104 | tf_op jit(solution)/shard_map/ppermute | solution.py:1269
  401.8 5.6 %fusion.4 = f32[512,2048]{1,0:T(8,128)S(1)} fusion(bf16[2048,1536]{1,0:T(8,128)(2,1)} %bitcast.79, bf16[512,512]{1,0:T(8,128)(2,1)S(1)} %bitcast.69, bf16[512,1024]{1,0:T(8,128)(2,1)S(1)} %get-tuple-element.70), kind=kOutput, calls=%fused_computation.14 | convolution fusion | flops 3224371200 | bytes 12058624 | tf_op jit(solution)/shard_map/dot_general | solution.py:1253
  407.6 2.1 add_convert_fusion
  411.2 1.5 fusion.3
  414.1 2.0 fusion.31
  416.6 1.7 broadcast_select_fusion.1
  418.3 1.5 pad_maximum_fusion.1
  420.7 3.4 multiply_reduce_fusion
  424.1 4.8 %convert_add_fusion = (f32[512,2048]{1,0:T(8,128)S(1)}, f32[512,2048]{1,0:T(8,128)}) fusion(bf16[512,2048]{1,0:T(8,128)(2,1)} %collective-permute-done.9, bf16[512,2048]{1,0:T(8,128)(2,1)} %add_convert_fusion, f32[512]{0:T(512)S(1)} %broadcast_multiply_fusion, f32[512]{0:T(512)S(1)} %multiply_multiply_fusion, bf16[2,256,2048]{2,1,0:T(8,128)(2,1)S(1)} %copy-done.25, ...), kind=kLoop, calls=%fused_computation.2 | loop fusion | flops 11534336 | bytes 16791552 | tf_op jit(solution)/shard_map/add | solution.py:1432
  429.3 26.3 %plane_total.1 = bf16[4,352,128]{2,1,0:T(8,128)(2,1)S(1)} custom-call(f32[1408,128]{1,0:T(8,128)S(1)} %pad.24.part), custom_call_target="tpu_custom_call" | custom-call | tf_op jit(solution)/shard_map/plane_total/pallas_call | solution.py:400
  (192 shorter events, 25.4 us)
Async XLA Ops:
  7.2 216.7 %all-gather.3.cloned.1.call-start = ((), (), s32[]{:S(2)}) async-start(), calls=%async_computation | async-start | bytes 11796480 | tf_op jit(solution)/shard_map/all_gather | solution.py:1309
  11.9 1.9 copy-start.23
  13.8 195.9 %copy-start.17 = (bf16[1,2048]{1,0:T(2,128)(2,1)}, bf16[1,2048]{1,0:T(2,128)(2,1)S(1)}, u32[]{:S(2)}) copy-start(bf16[1,2048]{1,0:T(2,128)(2,1)S(1)} %reshape.164.gain) | copy-start | bytes 12292
  192.0 17.7 %copy-start.9 = (bf16[1024,8]{1,0:T(8,128)(2,1)S(1)}, bf16[1024,8]{1,0:T(8,128)(2,1)}, u32[]{:S(2)}) copy-start(bf16[1024,8]{1,0:T(8,128)(2,1)} %copy.42.first.down) | copy-start | bytes 49156
  192.0 17.7 %copy-start.18 = (bf16[8,2048]{1,0:T(8,128)(2,1)S(1)}, bf16[8,2048]{1,0:T(8,128)(2,1)}, u32[]{:S(2)}) copy-start(bf16[8,2048]{1,0:T(8,128)(2,1)} %second.1) | copy-start | bytes 98308
  209.7 8.6 %copy-start.2 = (bf16[512,1024]{1,0:T(8,128)(2,1)}, bf16[512,1024]{1,0:T(8,128)(2,1)S(1)}, u32[]{:S(2)}) copy-start(bf16[512,1024]{1,0:T(8,128)(2,1)S(1)} %get-tuple-element.56.attn) | copy-start | bytes 3145732
  209.7 11.6 %copy-start.24 = (bf16[2,256,2048]{2,1,0:T(8,128)(2,1)S(1)}, bf16[2,256,2048]{2,1,0:T(8,128)(2,1)}, u32[]{:S(2)}) copy-start(bf16[2,256,2048]{2,1,0:T(8,128)(2,1)} %param.21) | copy-start | bytes 6291460
  354.2 4.0 copy-start.36
  354.2 8.1 %copy-start.7 = (bf16[512,1024]{1,0:T(8,128)(2,1)S(1)}, bf16[512,1024]{1,0:T(8,128)(2,1)}, u32[]{:S(2)}) copy-start(bf16[512,1024]{1,0:T(8,128)(2,1)} %copy-done.5) | copy-start | bytes 3145732
  354.2 8.1 %copy-start.12 = (bf16[4,64,64]{2,1,0:T(8,128)(2,1)S(1)}, bf16[4,64,64]{2,1,0:T(8,128)(2,1)}, u32[]{:S(2)}) copy-start(bf16[4,64,64]{2,1,0:T(8,128)(2,1)} %kmaps.5) | copy-start | bytes 98308
  354.2 8.1 %copy-start.14 = (bf16[16,64,64]{2,1,0:T(8,128)(2,1)S(1)}, bf16[16,64,64]{2,1,0:T(8,128)(2,1)}, u32[]{:S(2)}) copy-start(bf16[16,64,64]{2,1,0:T(8,128)(2,1)} %qmaps.3) | copy-start | bytes 393220
  354.2 8.1 %copy-start.20 = (bf16[2,2,2,2,512,128]{5,4,3,2,1,0:T(8,128)(2,1)S(1)}, bf16[2,2,2,2,512,128]{5,4,3,2,1,0:T(8,128)(2,1)}, u32[]{:S(2)}) copy-start(bf16[2,2,2,2,512,128]{5,4,3,2,1,0:T(8,128)(2,1)} %copy-done.19) | copy-start | bytes 6291460
  356.1 28.2 %collective-permute-start.3 = (bf16[2,128,2048]{2,1,0:T(8,128)(2,1)S(1)}, bf16[2,128,2048]{2,1,0:T(8,128)(2,1)S(1)}, u32[]{:S(2)}, u32[]{:S(2)}) collective-permute-start(bf16[2,128,2048]{2,1,0:T(8,128)(2,1)S(1)} %get-tuple-element.95), channel_id=1, source_target_pairs={{0,1},{1,0},{2,3},{3,2},{4,5},{5,4},{6,7},{7,6},{8,9},{9,8},{10,11... | collective-permute-start | bytes 3145736 | tf_op jit(solution)/shard_map/ppermute | solution.py:1374
  357.6 26.7 %collective-permute-start.4 = (bf16[2,128,2048]{2,1,0:T(8,128)(2,1)S(1)}, bf16[2,128,2048]{2,1,0:T(8,128)(2,1)S(1)}, u32[]{:S(2)}, u32[]{:S(2)}) collective-permute-start(bf16[2,128,2048]{2,1,0:T(8,128)(2,1)S(1)} %get-tuple-element.94), channel_id=1, source_target_pairs={{0,2},{1,3},{2,0},{3,1},{4,6},{5,7},{6,4},{7,5},{8,10},{9,11},{10,... | collective-permute-start | bytes 3145736 | tf_op jit(solution)/shard_map/ppermute | solution.py:1374
  358.2 26.0 %collective-permute-start = (bf16[528,128]{1,0:T(8,128)(2,1)S(1)}, bf16[528,128]{1,0:T(8,128)(2,1)S(1)}, u32[]{:S(2)}, u32[]{:S(2)}) collective-permute-start(bf16[528,128]{1,0:T(8,128)(2,1)S(1)} %fusion.22), channel_id=1, source_target_pairs={{8,0},{16,8},{24,16},{9,1},{17,9},{25,17},{10,2},{18,10},{26,18},{... | collective-permute-start | bytes 405512 | tf_op jit(solution)/shard_map/ppermute | solution.py:1269
  359.5 24.7 %collective-permute-start.1 = (bf16[528,128]{1,0:T(8,128)(2,1)S(1)}, bf16[528,128]{1,0:T(8,128)(2,1)S(1)}, u32[]{:S(2)}, u32[]{:S(2)}) collective-permute-start(bf16[528,128]{1,0:T(8,128)(2,1)S(1)} %fusion.22), channel_id=1, source_target_pairs={{16,0},{24,8},{17,1},{25,9},{18,2},{26,10},{19,3},{27,11},{20,4},{... | collective-permute-start | bytes 405512 | tf_op jit(solution)/shard_map/ppermute | solution.py:1269
  360.8 23.4 %collective-permute-start.2 = (bf16[528,128]{1,0:T(8,128)(2,1)S(1)}, bf16[528,128]{1,0:T(8,128)(2,1)S(1)}, u32[]{:S(2)}, u32[]{:S(2)}) collective-permute-start(bf16[528,128]{1,0:T(8,128)(2,1)S(1)} %fusion.22), channel_id=1, source_target_pairs={{24,0},{25,1},{26,2},{27,3},{28,4},{29,5},{30,6},{31,7}} | collective-permute-start | bytes 405512 | tf_op jit(solution)/shard_map/ppermute | solution.py:1269
  364.0 19.8 %copy-start.16 = (f32[512,8]{1,0:T(8,128)S(1)}, f32[512,8]{1,0:T(8,128)}, u32[]{:S(2)}) copy-start(f32[512,8]{1,0:T(8,128)} %copy-done.15) | copy-start | bytes 49156
  364.0 19.8 %copy-start.27 = (bf16[2,256,2048]{2,1,0:T(8,128)(2,1)S(1)}, bf16[2,256,2048]{2,1,0:T(8,128)(2,1)}, u32[]{:S(2)}) copy-start(bf16[2,256,2048]{2,1,0:T(8,128)(2,1)} %get-tuple-element.63) | copy-start | bytes 6291460
  391.6 2.2 copy-start.29
  391.8 4.5 copy-start.38
  391.9 9.6 %collective-permute-start.5 = (bf16[2,64,512]{2,1,0:T(8,128)(2,1)S(1)}, bf16[2,64,512]{2,1,0:T(8,128)(2,1)S(1)}, u32[]{:S(2)}, u32[]{:S(2)}) collective-permute-start(bf16[2,64,512]{2,1,0:T(8,128)(2,1)S(1)} %slice.181), channel_id=1, source_target_pairs={{8,0},{16,8},{24,16},{9,1},{17,9},{25,17},{10,2},{18,10},{26,18},{... | collective-permute-start | bytes 393224 | tf_op jit(solution)/shard_map/ppermute | solution.py:1269
  394.2 7.4 %copy-start.47 = (bf16[8,256]{1,0:T(8,128)(2,1)S(1)}, bf16[8,256]{1,0:T(8,128)(2,1)}, u32[]{:S(2)}) copy-start(bf16[8,256]{1,0:T(8,128)(2,1)} %param.37) | copy-start | bytes 12292
  394.2 15.4 %collective-permute-start.6 = (bf16[128,2048]{1,0:T(8,128)(2,1)S(1)}, bf16[128,2048]{1,0:T(8,128)(2,1)S(1)}, u32[]{:S(2)}, u32[]{:S(2)}) collective-permute-start(bf16[128,2048]{1,0:T(8,128)(2,1)S(1)} %get-tuple-element.93), channel_id=1, source_target_pairs={{0,2},{1,3},{2,0},{3,1},{4,6},{5,7},{6,4},{7,5},{8,10},{9,11},{10,... | collective-permute-start | bytes 1572872 | tf_op jit(solution)/shard_map/ppermute | solution.py:1374
  395.7 14.0 %collective-permute-start.7 = (bf16[128,2048]{1,0:T(8,128)(2,1)S(1)}, bf16[128,2048]{1,0:T(8,128)(2,1)S(1)}, u32[]{:S(2)}, u32[]{:S(2)}) collective-permute-start(bf16[128,2048]{1,0:T(8,128)(2,1)S(1)} %get-tuple-element.92), channel_id=1, source_target_pairs={{0,1},{1,0},{2,3},{3,2},{4,5},{5,4},{6,7},{7,6},{8,9},{9,8},{10,11... | collective-permute-start | bytes 1572872 | tf_op jit(solution)/shard_map/ppermute | solution.py:1374
  401.8 5.6 %copy-start.49 = (bf16[8,256]{1,0:T(8,128)(2,1)S(1)}, bf16[8,256]{1,0:T(8,128)(2,1)}, u32[]{:S(2)}) copy-start(bf16[8,256]{1,0:T(8,128)(2,1)} %param.35) | copy-start | bytes 12292
  401.8 5.8 %copy-start.32 = (bf16[2048,24]{0,1:T(8,128)(2,1)S(1)}, bf16[2048,24]{0,1:T(8,128)(2,1)}, u32[]{:S(2)}) copy-start(bf16[2048,24]{0,1:T(8,128)(2,1)} %copy-done.31) | copy-start | bytes 294916
  409.7 10.2 %collective-permute-start.9 = (bf16[512,2048]{1,0:T(8,128)(2,1)}, bf16[512,2048]{1,0:T(8,128)(2,1)}, u32[]{:S(2)}, u32[]{:S(2)}) collective-permute-start(bf16[512,2048]{1,0:T(8,128)(2,1)} %add_convert_fusion), channel_id=1, source_target_pairs={{0,4},{4,0},{1,5},{5,1},{2,6},{6,2},{3,7},{7,3},{8,12},{12,8},{9,1... | collective-permute-start | bytes 6291464 | tf_op jit(solution)/shard_map/ppermute | solution.py:1273
  412.7 3.9 collective-permute-start.8
  418.3 2.4 copy-start.25
  419.8 4.2 copy-start.28
  424.1 4.8 %copy-start.26 = (f32[512,2048]{1,0:T(8,128)S(1)}, f32[512,2048]{1,0:T(8,128)}, u32[]{:S(2)}) copy-start(f32[512,2048]{1,0:T(8,128)} %bitcast_convert_fusion.1) | copy-start | bytes 12582916
  (29 other events, 37.3 us)
Sparse Core Ops, SparseCore 0:
  12.0 205.5 all-gather.2

commit v6 on v5

--- a/solution.py
+++ b/solution.py
@@ -330,14 +330,66 @@
     )(*arrays, block, tok, gain, downs, seconds, kmaps)
 
 
-def plane_total_kernel(
-    n, shared, part, out, mine, core_in, near, line, c_send, c_recv, p_send, p_recv, z_send, z_recv, g_send, g_recv
+WIDE = 512
+
+
+def grad_total_kernel(
+    n,
+    down_terms,
+    oup_term,
+    attn_rows,
+    mlp_rows,
+    q_term,
+    k_term,
+    v_term,
+    odown_term,
+    dqm,
+    dkm,
+    gains_out,
+    downs_out,
+    oup_out,
+    ups_out,
+    odown_out,
+    qm_out,
+    km_out,
+    stage,
+    mine,
+    core_in,
+    near,
+    line,
+    whole,
+    c_send,
+    c_recv,
+    p_send,
+    p_recv,
+    z_send,
+    z_recv,
+    g_send,
+    g_recv,
 ):
     spot = Spot()
     s, m, d = spot.s, spot.m, spot.d
-    h = out.shape[1]
+    h = whole.shape[1]
     f32, b16 = jnp.float32, jnp.bfloat16
-    mine[...] = part[...].astype(b16)
+    blocks = down_terms.shape[1] // WIDE
+    shared = core_in.shape[0]
+    stage[...] = jnp.zeros_like(stage)
+    for b in range(blocks):
+        at = slice(b * WIDE, (b + 1) * WIDE)
+        stage[b * 24 : b * 24 + 24] = down_terms[:, at]
+        stage[96 + b * 8 : 104 + b * 8] = oup_term[:, at]
+    stage[144:152] = q_term[:, :WIDE]
+    stage[152:160] = q_term[:, WIDE:]
+    stage[160:168] = jnp.concatenate([k_term[...], v_term[...]], 1)
+    stage[168:176] = odown_term[:, :WIDE]
+    stage[176:184] = odown_term[:, WIDE:]
+    for i in range(2):
+        stage[192 + 64 * i : 256 + 64 * i] = jnp.concatenate([dqm[i * 8 + h] for h in range(8)], 1)
+    km = jnp.concatenate([dkm[h] for h in range(4)], 1)
+    stage[320:352] = jnp.concatenate([km[:32], km[32:]], 1)
+    gains = [jnp.sum(v[...], 0, keepdims=True) for v in (attn_rows, mlp_rows)]
+    stage[128:136] = jnp.concatenate([v[:, b * WIDE : (b + 1) * WIDE] for v in gains for b in range(blocks)], 0)
+    mine[...] = stage[...].astype(b16)
     bar = pltpu.get_barrier_semaphore()
     plane = [{"seq": s, "mp": m, "dp": (d + i) % 4} for i in range(1, 4)]
     lines = [{"seq": (s + i) % n, "mp": m, "dp": d} for i in range(1, n)]
@@ -374,16 +426,34 @@
     total = line[0].astype(f32)
     for i in range(1, n):
         total = total + line[i].astype(f32)
-    out[d] = total.astype(b16)
+    whole[d] = total.astype(b16)
 
     def back(i, sending):
         who = d if sending else (d - i) % 4
-        return remote(out.at[who], out.at[who], g_send.at[i - 1], g_recv.at[i - 1], plane[i - 1])
+        return remote(whole.at[who], whole.at[who], g_send.at[i - 1], g_recv.at[i - 1], plane[i - 1])
 
     for i in (2, 1, 3):
         back(i, True).start()
     for i in range(1, 4):
         back(i, False).wait_recv()
+    for i in range(4):
+        stage[i * h : (i + 1) * h] = whole[i].astype(f32)
+    for b in range(blocks):
+        at = slice(b * WIDE, (b + 1) * WIDE)
+        downs_out[:, at] = stage[b * 24 : b * 24 + 24]
+        oup_out[:, at] = stage[96 + b * 8 : 104 + b * 8]
+    gains_out[...] = stage[128:136]
+    ups_out[:, :WIDE] = stage[144:152]
+    ups_out[:, WIDE : 2 * WIDE] = stage[152:160]
+    ups_out[:, 2 * WIDE :] = stage[160:168]
+    odown_out[:, :WIDE] = stage[168:176]
+    odown_out[:, WIDE:] = stage[176:184]
+    for i in range(2):
+        for h2 in range(8):
+            qm_out[i * 8 + h2] = stage[192 + 64 * i : 256 + 64 * i, h2 * 64 : h2 * 64 + 64]
+    for h2 in range(4):
+        km_out[h2, :32] = stage[320:352, h2 * 64 : h2 * 64 + 64]
+        km_out[h2, 32:] = stage[320:352, 256 + h2 * 64 : 320 + h2 * 64]
     for i in range(1, 4):
         scatter(i).wait_send()
         back(i, True).wait_send()
@@ -391,22 +461,26 @@
         along(i, True).wait_send()
 
 
-def plane_total(n, part, shared, cid):
-    DMA = pltpu.SemaphoreType.DMA
-    V = pltpu.VMEM
-    b = jnp.bfloat16
-    rows, w = part.shape
+def grad_total(n, args, cid):
+    DMA, V = pltpu.SemaphoreType.DMA, pltpu.VMEM
+    b, f32 = jnp.bfloat16, jnp.float32
+    width, wide, kv_wide = args[0].shape[1], args[4].shape[1], args[5].shape[1]
+    rows, shared = 384, 144
     h = rows // 4
+    vmem = pl.BlockSpec(memory_space=pltpu.VMEM)
+    shapes = [(8, WIDE), (24, width), (8, width), (8, wide + 2 * kv_wide), (8, wide), (16, 64, 64), (4, 64, 64)]
     return pl.pallas_call(
-        functools.partial(plane_total_kernel, n, shared),
-        out_shape=jax.ShapeDtypeStruct((4, h, w), b),
-        in_specs=[pl.BlockSpec(memory_space=pltpu.VMEM)],
-        out_specs=pl.BlockSpec(memory_space=pltpu.VMEM),
+        functools.partial(grad_total_kernel, n),
+        out_shape=[jax.ShapeDtypeStruct(shape, f32) for shape in shapes],
+        in_specs=[vmem] * len(args),
+        out_specs=[vmem] * len(shapes),
         scratch_shapes=[
-            V((rows, w), b),
-            V((shared, w), b),
-            V((3, h, w), b),
-            V((n, h, w), b),
+            V((rows, WIDE), f32),
+            V((rows, WIDE), b),
+            V((shared, WIDE), b),
+            V((3, h, WIDE), b),
+            V((n, h, WIDE), b),
+            V((4, h, WIDE), b),
             DMA,
             DMA,
             DMA((3,)),
@@ -418,7 +492,7 @@
         ],
         compiler_params=pltpu.CompilerParams(collective_id=cid, has_side_effects=True, vmem_limit_bytes=40 << 20),
         name="plane_total",
-    )(part)
+    )(*args)
 
 
 SPAN, TILE = 64, 128
@@ -819,6 +893,41 @@
     )(kv_ext, kv_ext, later, later, kmaps, dk, dv, dkf)
 
 
+def norm_close_kernel(part, other, tok, dres, gain, out, sums):
+    f32 = jnp.float32
+    i, m = pl.program_id(0), lax.axis_index("mp")
+    dn = part[...].astype(f32) + other[...].astype(f32)
+    x = tok[...].astype(f32)
+    inv = lax.rsqrt(jnp.mean(x * x, -1, keepdims=True) + epsilon)
+    xi = x * inv
+    t = dn * xi
+    gain_wide = gain[...].astype(f32)
+    out[...] = dres[...].astype(f32) + inv * (gain_wide * dn - xi * jnp.mean(gain_wide * t, -1, keepdims=True))
+
+    @pl.when(i == 0)
+    def _():
+        sums[...] = jnp.zeros_like(sums)
+
+    @pl.when(i // (pl.num_programs(0) // 2) == m)
+    def _():
+        sums[...] += jnp.sum(t.reshape(t.shape[0] // 8, 8, -1), 0)
+
+
+def norm_close(part, other, tok, dres, gain):
+    rows, width = tok.shape
+    step = 128
+    piece = pl.BlockSpec((step, width), lambda i: (i, 0))
+    return pl.pallas_call(
+        norm_close_kernel,
+        grid=(rows // step,),
+        out_shape=[jax.ShapeDtypeStruct((rows, width), jnp.float32), jax.ShapeDtypeStruct((8, width), jnp.float32)],
+        in_specs=[piece] * 4 + [pl.BlockSpec((1, width), lambda i: (0, 0))],
+        out_specs=[piece, pl.BlockSpec((8, width), lambda i: (0, 0))],
+        compiler_params=pltpu.CompilerParams(vmem_limit_bytes=40 << 20),
+        name="norm_close",
+    )(part, other, tok, dres, gain)
+
+
 CHUNKS = 4
 
 
@@ -1378,7 +1487,6 @@
     lower_in = swap_chip(out_part[0::2, cut:], 2)
 
 
-    mlp_gain_term = jnp.sum(mlp_gain_rows, 0)
     du_o = dot_t(dresid16, output_adapter_up)
     oup_term = t_dot(inner_output.astype(b16), dresid16)
     du_o16 = du_o.astype(b16)
@@ -1417,9 +1525,6 @@
     up_terms = [
         t_dot(inner16[:, i * rank : (i + 1) * rank], dqkv16[:, a:b]) for i, (a, b) in enumerate(bounds)
     ]
-    inputs = tok2.astype(f32)
-    gain_attn = attention_norm_gain.astype(f32)
-    rms_attn = lax.rsqrt(jnp.mean(inputs * inputs, -1, keepdims=True) + epsilon)
     dnormed, upper_in2, lower_in2 = lax.optimization_barrier((dnormed, upper_in2, lower_in2))
     mlp_out = out_part[3].astype(f32) + jnp.concatenate(
         [
@@ -1429,25 +1534,18 @@
         0,
     )
     output = both_halves((resid + mlp_out).astype(b16)).reshape(seq_count, rows_here, width)
-    dnormed = dnormed.astype(f32) + swap_core(dnormed).astype(f32)
-    attn_gain_term = jnp.sum(my_half(dnormed * inputs * rms_attn), 0)
-    tokens_grad = (dresid16.astype(f32) + norm_back(inputs, rms_attn, gain_attn, dnormed)).reshape(
-        seq_count, rows_here, width
-    )
-
-    shared = [attn_gain_term, mlp_gain_term, down_terms, oup_term]
-    split = up_terms + [odown_term, dqmaps, dkmaps]
-    flat = [a.reshape(-1, 128) for a in shared + split]
-    sizes = [a.shape[0] for a in flat]
-    shared_rows = sum(sizes[:4])
-    flat = jnp.concatenate(flat, 0)
-    flat = jnp.pad(flat, ((0, -flat.shape[0] % 128), (0, 0)))
-    summed = plane_total(n, flat, shared_rows, 8).reshape(-1, 128).astype(f32)
-    parts, at = [], 0
-    for term, size in zip(shared + split, sizes):
-        parts.append(summed[at : at + size].reshape(term.shape))
-        at += size
-    attn_gain, mlp_gain, downs_g, oup, qup, kup, vup, odown, qmaps_g, kmaps_g = parts
+    tokens_grad, attn_gain_rows = norm_close(
+        dnormed, swap_core(dnormed), tok2, dresid16, attention_norm_gain.reshape(1, width)
+    )
+    tokens_grad = tokens_grad.reshape(seq_count, rows_here, width)
+    gains, downs_g, oup, ups, odown, qmaps_g, kmaps_g = grad_total(
+        n,
+        (down_terms, oup_term, attn_gain_rows, mlp_gain_rows, *up_terms, odown_term, dqmaps, dkmaps),
+        8,
+    )
+    gains = gains.reshape(2, width)
+    attn_gain, mlp_gain = gains[0], gains[1]
+    qup, kup, vup = ups[:, :wide], ups[:, wide : wide + kv_wide], ups[:, wide + kv_wide :]
     downs_g = downs_g.T
     return (
         output,
@@ -1462,7 +1560,7 @@
         vup,
         odown.T,
         oup,
-        qmaps_g.reshape(query_feature_matrix.shape),
+        qmaps_g,
         kmaps_g,
     )
 

time: 476 us -> 463 us (0.973); the launches traced: 469 us -> 463 us
  other arithmetic: 21 us -> 5.57 us
  Pallas kernels: 376 us -> 387 us
  waiting for transfers between devices: 4.87 us -> 9.71 us
    pallas_call x1 -> x2, Pallas kernels: 26.3 us -> 34.1 us  [the longest x1 29.7 us: grad_total(): pl.pallas_call(functools.partial(grad_total_kernel, n), out_shape=[jax.Sh...]
    pallas_call x1, Pallas kernels: 114 us -> 119 us  [feed(): pl.pallas_call(functools.partial(feed_kernel, n, k, early), out_shape=[ja...]
    reshape x16 -> x0, local copies, waits for them, and re-layouts: 5.14 us -> none  [the longest x8 4.82 us: per_device(): parts.append(summed[at:at + size].reshape(term.shape))]
    add x1 -> x0, other arithmetic: 4.76 us -> none  [per_device(): dnormed = dnormed.astype(f32) + swap_core(dnormed).astype(f32)]
    unnamed x115 -> x102, local copies, waits for them, and re-layouts: 14.4 us -> 15.5 us
  transfers between devices with their start and end apart: 11 -> 11, of which waited for: 1 -> 3; matrix products, arithmetic and copies ran while one was open for 5% -> 3% of each run, Pallas kernels for 46% -> 46%
where the time goes in v6:
time: 463 us
  Pallas kernels  387 us (84%)
  local copies, waits for them, and re-layouts  23.2 us (5%)
  between operations  14.8 us (3%)
  matrix products  11.9 us (3%)
  starting transfers between devices  10.4 us (2%)
  waiting for transfers between devices  9.71 us (2%)
  other arithmetic  5.57 us (1%)
    pallas_call x1, Pallas kernels, opening(): pl.pallas_call(functools.partial(opening_kernel, n, k), out_shape=[jax.Sh...  172 us
    pallas_call x1, Pallas kernels, feed(): pl.pallas_call(functools.partial(feed_kernel, n, k, early), out_shape=[ja...  119 us
    pallas_call x1, Pallas kernels, grad_total(): pl.pallas_call(functools.partial(grad_total_kernel, n), out_shape=[jax.Sh...  29.7 us
    pallas_call x1, Pallas kernels, attend_back(): pl.pallas_call(attend_back_kernel, grid=(2, 2), out_shape=[jax.ShapeDtype...  19.9 us
    unnamed x102, local copies, waits for them, and re-layouts  15.5 us
    pallas_call x1, Pallas kernels, attend(): pl.pallas_call(attend_kernel, grid=(2, 2), out_shape=[jax.ShapeDtypeStruc...  13.4 us
    pallas_call x1, Pallas kernels, state_back(): pl.pallas_call(state_back_kernel, grid=(2, 2), out_shape=[jax.ShapeDtypeS...  12.5 us
    dot_general x6, matrix products, dot_t(): lax.dot_general(left, right, (((1,), (1,)), ((), ())), preferred_element_...  10 us
  transfers between devices with their start and end apart: 11, of which 3 were waited for; matrix products, arithmetic and copies ran while one was open for 3% of the time, Pallas kernels for 46%

profile of v6, /device:TPU:0, one launch (start us, length us, event | category | flops | bytes accessed | tf_op | source)
XLA Modules:
  0.0 462.6 jit_solution(9704131720507025581)
XLA Ops:
  7.2 1.3 constant_dynamic-slice_fusion.3
  8.5 1.5 constant_dynamic-slice_fusion.4
  10.2 1.7 pad_maximum_fusion
  12.6 0.8 copy.42.first.down
  14.7 172.1 %opening.1 = (bf16[4,512,1536]{2,1,0:T(8,128)(2,1)}, bf16[4,1024,512]{2,1,0:T(8,128)(2,1)}, bf16[4,256,2048]{2,1,0:T(8,128)(2,1)}, bf16[512,2048]{1,0:T(8,128)(2...) custom-call(bf16[512,1536]{1,0:T(8,128)(2,1)S(1)} %pad_maximum_fusio, ...), custom_call_target="tpu_custom_call" | custom-call | tf_op jit(solution)/shard_map/opening/pallas_call | solution.py:296
  187.6 13.4 %attend.1 = (bf16[512,1024]{1,0:T(8,128)(2,1)S(1)}, bf16[2,2,2,2,512,128]{5,4,3,2,1,0:T(8,128)(2,1)S(1)}, f32[2,512,8]{2,1,0:T(8,128)S(1)}) custom-call(bf16[512,1024]{1,0:T(8,128)(2,1)S(1)} %get-tuple-element.61.q, bf16[2,320,512]{2,1,0:T(8,128)(2,1)S(1)} %constant_dynamic-update-slice_fusion.3.k.v, ...), custom_call_target="tpu_custom_call" | custom-call | tf_op jit(solution)/shard_map/attend/pallas_call | solution.py:648
  201.0 1.3 copy-done.21
  203.1 8.5 %branch.1 = (f32[256,2048]{1,0:T(8,128)S(1)}, bf16[256,2048]{1,0:T(8,128)(2,1)S(1)}, f32[512,8]{1,0:T(8,128)S(1)}) custom-call(bf16[512,1024]{1,0:T(8,128)(2,1)S(1)} %get-tuple-element.65.attn, bf16[4,1024,512]{2,1,0:T(8,128)(2,1)} %get-tuple-element.66.weight, bf16[1024,8]{1,0:T(8,128)(2,1)S(1)} %copy-done.10, bf16[8,2048]{1,0:T(8,128)(2,1)S(1)} %copy-done.20, ...), custom_call_target="tpu_custom_call" | custom-call | tf_op jit(solution)/shard_map/branch/pallas_call | solution.py:1336
  211.7 1.3 copy-done.2
  213.0 1.0 copy-done.9
  214.7 1.9 all-gather.3.cloned.1.call-done
  216.5 119.3 %feed.1 = (f32[8,2048]{1,0:T(8,128)}, bf16[2,256,2048]{2,1,0:T(8,128)(2,1)}, bf16[4,256,2048]{2,1,0:T(8,128)(2,1)}) custom-call(bf16[256,2048]{1,0:T(8,128)(2,1)} %copy-done.9, bf16[4,256,2048]{2,1,0:T(8,128)(2,1)} %get-tuple-element.69.ct_all, bf16[4,3,1536,256]{3,2,1,0:T(8,128)(2,1)} %bitcast.57, bf16[512,4096]{1,0:T(8,128)(2,1)} %gate.1, ...), custom_call_target="tpu_custom_call" | custom-call | tf_op jit(solution)/shard_map/feed/pallas_call | solution.py:1262
  335.9 2.9 convolution_convert_fusion.du
  338.8 12.5 %state_back.1 = (bf16[2,2,2,2,512,128]{5,4,3,2,1,0:T(8,128)(2,1)}, bf16[512,128]{1,0:T(8,128)(2,1)}, bf16[2,2,16,128]{3,2,1,0:T(8,128)(2,1)}) custom-call(bf16[512,1024]{1,0:T(8,128)(2,1)} %copy-done.4, bf16[512,2048]{1,0:T(8,128)(2,1)} %bitcast.52, bf16[4,1024,512]{2,1,0:T(8,128)(2,1)} %get-tuple-element.66.weight, ...), custom_call_target="tpu_custom_call" | custom-call | flops 8000000000 | bytes 1000000 | tf_op jit(solution)/shard_map/state_back/pallas_call | solution.py:706
  352.2 1.8 fusion.33
  354.0 1.6 collective-permute-start.4
  356.1 1.3 collective-permute-start.2
  357.4 1.3 collective-permute-start.1
  358.7 1.6 collective-permute-start
  360.3 1.6 copy-done.24
  361.9 19.9 %attend_back.1 = (bf16[512,1024]{1,0:T(8,128)(2,1)S(1)}, f32[2,320,256]{2,1,0:T(8,128)S(1)}, f32[2,320,256]{2,1,0:T(8,128)S(1)}, f32[2,4,320,128]{3,2,1,0:T(8,128)S(1)}, f32[16,64,64]{2,1,0:T(8,128)S(1)}) custom-call(bf16[512,1024]{1,0:T(8,128)(2,1)S(1)} %copy-done.8, bf16[2,320,512]{2,1,0:T(8,128)(2,1)S(1)} %constant_dynamic-update-slice_fusion.3.k.v, ...), custom_call_target="tpu_custom_call" | custom-call | flops 8000000000 | bytes 10000000 | tf_op jit(solution)/shard_map/attend_back/pallas_call | solution.py:806
  382.4 7.2 %key_back.1 = (f32[2,320,256]{2,1,0:T(8,128)S(1)}, f32[2,320,256]{2,1,0:T(8,128)S(1)}, f32[4,64,64]{2,1,0:T(8,128)S(1)}) custom-call(bf16[2,320,512]{2,1,0:T(8,128)(2,1)S(1)} %constant_dynamic-update-slice_fusion.3.k.v, bf16[2,320,512]{2,1,0:T(8,128)(2,1)S(1)} %constant_dynamic-update-slice_fusion.3.k.v, f32[528,128]{1,0:T(8,128)S(1)} %convert_add_fusion.2.later.tot, ...), custom_call_target="tpu_custom_call" | custom-call | tf_op jit(solution)/shard_map/key_back/pallas_call | solution.py:872
  389.9 1.9 collective-permute-start.5
  392.2 1.6 collective-permute-start.7
  394.7 5.8 %collective-permute-done.5 = bf16[2,64,512]{2,1,0:T(8,128)(2,1)S(1)} collective-permute-done((bf16[2,64,512]{2,1,0:T(8,128)(2,1)S(1)}, bf16[2,64,512]{2,1,0:T(8,128)(2,1)S(1)}, u32[]{:S(2)}, u32[]{:S(2)}) %collective-permute-start.5) | collective-permute-done | bytes 131104 | tf_op jit(solution)/shard_map/ppermute | solution.py:1378
  400.8 5.6 %fusion.2 = f32[512,2048]{1,0:T(8,128)S(1)} fusion(bf16[2048,1536]{1,0:T(8,128)(2,1)} %bitcast.67, bf16[512,512]{1,0:T(8,128)(2,1)S(1)} %bitcast.60, bf16[512,1024]{1,0:T(8,128)(2,1)S(1)} %get-tuple-element.79), kind=kOutput, calls=%fused_computation.7 | convolution fusion | flops 3224371200 | bytes 12058624 | tf_op jit(solution)/shard_map/dot_general | solution.py:1362
  407.8 1.2 copy-done.3
  411.4 2.0 collective-permute-done.8
  413.6 1.5 pad_maximum_fusion.1
  415.0 0.9 copy-done
  415.9 4.4 norm_close.1
  420.3 29.7 %plane_total.1 = (f32[8,512]{1,0:T(8,128)S(1)}, f32[24,2048]{1,0:T(8,128)S(1)}, f32[8,2048]{1,0:T(8,128)S(1)}, f32[8,1536]{1,0:T(8,128)S(1)}, f32[8,1024]{1,0:T(...) custom-call(f32[24,2048]{1,0:T(8,128)S(1)} %fusion.29.down_terms, f32[8,2048]{1,0:T(8,128)S(1)} %fusion.25.oup_term, ...), custom_call_target="tpu_custom_call" | custom-call | tf_op jit(solution)/shard_map/plane_total/pallas_call | solution.py:472
  (147 shorter events, 17.7 us)
Async XLA Ops:
  7.2 209.3 %all-gather.3.cloned.1.call-start = ((), (), s32[]{:S(2)}) async-start(), calls=%async_computation | async-start | bytes 11796480 | tf_op jit(solution)/shard_map/all_gather | solution.py:1418
  12.6 190.5 %copy-start.18 = (bf16[1,2048]{1,0:T(2,128)(2,1)}, bf16[1,2048]{1,0:T(2,128)(2,1)S(1)}, u32[]{:S(2)}) copy-start(bf16[1,2048]{1,0:T(2,128)(2,1)S(1)} %reshape.77.gain) | copy-start | bytes 12292
  13.5 173.3 %copy-start.29 = (bf16[2048,24]{0,1:T(8,128)(2,1)}, bf16[2048,24]{0,1:T(8,128)(2,1)S(1)}, u32[]{:S(2)}) copy-start(bf16[2048,24]{0,1:T(8,128)(2,1)S(1)} %constant_dynamic-update-slice_fusion) | copy-start | bytes 294916
  14.7 172.9 %copy-start.12 = (bf16[4,64,64]{2,1,0:T(8,128)(2,1)S(1)}, bf16[4,64,64]{2,1,0:T(8,128)(2,1)}, u32[]{:S(2)}) copy-start(bf16[4,64,64]{2,1,0:T(8,128)(2,1)} %kmaps.5) | copy-start | bytes 98308
  14.7 172.9 %copy-start.14 = (bf16[16,64,64]{2,1,0:T(8,128)(2,1)S(1)}, bf16[16,64,64]{2,1,0:T(8,128)(2,1)}, u32[]{:S(2)}) copy-start(bf16[16,64,64]{2,1,0:T(8,128)(2,1)} %qmaps.3) | copy-start | bytes 393220
  186.8 14.2 %copy-start.7 = (bf16[512,1024]{1,0:T(8,128)(2,1)}, bf16[512,1024]{1,0:T(8,128)(2,1)S(1)}, u32[]{:S(2)}) copy-start(bf16[512,1024]{1,0:T(8,128)(2,1)S(1)} %get-tuple-element.61.q) | copy-start | bytes 3145732
  187.5 15.6 %copy-start.10 = (bf16[1024,8]{1,0:T(8,128)(2,1)S(1)}, bf16[1024,8]{1,0:T(8,128)(2,1)}, u32[]{:S(2)}) copy-start(bf16[1024,8]{1,0:T(8,128)(2,1)} %copy.42.first.down) | copy-start | bytes 49156
  187.5 15.6 %copy-start.20 = (bf16[8,2048]{1,0:T(8,128)(2,1)S(1)}, bf16[8,2048]{1,0:T(8,128)(2,1)}, u32[]{:S(2)}) copy-start(bf16[8,2048]{1,0:T(8,128)(2,1)} %second.1) | copy-start | bytes 98308
  203.1 8.5 %copy-start.4 = (bf16[512,1024]{1,0:T(8,128)(2,1)}, bf16[512,1024]{1,0:T(8,128)(2,1)S(1)}, u32[]{:S(2)}) copy-start(bf16[512,1024]{1,0:T(8,128)(2,1)S(1)} %get-tuple-element.65.attn) | copy-start | bytes 3145732
  352.1 4.0 copy-start.34
  352.1 8.2 %copy-start.8 = (bf16[512,1024]{1,0:T(8,128)(2,1)S(1)}, bf16[512,1024]{1,0:T(8,128)(2,1)}, u32[]{:S(2)}) copy-start(bf16[512,1024]{1,0:T(8,128)(2,1)} %copy-done.7) | copy-start | bytes 3145732
  352.1 8.2 %copy-start.13 = (bf16[4,64,64]{2,1,0:T(8,128)(2,1)S(1)}, bf16[4,64,64]{2,1,0:T(8,128)(2,1)}, u32[]{:S(2)}) copy-start(bf16[4,64,64]{2,1,0:T(8,128)(2,1)} %kmaps.5) | copy-start | bytes 98308
  352.1 8.2 %copy-start.15 = (bf16[16,64,64]{2,1,0:T(8,128)(2,1)S(1)}, bf16[16,64,64]{2,1,0:T(8,128)(2,1)}, u32[]{:S(2)}) copy-start(bf16[16,64,64]{2,1,0:T(8,128)(2,1)} %qmaps.3) | copy-start | bytes 393220
  352.1 8.2 %copy-start.22 = (bf16[2,2,2,2,512,128]{5,4,3,2,1,0:T(8,128)(2,1)S(1)}, bf16[2,2,2,2,512,128]{5,4,3,2,1,0:T(8,128)(2,1)}, u32[]{:S(2)}) copy-start(bf16[2,2,2,2,512,128]{5,4,3,2,1,0:T(8,128)(2,1)} %copy-done.21) | copy-start | bytes 6291460
  354.0 28.3 %collective-permute-start.4 = (bf16[2,128,2048]{2,1,0:T(8,128)(2,1)S(1)}, bf16[2,128,2048]{2,1,0:T(8,128)(2,1)S(1)}, u32[]{:S(2)}, u32[]{:S(2)}) collective-permute-start(bf16[2,128,2048]{2,1,0:T(8,128)(2,1)S(1)} %get-tuple-element.110), channel_id=1, source_target_pairs={{0,2},{1,3},{2,0},{3,1},{4,6},{5,7},{6,4},{7,5},{8,10},{9,11},{10,... | collective-permute-start | bytes 3145736 | tf_op jit(solution)/shard_map/ppermute | solution.py:1483
  355.6 26.8 %collective-permute-start.3 = (bf16[2,128,2048]{2,1,0:T(8,128)(2,1)S(1)}, bf16[2,128,2048]{2,1,0:T(8,128)(2,1)S(1)}, u32[]{:S(2)}, u32[]{:S(2)}) collective-permute-start(bf16[2,128,2048]{2,1,0:T(8,128)(2,1)S(1)} %get-tuple-element.111), channel_id=1, source_target_pairs={{0,1},{1,0},{2,3},{3,2},{4,5},{5,4},{6,7},{7,6},{8,9},{9,8},{10,11... | collective-permute-start | bytes 3145736 | tf_op jit(solution)/shard_map/ppermute | solution.py:1483
  356.1 26.2 %collective-permute-start.2 = (bf16[528,128]{1,0:T(8,128)(2,1)S(1)}, bf16[528,128]{1,0:T(8,128)(2,1)S(1)}, u32[]{:S(2)}, u32[]{:S(2)}) collective-permute-start(bf16[528,128]{1,0:T(8,128)(2,1)S(1)} %fusion.20), channel_id=1, source_target_pairs={{24,0},{25,1},{26,2},{27,3},{28,4},{29,5},{30,6},{31,7}} | collective-permute-start | bytes 405512 | tf_op jit(solution)/shard_map/ppermute | solution.py:1378
  357.4 24.9 %collective-permute-start.1 = (bf16[528,128]{1,0:T(8,128)(2,1)S(1)}, bf16[528,128]{1,0:T(8,128)(2,1)S(1)}, u32[]{:S(2)}, u32[]{:S(2)}) collective-permute-start(bf16[528,128]{1,0:T(8,128)(2,1)S(1)} %fusion.20), channel_id=1, source_target_pairs={{16,0},{24,8},{17,1},{25,9},{18,2},{26,10},{19,3},{27,11},{20,4},{... | collective-permute-start | bytes 405512 | tf_op jit(solution)/shard_map/ppermute | solution.py:1378
  358.7 23.6 %collective-permute-start = (bf16[528,128]{1,0:T(8,128)(2,1)S(1)}, bf16[528,128]{1,0:T(8,128)(2,1)S(1)}, u32[]{:S(2)}, u32[]{:S(2)}) collective-permute-start(bf16[528,128]{1,0:T(8,128)(2,1)S(1)} %fusion.20), channel_id=1, source_target_pairs={{8,0},{16,8},{24,16},{9,1},{17,9},{25,17},{10,2},{18,10},{26,18},{... | collective-permute-start | bytes 405512 | tf_op jit(solution)/shard_map/ppermute | solution.py:1378
  361.9 19.9 %copy-start.1 = (bf16[2,256,2048]{2,1,0:T(8,128)(2,1)S(1)}, bf16[2,256,2048]{2,1,0:T(8,128)(2,1)}, u32[]{:S(2)}) copy-start(bf16[2,256,2048]{2,1,0:T(8,128)(2,1)} %get-tuple-element.72) | copy-start | bytes 6291460
  361.9 20.0 %copy-start.17 = (f32[512,8]{1,0:T(8,128)S(1)}, f32[512,8]{1,0:T(8,128)}, u32[]{:S(2)}) copy-start(f32[512,8]{1,0:T(8,128)} %copy-done.16) | copy-start | bytes 49156
  389.7 2.2 copy-start.25
  389.9 4.5 copy-start.36
  389.9 10.6 %collective-permute-start.5 = (bf16[2,64,512]{2,1,0:T(8,128)(2,1)S(1)}, bf16[2,64,512]{2,1,0:T(8,128)(2,1)S(1)}, u32[]{:S(2)}, u32[]{:S(2)}) collective-permute-start(bf16[2,64,512]{2,1,0:T(8,128)(2,1)S(1)} %slice.163), channel_id=1, source_target_pairs={{8,0},{16,8},{24,16},{9,1},{17,9},{25,17},{10,2},{18,10},{26,18},{... | collective-permute-start | bytes 393224 | tf_op jit(solution)/shard_map/ppermute | solution.py:1378
  392.2 15.1 %collective-permute-start.7 = (bf16[128,2048]{1,0:T(8,128)(2,1)S(1)}, bf16[128,2048]{1,0:T(8,128)(2,1)S(1)}, u32[]{:S(2)}, u32[]{:S(2)}) collective-permute-start(bf16[128,2048]{1,0:T(8,128)(2,1)S(1)} %get-tuple-element.108), channel_id=1, source_target_pairs={{0,1},{1,0},{2,3},{3,2},{4,5},{5,4},{6,7},{7,6},{8,9},{9,8},{10,11... | collective-permute-start | bytes 1572872 | tf_op jit(solution)/shard_map/ppermute | solution.py:1483
  393.8 13.6 %collective-permute-start.6 = (bf16[128,2048]{1,0:T(8,128)(2,1)S(1)}, bf16[128,2048]{1,0:T(8,128)(2,1)S(1)}, u32[]{:S(2)}, u32[]{:S(2)}) collective-permute-start(bf16[128,2048]{1,0:T(8,128)(2,1)S(1)} %get-tuple-element.109), channel_id=1, source_target_pairs={{0,2},{1,3},{2,0},{3,1},{4,6},{5,7},{6,4},{7,5},{8,10},{9,11},{10,... | collective-permute-start | bytes 1572872 | tf_op jit(solution)/shard_map/ppermute | solution.py:1483
  400.8 5.8 %copy-start.30 = (bf16[2048,24]{0,1:T(8,128)(2,1)S(1)}, bf16[2048,24]{0,1:T(8,128)(2,1)}, u32[]{:S(2)}) copy-start(bf16[2048,24]{0,1:T(8,128)(2,1)} %copy-done.29) | copy-start | bytes 294916
  407.7 2.2 copy-start.26
  407.7 7.3 %collective-permute-start.9 = (bf16[512,2048]{1,0:T(8,128)(2,1)S(1)}, bf16[512,2048]{1,0:T(8,128)(2,1)S(1)}, u32[]{:S(2)}, u32[]{:S(2)}) collective-permute-start(bf16[512,2048]{1,0:T(8,128)(2,1)S(1)} %add_convert_fusion.part), channel_id=1, source_target_pairs={{0,4},{4,0},{1,5},{5,1},{2,6},{6,2},{3,7},{7,3},{8,12},{12,8},{9,1... | collective-permute-start | bytes 6291464 | tf_op jit(solution)/shard_map/ppermute | solution.py:1382
  409.5 3.9 collective-permute-start.8
  413.5 2.4 copy-start
  415.0 5.2 %copy-start.19 = (f32[8,2048]{1,0:T(8,128)S(1)}, f32[8,2048]{1,0:T(8,128)}, u32[]{:S(2)}) copy-start(f32[8,2048]{1,0:T(8,128)} %get-tuple-element.97.mlp_rows) | copy-start | bytes 196612
  (24 other events, 34.5 us)
Sparse Core Ops, SparseCore 0:
  12.1 204.3 all-gather.2

commit v7 on v6

--- a/solution.py
+++ b/solution.py
@@ -397,18 +397,29 @@
         pl.semaphore_signal(bar, inc=1, device_id=where, device_id_type=MESH)
     pl.semaphore_wait(bar, n + 3)
     core = remote(mine.at[pl.ds(0, shared)], core_in, c_send, c_recv, spot.to("c"))
+    def rows(who):
+        return pl.ds(pl.multiple_of(who * h, h), h)
+
+    def scatter(i):
+        return remote(mine.at[rows((d + i) % 4)], near.at[i - 1], p_send.at[i - 1], p_recv.at[i - 1], plane[i - 1])
+
+    free = -(-shared // h)
     core.start()
+    for i in (2, 1, 3):
+
+        @pl.when((d + i) % 4 >= free)
+        def _():
+            scatter(i).start()
+
     core.wait()
     mine[:shared] = (mine[:shared].astype(f32) + core_in[...].astype(f32)).astype(b16)
 
-    def rows(who):
-        return pl.ds(pl.multiple_of(who * h, h), h)
-
-    def scatter(i):
-        return remote(mine.at[rows((d + i) % 4)], near.at[i - 1], p_send.at[i - 1], p_recv.at[i - 1], plane[i - 1])
-
     for i in (2, 1, 3):
-        scatter(i).start()
+
+        @pl.when((d + i) % 4 < free)
+        def _():
+            scatter(i).start()
+
     total = mine[rows(d)].astype(f32)
     for i in range(1, 4):
         scatter(i).wait_recv()
@@ -931,7 +942,7 @@
 CHUNKS = 4
 
 
-def feed_kernel(n, k, early, xn_own, ct_all, packed, gate, up, down, res, gain, gsum, dres16, out_part, *scratch):
+def feed_kernel(n, k, early, xn_own, ct_all, packed, gate, up, down, res, gain, gsum, dres16, up_go, low_go, up_keep, low_keep, *scratch):
     (xn, ct, gw, uw, dw, da, oa, xin, yin, t2, xin2, yin2) = scratch[:12]
     (o_sem, a_send, a_recv, w_sem, w_send, w_recv, z_sem, z_send, z_recv, c_send, c_recv, p_send, p_recv, st_sem, e_sem) = scratch[12:]
     spot = Spot()
@@ -1073,7 +1084,11 @@
         remote(xn.at[1, A], xin.at[0], p_send.at[2], p_recv.at[2], spot.to("x")),
         remote(xn.at[2, B], yin.at[0], p_send.at[3], p_recv.at[3], spot.to("y")),
     )
-    stores = [pltpu.make_async_copy(ct.at[i], out_part.at[i], st_sem.at[i]) for i in range(4)]
+    places = ((up_go.at[0], low_go.at[0]), (up_go.at[1], low_keep.at[0]), (up_keep.at[0], low_go.at[1]), (up_keep.at[1], low_keep.at[1]))
+    stores = [
+        [pltpu.make_async_copy(ct.at[i, rows], places[i][j], st_sem.at[i, j]) for j, rows in enumerate((A, B))]
+        for i in range(4)
+    ]
 
     again = (
         pltpu.make_async_copy(res, da.at[0], e_sem.at[0]),
@@ -1169,7 +1184,8 @@
 
             @pl.when(step == steps - 4 + i)
             def _():
-                stores[i].start()
+                for store in stores[i]:
+                    store.start()
                 if i == 1:
                     again[0].start()
                 if i == 0:
@@ -1182,7 +1198,8 @@
         remote(t2.at[0], yin2, p_send.at[4], p_recv.at[4], spot.to("y")),
         remote(t2.at[1], xin2, p_send.at[5], p_recv.at[5], spot.to("x")),
     )
-    stores[0].wait()
+    for store in stores[0]:
+        store.wait()
     again[1].start()
     first[0].wait_recv()
     t2[0] = (xn[2, A].astype(f32) + xin[1].astype(f32)).astype(b16)
@@ -1223,8 +1240,9 @@
     keep.wait()
     swap.wait_send()
     remote(xn.at[0], dres16.at[1 - m], e_sem.at[2], e_sem.at[3], spot.to("c")).wait_recv()
-    for c in stores[1:]:
-        c.wait()
+    for pair in stores[1:]:
+        for store in pair:
+            store.wait()
     for c in second:
         c.wait_send()
     for q in range(early):
@@ -1258,16 +1276,16 @@
     scratch += [DMA((2,)), DMA((4,)), DMA((4,))]
     scratch += [DMA((max(early, 1), pieces))] * 3
     scratch += [DMA((late, 3)), DMA((late, 3, 2, n - 1)), DMA((late, 3, 2, n - 1)), DMA((late, 3, n)), DMA((late, 3, n))]
-    scratch += [DMA((6,)), DMA((6,)), DMA((4,)), DMA((5,))]
+    scratch += [DMA((6,)), DMA((6,)), DMA((4, 2)), DMA((5,))]
     return pl.pallas_call(
         functools.partial(feed_kernel, n, k, early),
         out_shape=[
             jax.ShapeDtypeStruct((8, w), f32),
             jax.ShapeDtypeStruct((2, r, w), b),
-            jax.ShapeDtypeStruct((4, r, w), b),
+            *[jax.ShapeDtypeStruct((2, r // 2, w), b)] * 4,
         ],
         in_specs=[pl.BlockSpec(memory_space=ANY)] * 7 + [pl.BlockSpec(memory_space=pltpu.VMEM)],
-        out_specs=[pl.BlockSpec(memory_space=pltpu.VMEM)] + [pl.BlockSpec(memory_space=ANY)] * 2,
+        out_specs=[pl.BlockSpec(memory_space=pltpu.VMEM)] + [pl.BlockSpec(memory_space=ANY)] * 5,
         scratch_shapes=scratch,
         compiler_params=pltpu.CompilerParams(collective_id=cid, has_side_effects=True, vmem_limit_bytes=62 << 20),
         name="feed",
@@ -1464,7 +1482,7 @@
         feedforward_norm_gain.reshape(1, width),
         5,
     )
-    mlp_gain_rows, dresid16, out_part = feed(
+    mlp_gain_rows, dresid16, up_go, low_go, up_keep, low_keep = feed(
         n,
         EARLY,
         normed_mlp,
@@ -1482,9 +1500,8 @@
     def swap_chip(value, bit):
         return lax.ppermute(value, "dp", [(i, i ^ bit) for i in range(4)])
 
-    cut = half // 2
-    upper_in = swap_chip(out_part[0:2, :cut], 1)
-    lower_in = swap_chip(out_part[0::2, cut:], 2)
+    upper_in = swap_chip(up_go, 1)
+    lower_in = swap_chip(low_go, 2)
 
 
     du_o = dot_t(dresid16, output_adapter_up)
@@ -1501,8 +1518,8 @@
         query_half, kv_ext, states, query_feature_matrix, key_feature_matrix, qfeats, grad1
     )
     dq16, later, upper_in, lower_in = lax.optimization_barrier((dq16, later, upper_in, lower_in))
-    upper_in2 = swap_chip((out_part[2, :cut].astype(f32) + upper_in[0].astype(f32)).astype(b16), 2)
-    lower_in2 = swap_chip((out_part[1, cut:].astype(f32) + lower_in[0].astype(f32)).astype(b16), 1)
+    upper_in2 = swap_chip((up_keep[0].astype(f32) + upper_in[0].astype(f32)).astype(b16), 2)
+    lower_in2 = swap_chip((low_keep[0].astype(f32) + lower_in[0].astype(f32)).astype(b16), 1)
     later = functools.reduce(jnp.add, [a.astype(f32) for a in later])
     dk_ext, dv_ext, dkmaps = key_back(kv_ext, later, key_feature_matrix, dk_ext, dv_ext, dkfeats)
     dkv_ext = jnp.concatenate([dk_ext, dv_ext], -1)
@@ -1526,10 +1543,10 @@
         t_dot(inner16[:, i * rank : (i + 1) * rank], dqkv16[:, a:b]) for i, (a, b) in enumerate(bounds)
     ]
     dnormed, upper_in2, lower_in2 = lax.optimization_barrier((dnormed, upper_in2, lower_in2))
-    mlp_out = out_part[3].astype(f32) + jnp.concatenate(
+    mlp_out = jnp.concatenate(
         [
-            upper_in[1].astype(f32) + upper_in2.astype(f32),
-            lower_in[1].astype(f32) + lower_in2.astype(f32),
+            up_keep[1].astype(f32) + upper_in[1].astype(f32) + upper_in2.astype(f32),
+            low_keep[1].astype(f32) + lower_in[1].astype(f32) + lower_in2.astype(f32),
         ],
         0,
     )

time: 463 us -> 468 us (1.011); the launches traced: 463 us -> 461 us
    unnamed x102 -> x104, local copies, waits for them, and re-layouts: 15.5 us -> 17.8 us
where the time goes in v7:
time: 468 us; the launch traced here: 461 us
  Pallas kernels  384 us (82%)
  local copies, waits for them, and re-layouts  23.6 us (5%)
  between operations  15.1 us (3%)
  waiting for transfers between devices  12.1 us (3%)
  starting transfers between devices  10.1 us (2%)
  matrix products  9.72 us (2%)
  other arithmetic  6.58 us (1%)
    pallas_call x1, Pallas kernels, opening(): pl.pallas_call(functools.partial(opening_kernel, n, k), out_shape=[jax.Sh...  172 us
    pallas_call x1, Pallas kernels, feed(): pl.pallas_call(functools.partial(feed_kernel, n, k, early), out_shape=[ja...  119 us
    pallas_call x1, Pallas kernels, grad_total(): pl.pallas_call(functools.partial(grad_total_kernel, n), out_shape=[jax.Sh...  26.9 us
    pallas_call x1, Pallas kernels, attend_back(): pl.pallas_call(attend_back_kernel, grid=(2, 2), out_shape=[jax.ShapeDtype...  19.8 us
    unnamed x104, local copies, waits for them, and re-layouts  17.8 us
    pallas_call x1, Pallas kernels, attend(): pl.pallas_call(attend_kernel, grid=(2, 2), out_shape=[jax.ShapeDtypeStruc...  13.4 us
    pallas_call x1, Pallas kernels, state_back(): pl.pallas_call(state_back_kernel, grid=(2, 2), out_shape=[jax.ShapeDtypeS...  12.7 us
  transfers between devices with their start and end apart: 11, of which 3 were waited for; matrix products, arithmetic and copies ran while one was open for 3% of the time, Pallas kernels for 46%

profile of v7, /device:TPU:0, one launch (start us, length us, event | category | flops | bytes accessed | tf_op | source)
XLA Modules:
  0.0 461.4 jit_solution(14431614205997406901)
XLA Ops:
  7.2 1.3 constant_dynamic-slice_fusion.3
  8.5 1.5 constant_dynamic-slice_fusion.4
  10.2 1.7 pad_maximum_fusion
  14.7 172.1 %opening.1 = (bf16[4,512,1536]{2,1,0:T(8,128)(2,1)}, bf16[4,1024,512]{2,1,0:T(8,128)(2,1)}, bf16[4,256,2048]{2,1,0:T(8,128)(2,1)}, bf16[512,2048]{1,0:T(8,128)(2...) custom-call(bf16[512,1536]{1,0:T(8,128)(2,1)S(1)} %pad_maximum_fusio, ...), custom_call_target="tpu_custom_call" | custom-call | tf_op jit(solution)/shard_map/opening/pallas_call | solution.py:296
  187.6 13.4 %attend.1 = (bf16[512,1024]{1,0:T(8,128)(2,1)S(1)}, bf16[2,2,2,2,512,128]{5,4,3,2,1,0:T(8,128)(2,1)S(1)}, f32[2,512,8]{2,1,0:T(8,128)S(1)}) custom-call(bf16[512,1024]{1,0:T(8,128)(2,1)S(1)} %get-tuple-element.64.q, bf16[2,320,512]{2,1,0:T(8,128)(2,1)S(1)} %constant_dynamic-update-slice_fusion.3.k.v, ...), custom_call_target="tpu_custom_call" | custom-call | tf_op jit(solution)/shard_map/attend/pallas_call | solution.py:659
  201.1 1.3 copy-done.21
  203.2 8.5 %branch.1 = (f32[256,2048]{1,0:T(8,128)S(1)}, bf16[256,2048]{1,0:T(8,128)(2,1)S(1)}, f32[512,8]{1,0:T(8,128)S(1)}) custom-call(bf16[512,1024]{1,0:T(8,128)(2,1)S(1)} %get-tuple-element.68.attn, bf16[4,1024,512]{2,1,0:T(8,128)(2,1)} %get-tuple-element.69.weight, bf16[1024,8]{1,0:T(8,128)(2,1)S(1)} %copy-done.10, bf16[8,2048]{1,0:T(8,128)(2,1)S(1)} %copy-done.20, ...), custom_call_target="tpu_custom_call" | custom-call | tf_op jit(solution)/shard_map/branch/pallas_call | solution.py:1354
  211.7 1.3 copy-done.2
  213.0 1.0 copy-done.9
  214.7 1.8 all-gather.3.cloned.1.call-done
  216.5 119.4 %feed.1 = (f32[8,2048]{1,0:T(8,128)}, bf16[2,256,2048]{2,1,0:T(8,128)(2,1)}, bf16[2,128,2048]{2,1,0:T(8,128)(2,1)}, bf16[2,128,2048]{2,1,0:T(8,128)(2,1)}, bf16[...) custom-call(bf16[256,2048]{1,0:T(8,128)(2,1)} %copy-done.9, bf16[4,256,2048]{2,1,0:T(8,128)(2,1)} %get-tuple-element.72.ct_all, ...), custom_call_target="tpu_custom_call" | custom-call | tf_op jit(solution)/shard_map/feed/pallas_call | solution.py:1280
  335.9 2.9 convolution_convert_fusion.du
  338.9 12.7 %state_back.1 = (bf16[2,2,2,2,512,128]{5,4,3,2,1,0:T(8,128)(2,1)}, bf16[512,128]{1,0:T(8,128)(2,1)}, bf16[2,2,16,128]{3,2,1,0:T(8,128)(2,1)}) custom-call(bf16[512,1024]{1,0:T(8,128)(2,1)} %copy-done.4, bf16[512,2048]{1,0:T(8,128)(2,1)} %bitcast.47, bf16[4,1024,512]{2,1,0:T(8,128)(2,1)} %get-tuple-element.69.weight, ...), custom_call_target="tpu_custom_call" | custom-call | flops 8000000000 | bytes 1000000 | tf_op jit(solution)/shard_map/state_back/pallas_call | solution.py:717
  352.3 1.6 collective-permute-start.3
  354.4 0.9 fusion.19
  355.3 1.3 collective-permute-start.2
  356.6 1.3 collective-permute-start.1
  357.9 1.5 collective-permute-start
  359.4 1.6 copy-done.22
  361.0 1.6 copy-done.24
  362.6 19.8 %attend_back.1 = (bf16[512,1024]{1,0:T(8,128)(2,1)S(1)}, f32[2,320,256]{2,1,0:T(8,128)S(1)}, f32[2,320,256]{2,1,0:T(8,128)S(1)}, f32[2,4,320,128]{3,2,1,0:T(8,128)S(1)}, f32[16,64,64]{2,1,0:T(8,128)S(1)}) custom-call(bf16[512,1024]{1,0:T(8,128)(2,1)S(1)} %copy-done.8, bf16[2,320,512]{2,1,0:T(8,128)(2,1)S(1)} %constant_dynamic-update-slice_fusion.3.k.v, ...), custom_call_target="tpu_custom_call" | custom-call | flops 8000000000 | bytes 10000000 | tf_op jit(solution)/shard_map/attend_back/pallas_call | solution.py:817
  383.0 7.2 %key_back.1 = (f32[2,320,256]{2,1,0:T(8,128)S(1)}, f32[2,320,256]{2,1,0:T(8,128)S(1)}, f32[4,64,64]{2,1,0:T(8,128)S(1)}) custom-call(bf16[2,320,512]{2,1,0:T(8,128)(2,1)S(1)} %constant_dynamic-update-slice_fusion.3.k.v, bf16[2,320,512]{2,1,0:T(8,128)(2,1)S(1)} %constant_dynamic-update-slice_fusion.3.k.v, f32[528,128]{1,0:T(8,128)S(1)} %convert_add_fusion.later.tot, ...), custom_call_target="tpu_custom_call" | custom-call | tf_op jit(solution)/shard_map/key_back/pallas_call | solution.py:883
  390.5 1.0 copy-done.29
  391.6 1.6 collective-permute-start.7
  394.0 1.5 collective-permute-start.5
  395.9 7.9 %collective-permute-done.5 = bf16[2,64,512]{2,1,0:T(8,128)(2,1)S(1)} collective-permute-done((bf16[2,64,512]{2,1,0:T(8,128)(2,1)S(1)}, bf16[2,64,512]{2,1,0:T(8,128)(2,1)S(1)}, u32[]{:S(2)}, u32[]{:S(2)}) %collective-permute-start.5) | collective-permute-done | bytes 131104 | tf_op jit(solution)/shard_map/ppermute | solution.py:1396
  404.0 3.4 fusion.1
  409.0 1.0 copy-done.3
  412.3 2.3 collective-permute-done.8
  414.9 1.6 pad_maximum_fusion.1
  417.3 4.4 norm_close.1
  421.6 26.9 %plane_total.1 = (f32[8,512]{1,0:T(8,128)S(1)}, f32[24,2048]{1,0:T(8,128)S(1)}, f32[8,2048]{1,0:T(8,128)S(1)}, f32[8,1536]{1,0:T(8,128)S(1)}, f32[8,1024]{1,0:T(...) custom-call(f32[24,2048]{1,0:T(8,128)S(1)} %fusion.28.down_terms, f32[8,2048]{1,0:T(8,128)S(1)} %fusion.24.oup_term, ...), custom_call_target="tpu_custom_call" | custom-call | tf_op jit(solution)/shard_map/plane_total/pallas_call | solution.py:483
  (150 shorter events, 19.2 us)
Async XLA Ops:
  7.2 209.3 %all-gather.3.cloned.1.call-start = ((), (), s32[]{:S(2)}) async-start(), calls=%async_computation | async-start | bytes 11796480 | tf_op jit(solution)/shard_map/all_gather | solution.py:1436
  11.9 1.9 copy-start.27
  11.9 1.9 copy-start.32
  11.9 1.9 copy-start.33
  12.6 190.6 %copy-start.18 = (bf16[1,2048]{1,0:T(2,128)(2,1)}, bf16[1,2048]{1,0:T(2,128)(2,1)S(1)}, u32[]{:S(2)}) copy-start(bf16[1,2048]{1,0:T(2,128)(2,1)S(1)} %reshape.77.gain) | copy-start | bytes 12292
  14.7 172.9 %copy-start.12 = (bf16[4,64,64]{2,1,0:T(8,128)(2,1)S(1)}, bf16[4,64,64]{2,1,0:T(8,128)(2,1)}, u32[]{:S(2)}) copy-start(bf16[4,64,64]{2,1,0:T(8,128)(2,1)} %kmaps.5) | copy-start | bytes 98308
  14.7 172.9 %copy-start.14 = (bf16[16,64,64]{2,1,0:T(8,128)(2,1)S(1)}, bf16[16,64,64]{2,1,0:T(8,128)(2,1)}, u32[]{:S(2)}) copy-start(bf16[16,64,64]{2,1,0:T(8,128)(2,1)} %qmaps.3) | copy-start | bytes 393220
  186.8 14.2 %copy-start.7 = (bf16[512,1024]{1,0:T(8,128)(2,1)}, bf16[512,1024]{1,0:T(8,128)(2,1)S(1)}, u32[]{:S(2)}) copy-start(bf16[512,1024]{1,0:T(8,128)(2,1)S(1)} %get-tuple-element.64.q) | copy-start | bytes 3145732
  187.5 15.6 %copy-start.10 = (bf16[1024,8]{1,0:T(8,128)(2,1)S(1)}, bf16[1024,8]{1,0:T(8,128)(2,1)}, u32[]{:S(2)}) copy-start(bf16[1024,8]{1,0:T(8,128)(2,1)} %copy.42.first.down) | copy-start | bytes 49156
  187.6 15.6 %copy-start.20 = (bf16[8,2048]{1,0:T(8,128)(2,1)S(1)}, bf16[8,2048]{1,0:T(8,128)(2,1)}, u32[]{:S(2)}) copy-start(bf16[8,2048]{1,0:T(8,128)(2,1)} %second.1) | copy-start | bytes 98308
  203.2 8.5 %copy-start.4 = (bf16[512,1024]{1,0:T(8,128)(2,1)}, bf16[512,1024]{1,0:T(8,128)(2,1)S(1)}, u32[]{:S(2)}) copy-start(bf16[512,1024]{1,0:T(8,128)(2,1)S(1)} %get-tuple-element.68.attn) | copy-start | bytes 3145732
  338.9 20.6 %copy-start.8 = (bf16[512,1024]{1,0:T(8,128)(2,1)S(1)}, bf16[512,1024]{1,0:T(8,128)(2,1)}, u32[]{:S(2)}) copy-start(bf16[512,1024]{1,0:T(8,128)(2,1)} %copy-done.7) | copy-start | bytes 3145732
  338.9 20.6 %copy-start.13 = (bf16[4,64,64]{2,1,0:T(8,128)(2,1)S(1)}, bf16[4,64,64]{2,1,0:T(8,128)(2,1)}, u32[]{:S(2)}) copy-start(bf16[4,64,64]{2,1,0:T(8,128)(2,1)} %kmaps.5) | copy-start | bytes 98308
  338.9 20.6 %copy-start.15 = (bf16[16,64,64]{2,1,0:T(8,128)(2,1)S(1)}, bf16[16,64,64]{2,1,0:T(8,128)(2,1)}, u32[]{:S(2)}) copy-start(bf16[16,64,64]{2,1,0:T(8,128)(2,1)} %qmaps.3) | copy-start | bytes 393220
  352.3 30.6 %collective-permute-start.3 = (bf16[2,128,2048]{2,1,0:T(8,128)(2,1)}, bf16[2,128,2048]{2,1,0:T(8,128)(2,1)S(1)}, u32[]{:S(2)}, u32[]{:S(2)}) collective-permute-start(bf16[2,128,2048]{2,1,0:T(8,128)(2,1)} %get-tuple-element.81), channel_id=1, source_target_pairs={{0,1},{1,0},{2,3},{3,2},{4,5},{5,4},{6,7},{7,6},{8,9},{9,8},{10,11... | collective-permute-start | bytes 3145736 | tf_op jit(solution)/shard_map/ppermute | solution.py:1501
  353.9 29.0 %collective-permute-start.4 = (bf16[2,128,2048]{2,1,0:T(8,128)(2,1)}, bf16[2,128,2048]{2,1,0:T(8,128)(2,1)S(1)}, u32[]{:S(2)}, u32[]{:S(2)}) collective-permute-start(bf16[2,128,2048]{2,1,0:T(8,128)(2,1)} %get-tuple-element.82), channel_id=1, source_target_pairs={{0,2},{1,3},{2,0},{3,1},{4,6},{5,7},{6,4},{7,5},{8,10},{9,11},{10,... | collective-permute-start | bytes 3145736 | tf_op jit(solution)/shard_map/ppermute | solution.py:1501
  355.3 27.6 %collective-permute-start.2 = (bf16[528,128]{1,0:T(8,128)(2,1)S(1)}, bf16[528,128]{1,0:T(8,128)(2,1)S(1)}, u32[]{:S(2)}, u32[]{:S(2)}) collective-permute-start(bf16[528,128]{1,0:T(8,128)(2,1)S(1)} %fusion.19), channel_id=1, source_target_pairs={{24,0},{25,1},{26,2},{27,3},{28,4},{29,5},{30,6},{31,7}} | collective-permute-start | bytes 405512 | tf_op jit(solution)/shard_map/ppermute | solution.py:1396
  356.6 26.3 %collective-permute-start.1 = (bf16[528,128]{1,0:T(8,128)(2,1)S(1)}, bf16[528,128]{1,0:T(8,128)(2,1)S(1)}, u32[]{:S(2)}, u32[]{:S(2)}) collective-permute-start(bf16[528,128]{1,0:T(8,128)(2,1)S(1)} %fusion.19), channel_id=1, source_target_pairs={{16,0},{24,8},{17,1},{25,9},{18,2},{26,10},{19,3},{27,11},{20,4},{... | collective-permute-start | bytes 405512 | tf_op jit(solution)/shard_map/ppermute | solution.py:1396
  357.9 25.0 %collective-permute-start = (bf16[528,128]{1,0:T(8,128)(2,1)S(1)}, bf16[528,128]{1,0:T(8,128)(2,1)S(1)}, u32[]{:S(2)}, u32[]{:S(2)}) collective-permute-start(bf16[528,128]{1,0:T(8,128)(2,1)S(1)} %fusion.19), channel_id=1, source_target_pairs={{8,0},{16,8},{24,16},{9,1},{17,9},{25,17},{10,2},{18,10},{26,18},{... | collective-permute-start | bytes 405512 | tf_op jit(solution)/shard_map/ppermute | solution.py:1396
  362.6 19.8 %copy-start.1 = (bf16[2,256,2048]{2,1,0:T(8,128)(2,1)S(1)}, bf16[2,256,2048]{2,1,0:T(8,128)(2,1)}, u32[]{:S(2)}) copy-start(bf16[2,256,2048]{2,1,0:T(8,128)(2,1)} %get-tuple-element.75) | copy-start | bytes 6291460
  362.6 19.8 %copy-start.17 = (f32[512,8]{1,0:T(8,128)S(1)}, f32[512,8]{1,0:T(8,128)}, u32[]{:S(2)}) copy-start(f32[512,8]{1,0:T(8,128)} %copy-done.16) | copy-start | bytes 49156
  382.9 21.1 %slice-start = ((s8[6291456]{0:T(1024)(128)(4,1)}), s8[4194304]{0:T(1024)(128)(4,1)S(1)}, s32[]{:S(2)}) async-start(s8[6291456]{0:T(1024)(128)(4,1)} %bitcast.62), calls=%async_computation.1 | async-start | bytes 8388608
  390.4 2.9 copy-start.28
  390.4 13.6 %slice-start.1 = ((s8[6291456]{0:T(1024)(128)(4,1)}), s8[2097152]{0:T(1024)(128)(4,1)S(1)}, s32[]{:S(2)}) async-start(s8[6291456]{0:T(1024)(128)(4,1)} %bitcast.62), calls=%async_computation.2 | async-start | bytes 4194304
  391.6 16.8 %collective-permute-start.7 = (bf16[128,2048]{1,0:T(8,128)(2,1)S(1)}, bf16[128,2048]{1,0:T(8,128)(2,1)S(1)}, u32[]{:S(2)}, u32[]{:S(2)}) collective-permute-start(bf16[128,2048]{1,0:T(8,128)(2,1)S(1)} %fusion.6), channel_id=1, source_target_pairs={{0,1},{1,0},{2,3},{3,2},{4,5},{5,4},{6,7},{7,6},{8,9},{9,8},{10,11... | collective-permute-start | bytes 1572872 | tf_op jit(solution)/shard_map/ppermute | solution.py:1501
  393.3 15.1 %collective-permute-start.6 = (bf16[128,2048]{1,0:T(8,128)(2,1)S(1)}, bf16[128,2048]{1,0:T(8,128)(2,1)S(1)}, u32[]{:S(2)}, u32[]{:S(2)}) collective-permute-start(bf16[128,2048]{1,0:T(8,128)(2,1)S(1)} %fusion.5), channel_id=1, source_target_pairs={{0,2},{1,3},{2,0},{3,1},{4,6},{5,7},{6,4},{7,5},{8,10},{9,11},{10,... | collective-permute-start | bytes 1572872 | tf_op jit(solution)/shard_map/ppermute | solution.py:1501
  394.0 9.8 %collective-permute-start.5 = (bf16[2,64,512]{2,1,0:T(8,128)(2,1)S(1)}, bf16[2,64,512]{2,1,0:T(8,128)(2,1)S(1)}, u32[]{:S(2)}, u32[]{:S(2)}) collective-permute-start(bf16[2,64,512]{2,1,0:T(8,128)(2,1)S(1)} %slice.159), channel_id=1, source_target_pairs={{8,0},{16,8},{24,16},{9,1},{17,9},{25,17},{10,2},{18,10},{26,18},{... | collective-permute-start | bytes 393224 | tf_op jit(solution)/shard_map/ppermute | solution.py:1396
  404.0 3.6 copy-start.31
  408.9 7.6 %collective-permute-start.9 = (bf16[512,2048]{1,0:T(8,128)(2,1)S(1)}, bf16[512,2048]{1,0:T(8,128)(2,1)S(1)}, u32[]{:S(2)}, u32[]{:S(2)}) collective-permute-start(bf16[512,2048]{1,0:T(8,128)(2,1)S(1)} %add_convert_fusion.part), channel_id=1, source_target_pairs={{0,4},{4,0},{1,5},{5,1},{2,6},{6,2},{3,7},{7,3},{8,12},{12,8},{9,1... | collective-permute-start | bytes 6291464 | tf_op jit(solution)/shard_map/ppermute | solution.py:1400
  410.3 4.3 collective-permute-start.8
  414.9 2.4 copy-start
  416.5 5.1 %copy-start.19 = (f32[8,2048]{1,0:T(8,128)S(1)}, f32[8,2048]{1,0:T(8,128)}, u32[]{:S(2)}) copy-start(f32[8,2048]{1,0:T(8,128)} %get-tuple-element.103.mlp_rows) | copy-start | bytes 196612
  (25 other events, 33.3 us)
Sparse Core Ops, SparseCore 0:
  12.1 204.3 all-gather.2
